TPU v7x, 512 devices: a whole 4x8x8 slice. The times are simulated.
512 devices in a mesh: expert: 8 (over z), tensor: 64 (over y, x, core).
Axes of the slice: x: 4, y: 8, z: 8, core: 2. Of those that a mesh axis runs over, the one named last changes fastest.
Arguments:
- activations: bfloat16 [1024, 3072], P('expert', 'tensor'), may hold values from -6 to 6
- out_grad: bfloat16 [1024, 3072], P('expert', 'tensor'), may hold values from -6 to 6
- token_scale: float32 [1024], P('expert'), may hold values from 0.25 to 4
- route_prob: float32 [1024, 2], P('expert'), may hold values from 0.1 to 0.9
- route_ids: int32 [1024, 2], P('expert'), may hold values from 0 to 7, all different within a row; in each aligned block of 128 rows (0 to 127, 128 to 255, ...) at most 40 rows name the same one
- w_gate: bfloat16 [8, 3072, 16384], P('expert', None, 'tensor'), may hold values from -0.109375 to 0.109375
- w_up: bfloat16 [8, 3072, 16384], P('expert', None, 'tensor'), may hold values from -0.109375 to 0.109375
- w_down: bfloat16 [8, 16384, 3072], P('expert', 'tensor'), may hold values from -0.046875 to 0.046875
Outputs:
- input_grad: bfloat16 [1024, 3072], P('expert', 'tensor')
Inputs may be any that keep to these rules, and one draw needn't show every extreme that they name: `route_ids`: each token names 2 different experts; within the tokens of one index of expert (aligned blocks of 128 rows) no expert is named by more than 40 tokens, a bound that some block reaches.
All inputs are finite; a program needn't handle non-finite values.
Results may differ from a plain program's by a relative error of at most 0.0055.
Values may be sent and summed in bfloat16 or wider, within the bound.
No kernel may reach another device: no remote copies, remote signals or barrier semaphores. Data moves between devices by JAX's collectives and lax.ppermute only.
A program may use at most 64 MiB of HBM per device.

v0:
```python
import jax
import jax.numpy as jnp
from jax import lax
from jax.sharding import PartitionSpec as P


def backward_tail(gate, upper, back):
    sigmoid_g = jax.nn.sigmoid(gate)
    slope = sigmoid_g * (1.0 + gate * (1.0 - sigmoid_g))
    d_gate = (back * upper * slope).astype(jnp.bfloat16)
    d_upper = (back * gate * sigmoid_g).astype(jnp.bfloat16)
    return (d_gate, d_upper)


def shards(activations, out_grad, token_scale, route_prob, route_ids, w_gate, w_up, w_down):
    experts_n = lax.axis_size("expert")
    groups = route_ids.shape[0]
    capacity = min(groups, 5 * groups // (2 * experts_n))
    labels = jnp.arange(experts_n, dtype=jnp.int32)
    onehot = route_ids[:, :, None] == labels[None, None, :]
    hits = jnp.sum(onehot.astype(jnp.int32), axis=1)
    slots = jnp.cumsum(hits, axis=0) - hits
    places = jnp.arange(capacity, dtype=jnp.int32)
    placed = (jnp.transpose(slots)[:, None, :] == places[None, :, None]) & (
        jnp.transpose(hits)[:, None, :] > 0
    )
    place_bf = placed.astype(jnp.bfloat16)
    wgate = w_gate[0]
    wupper = w_up[0]
    wdown = w_down[0]

    def packed(rows):
        return jnp.einsum("ect,tf->ecf", place_bf, rows, preferred_element_type=jnp.float32).astype(
            jnp.bfloat16
        )

    send_x = packed(activations)
    send_g = packed(out_grad)
    recv_x, recv_g = (
        lax.all_to_all(send_x, "expert", split_axis=0, concat_axis=0, tiled=True),
        lax.all_to_all(send_g, "expert", split_axis=0, concat_axis=0, tiled=True),
    )
    piece_x = lax.all_gather(recv_x, "tensor", axis=2, tiled=True)
    piece_g = lax.all_gather(recv_g, "tensor", axis=2, tiled=True)
    width = piece_x.shape[2]
    flat_x = piece_x.reshape(-1, width)
    flat_g = piece_g.reshape(-1, width)
    slab_gate = wgate
    slab_upper = wupper
    gate_sum = jnp.dot(flat_x, slab_gate, preferred_element_type=jnp.float32)
    upper_sum = jnp.dot(flat_x, slab_upper, preferred_element_type=jnp.float32)
    back_sum = lax.dot_general(
        flat_g, wdown, (((1,), (1,)), ((), ())), preferred_element_type=jnp.float32
    )
    d_gate, d_upper = backward_tail(gate_sum, upper_sum, back_sum)
    slab_gate = wgate
    slab_upper = wupper
    term = lax.dot_general(
        slab_gate, d_gate, (((1,), (1,)), ((), ())), preferred_element_type=jnp.float32
    )
    partial_t = lax.psum_scatter(
        term
        + lax.dot_general(
            slab_upper, d_upper, (((1,), (1,)), ((), ())), preferred_element_type=jnp.float32
        ),
        "tensor",
        scatter_dimension=0,
        tiled=True,
    )
    shaped = partial_t.reshape(partial_t.shape[0], experts_n, capacity)
    returned = lax.all_to_all(shaped, "expert", split_axis=1, concat_axis=1, tiled=True)
    weights = (
        jnp.sum(route_prob[:, :, None] * onehot.astype(jnp.float32), axis=1) * token_scale[:, None]
    )
    combine = placed.astype(jnp.float32) * jnp.transpose(weights)[:, None, :]
    result = jnp.einsum(
        "fec,ect->tf",
        returned,
        combine,
        precision=lax.Precision.HIGHEST,
        preferred_element_type=jnp.float32,
    )
    return result.astype(jnp.bfloat16)


def solution(mesh):
    placed = (
        P("expert", "tensor"),
        P("expert", "tensor"),
        P("expert"),
        P("expert", None),
        P("expert", None),
        P("expert", None, "tensor"),
        P("expert", None, "tensor"),
        P("expert", "tensor", None),
    )
    return jax.shard_map(
        shards, mesh=mesh, in_specs=placed, out_specs=P("expert", "tensor"), check_vma=False
    )
```

profile of v0, /device:TPU:1, one launch (start us, length us, event | category | flops | bytes accessed | tf_op | source)
XLA Modules:
  0.0 443.3 jit_solution(17376603601674115659)
XLA Ops:
  6.5 0.0 copy-start
  6.5 0.0 all-gather.3.cloned.1.call-start
  6.5 0.8 convert_reduce_fusion
  7.3 0.1 copy.27
  7.5 0.2 reduce_window_sum.11
  7.7 0.9 convolution_convert_fusion.1
  8.6 0.1 reshape.25
  8.7 17.5 %all_to_all.15 = bf16[8,2,960]{2,1,0:T(2,128)(2,1)S(1)} all-to-all(bf16[8,2,960]{2,1,0:T(2,128)(2,1)S(1)} %reshape.25), channel_id=1, replica_groups=mesh['expert'=8,'tensor'=64] {'expert'}, dimensions={0} | all-to-all | bytes 61440 | tf_op jit(solution)/shard_map/all_to_all | solution.py:41
  26.3 0.1 reshape.26
  26.4 0.8 copy.30
  27.1 0.0 all-gather.3.cloned.1.call-update
  27.2 0.0 all-gather.5.cloned.1.call-start
  27.2 0.9 convolution_convert_fusion
  28.1 0.1 reshape.27
  28.2 9.2 %all_to_all.16 = bf16[8,2,960]{2,1,0:T(2,128)(2,1)S(1)} all-to-all(bf16[8,2,960]{2,1,0:T(2,128)(2,1)S(1)} %reshape.27), channel_id=1, replica_groups=mesh['expert'=8,'tensor'=64] {'expert'}, dimensions={0} | all-to-all | bytes 61440 | tf_op jit(solution)/shard_map/all_to_all | solution.py:40
  37.5 0.1 reshape.28
  37.6 0.8 copy.32
  38.4 0.0 all-gather.5.cloned.1.call-update
  38.4 0.0 all-reduce.3.cloned.1.call-start
  38.5 73.2 %all-gather.3.cloned.1.call-done = bf16[8,40,3072]{1,0,2:T(8,128)(2,1)} async-done(((bf16[8,40,48]{1,0,2:T(8,128)(2,1)}), bf16[8,40,3072]{1,0,2:T(8,128)(2,1)}) %all-gather.3.cloned.1.call-update) | async-done | bytes 1966096 | tf_op jit(solution)/shard_map/all_gather | solution.py:44
  111.7 6.4 %copy.31 = bf16[8,40,3072]{2,1,0:T(8,128)(2,1)S(1)} copy(bf16[8,40,3072]{1,0,2:T(8,128)(2,1)} %all-gather.3.cloned.1.call-done) | data formatting | bytes 3932160 | tf_op jit(solution)/shard_map/all_gather | solution.py:44
  118.0 2.9 fusion.8
  120.9 77.4 %all-gather.5.cloned.1.call-done = bf16[8,40,3072]{1,0,2:T(8,128)(2,1)} async-done(((bf16[8,40,48]{1,0,2:T(8,128)(2,1)}), bf16[8,40,3072]{1,0,2:T(8,128)(2,1)}) %all-gather.5.cloned.1.call-update) | async-done | bytes 1966096 | tf_op jit(solution)/shard_map/all_gather | solution.py:43
  198.3 6.4 %copy.33 = bf16[8,40,3072]{2,1,0:T(8,128)(2,1)S(1)} copy(bf16[8,40,3072]{1,0,2:T(8,128)(2,1)} %all-gather.5.cloned.1.call-done) | data formatting | bytes 3932160 | tf_op jit(solution)/shard_map/all_gather | solution.py:43
  204.7 2.8 fusion.3
  207.5 0.0 copy-done
  207.5 5.7 %fusion.1 = f32[320,3072]{1,0:T(8,128)} fusion(bf16[1,3072,256]{2,1,0:T(8,128)(2,1)} %param.13, f32[320,256]{1,0:T(8,128)} %fusion.8, bf16[320,3072]{1,0:T(8,128)(2,1)S(1)} %bitcast.53, bf16[1,3072,256]{2,1,0:T(8,128)(2,1)S(1)} %copy-done, f32[320,256]{1,0:T(8,128)} %fusion.3), kind=kOutput, calls=%fused_computation.2 | convolution fusion | flops 1007452160 | bytes 9699328 | tf_op jit(solution)/shard_map/dot_general | solution.py:58
  213.2 4.9 %fusion = f32[3072,320]{0,1:T(8,128)} fusion(f32[320,3072]{1,0:T(8,128)} %fusion.1, bf16[1,3072,256]{2,1,0:T(8,128)(2,1)S(1)} %copy-done, f32[320,256]{1,0:T(8,128)} %fusion.8, f32[320,256]{1,0:T(8,128)} %fusion.3), kind=kOutput, calls=%fused_computation.1 | convolution fusion | flops 504791040 | bytes 10092544 | tf_op jit(solution)/shard_map/dot_general | solution.py:63
  218.1 0.0 copy-start.1
  218.1 0.0 copy-start.2
  218.1 0.0 copy-start.3
  218.1 0.0 all-reduce.3.cloned.1.call-update
  218.2 1.3 dynamic-slice
  220.1 0.0 copy-done.1
  220.1 0.0 copy-done.2
  220.1 198.0 %all-reduce.3.cloned.1.call-done = f32[3072,320]{0,1:T(8,128)} async-done(((f32[3072,320]{0,1:T(8,128)}), f32[3072,320]{0,1:T(8,128)}) %all-reduce.3.cloned.1.call-update) | async-done | bytes 3932176
  418.2 1.1 constant_dynamic-slice_fusion
  419.2 0.8 reshape.29
  420.0 7.1 %all-to-all-start.2 = ((f32[8,1,1920]{2,1,0:T(1,128)}), f32[8,1,1920]{2,1,0:T(1,128)S(1)}, u32[]{:S(2)}, u32[]{:S(2)}) async-start(f32[8,1,1920]{2,1,0:T(1,128)} %reshape.29), calls=%async_computation.2 | async-start | bytes 122880 | tf_op jit(solution)/shard_map/all_to_all | solution.py:71
  427.1 0.0 copy-done.3
  427.2 7.2 %all-to-all-done.2 = f32[8,1,1920]{2,1,0:T(1,128)S(1)} async-done(((f32[8,1,1920]{2,1,0:T(1,128)}), f32[8,1,1920]{2,1,0:T(1,128)S(1)}, u32[]{:S(2)}, u32[]{:S(2)}) %all-to-all-start.2) | async-done | bytes 61472 | tf_op jit(solution)/shard_map/all_to_all | solution.py:71
  434.3 0.5 broadcast.36
  434.8 0.8 reduce
  435.6 0.1 reshape.30
  435.7 1.0 fusion.21
  (5 shorter events, 0.1 us)
Async XLA Ops:
  6.5 200.9 %copy-start = (bf16[1,3072,256]{2,1,0:T(8,128)(2,1)S(1)}, bf16[1,3072,256]{2,1,0:T(8,128)(2,1)}, u32[]{:S(2)}) copy-start(bf16[1,3072,256]{2,1,0:T(8,128)(2,1)} %param.14) | copy-start | bytes 4718596
  6.5 105.1 %all-gather.3.cloned.1.call-start = ((), (), s32[]{:S(2)}) async-start(), calls=%async_computation.3 | async-start | bytes 6389760 | tf_op jit(solution)/shard_map/all_gather | solution.py:44
  27.2 171.1 %all-gather.5.cloned.1.call-start = ((), (), s32[]{:S(2)}) async-start(), calls=%async_computation.4 | async-start | bytes 6389760 | tf_op jit(solution)/shard_map/all_gather | solution.py:43
  38.4 379.8 %all-reduce.3.cloned.1.call-start = ((), (), s32[]{:S(2)}) async-start(), calls=%async_computation.5 | async-start | bytes 7864320
  218.1 2.0 copy-start.1
  218.1 2.0 copy-start.2
  218.1 209.0 %copy-start.3 = (f32[128]{0:T(128)S(1)}, f32[128]{0:T(128)}, u32[]{:S(2)}) copy-start(f32[128]{0:T(128)} %param.10) | copy-start | bytes 1540
  420.0 14.3 %all-to-all-start.2 = ((f32[8,1,1920]{2,1,0:T(1,128)}), f32[8,1,1920]{2,1,0:T(1,128)S(1)}, u32[]{:S(2)}, u32[]{:S(2)}) async-start(f32[8,1,1920]{2,1,0:T(1,128)} %reshape.29), calls=%async_computation.2 | async-start | bytes 122880 | tf_op jit(solution)/shard_map/all_to_all | solution.py:71
Sparse Core Ops, SparseCore 0:
  27.3 84.3 all-gather.2
  115.0 83.2 all-gather.4
  218.3 199.8 all-reduce.2
where the time goes:
time: 446 us; the launch traced here: 443 us
  waiting for transfers between devices  356 us (80%)
  blocking collectives  26.8 us (6%)
  matrix products  19.1 us (4%)
  local copies, waits for them, and re-layouts  18.7 us (4%)
  between operations  13.9 us (3%)
  starting transfers between devices  7.18 us (2%)
    unnamed x4, waiting for transfers between devices  198 us
    all_gather x1, waiting for transfers between devices, shards(): piece_x = lax.all_gather(recv_x, 'tensor', axis=2, tiled=True)  77.4 us
    all_gather x1, waiting for transfers between devices, shards(): piece_g = lax.all_gather(recv_g, 'tensor', axis=2, tiled=True)  73.2 us
    all_to_all x1, blocking collectives, shards(): lax.all_to_all(send_g, 'expert', split_axis=0, concat_axis=0, tiled=True)  17.5 us
    all_to_all x1, blocking collectives, shards(): lax.all_to_all(send_x, 'expert', split_axis=0, concat_axis=0, tiled=True)  9.25 us
  transfers between devices with their start and end apart: 4, of which 4 were waited for; matrix products, arithmetic and copies ran while one was open for 3% of the time, Pallas kernels for 0%

commit v1 on v0

v1 whole, which is shorter than its diff:
```python
import jax
import jax.numpy as jnp
from jax import lax
from jax.sharding import Mesh, PartitionSpec as P

BF16 = jnp.bfloat16
F32 = jnp.float32
LANES = 128
FINE = 16


def backward_tail(gate, upper, back):
    sigmoid_g = jax.nn.sigmoid(gate)
    slope = sigmoid_g * (1.0 + gate * (1.0 - sigmoid_g))
    d_gate = (back * upper * slope).astype(BF16)
    d_upper = (back * gate * sigmoid_g).astype(BF16)
    return d_gate, d_upper


def shards(activations, out_grad, token_scale, route_prob, route_ids, w_gate, w_up, w_down):
    nz, ny, nx, nc = (lax.axis_size(a) for a in ("z", "y", "x", "c"))
    core = lax.axis_index("c")
    tokens, feats = activations.shape
    capacity = min(tokens, 5 * tokens // (2 * nz))
    parts = feats // FINE
    hidden = w_gate.shape[2]
    rows = nz * capacity
    wide = feats * ny

    labels = jnp.arange(nz, dtype=jnp.int32)
    onehot = route_ids[:, :, None] == labels[None, None, :]
    hits = jnp.sum(onehot.astype(jnp.int32), axis=1)
    below = jnp.tril(jnp.ones((tokens, tokens), BF16), -1)
    slots = jnp.dot(below, hits.astype(BF16), preferred_element_type=F32).astype(jnp.int32)
    lane = jnp.arange(LANES, dtype=jnp.int32)
    lane_part = lane // capacity
    lane_slot = jnp.where(lane_part < parts, lane % capacity, -1)
    place = (slots[:, :, None] == lane_slot) & (hits[:, :, None] > 0)
    place_bf = place.astype(BF16).reshape(tokens, nz * LANES)

    def packed(values):
        spread = lax.dot_general(
            values, place_bf, (((0,), (0,)), ((), ())), preferred_element_type=F32
        ).astype(BF16)
        spread = spread.reshape(parts, FINE, nz, LANES)
        own = jnp.arange(parts)[:, None, None, None] == lane_part
        return jnp.sum(jnp.where(own, spread, 0), axis=0).transpose(1, 0, 2)

    block = jnp.concatenate([packed(activations), packed(out_grad)], axis=1)
    send = jnp.broadcast_to(block[:, None], (nz, ny) + block.shape[1:])
    send = send.reshape((nz * ny,) + block.shape[1:])
    got = lax.all_to_all(send, ("z", "y"), split_axis=0, concat_axis=0, tiled=True)

    def ordered(w):
        w = w.reshape(ny, nx, nc, parts, FINE, hidden).transpose(2, 1, 3, 0, 4, 5)
        return w.reshape(nc, nx * wide, hidden)

    w_in = jnp.concatenate([ordered(w_gate[0]), ordered(w_up[0])], axis=2)
    w_dn = ordered(w_down[0].T)
    in_own, in_other = (lax.dynamic_index_in_dim(w_in, i, 0, False) for i in (core, 1 - core))
    dn_own, dn_other = (lax.dynamic_index_in_dim(w_dn, i, 0, False) for i in (core, 1 - core))

    got = got.reshape(nz, ny, 2, FINE, LANES)[..., : parts * capacity]
    got = got.reshape(nz, ny, 2, FINE, parts, capacity).transpose(2, 0, 5, 4, 1, 3)
    mine = got.reshape(2 * rows, wide)

    copies = jnp.broadcast_to(mine[None], (nx,) + mine.shape)
    own = lax.all_to_all(copies, "x", split_axis=0, concat_axis=0, tiled=True)
    other = lax.ppermute(own, "c", [(0, 1), (1, 0)])

    def forward(block, w_a, w_b):
        total_a, total_b = 0.0, 0.0
        for i in range(nx):
            k = slice(i * wide, (i + 1) * wide)
            total_a += jnp.dot(block[i, :rows], w_a[k], preferred_element_type=F32)
            total_b += jnp.dot(block[i, rows:], w_b[k], preferred_element_type=F32)
        return total_a, total_b

    in_a, back_a = forward(own, in_own, dn_own)
    in_b, back_b = forward(other, in_other, dn_other)
    both = in_a + in_b
    d_gate, d_upper = backward_tail(both[:, :hidden], both[:, hidden:], back_a + back_b)
    d_both = jnp.concatenate([d_gate, d_upper], axis=1)

    def returned(w):
        return lax.dot_general(d_both, w, (((1,), (1,)), ((), ())), preferred_element_type=F32)

    from_other = lax.ppermute(returned(in_other).astype(BF16), "c", [(0, 1), (1, 0)])
    part = (returned(in_own) + from_other.astype(F32)).astype(BF16)
    part = part.reshape(rows, nx, wide).transpose(1, 0, 2)
    part = lax.all_to_all(part, "x", split_axis=0, concat_axis=0, tiled=True)
    part = jnp.sum(part.astype(F32), axis=0).astype(BF16)

    part = part.reshape(nz, capacity, parts, ny, FINE).transpose(0, 3, 4, 2, 1)
    part = part.reshape(nz * ny, FINE, parts * capacity)
    part = jnp.pad(part, ((0, 0), (0, 0), (0, LANES - parts * capacity)))
    part = lax.all_to_all(part, ("z", "y"), split_axis=0, concat_axis=0, tiled=True)
    part = jnp.sum(part.reshape(nz, ny, FINE, LANES).astype(F32), axis=1)

    weights = (
        jnp.sum(route_prob[:, :, None] * onehot.astype(F32), axis=1) * token_scale[:, None]
    )
    combine = jnp.where(place, weights[:, :, None], 0.0).reshape(tokens, nz * LANES)
    own_part = jnp.arange(parts)[:, None, None, None] == lane_part
    spread = jnp.where(own_part, part.transpose(1, 0, 2)[None], 0.0)
    spread = spread.reshape(feats, nz * LANES)
    result = lax.dot_general(
        combine,
        spread,
        (((1,), (1,)), ((), ())),
        precision=lax.Precision.HIGHEST,
        preferred_element_type=F32,
    )
    return result.astype(BF16)


def solution(mesh):
    devices = mesh.devices
    fine = Mesh(devices.reshape(devices.shape[0], 8, 4, 2), ("z", "y", "x", "c"))
    tensor = ("y", "x", "c")
    placed = (
        P("z", tensor),
        P("z", tensor),
        P("z"),
        P("z", None),
        P("z", None),
        P("z", None, tensor),
        P("z", None, tensor),
        P("z", tensor, None),
    )
    return jax.shard_map(
        shards, mesh=fine, in_specs=placed, out_specs=P("z", tensor), check_vma=False
    )
```

time: 446 us -> 132 us (0.30)
  waiting for transfers between devices: 356 us -> 25 us
  blocking collectives: 26.8 us -> 50.9 us
  between operations: 13.9 us -> 0.54 us
  starting transfers between devices: 7.18 us -> 19.4 us
  matrix products: 19.1 us -> 9.8 us
    unnamed x4 -> x0, waiting for transfers between devices: 198 us -> none
    all_gather x2 -> x0, waiting for transfers between devices: 151 us -> none  [the longest x1 77.4 us: shards(): piece_x = lax.all_gather(recv_x, 'tensor', axis=2, tiled=True)]
    all_to_all x2, blocking collectives: 26.8 us -> 50.9 us  [the longest x1 34.1 us: shards(): lax.all_to_all(send, ('z', 'y'), split_axis=0, concat_axis=0, tiled=True)]
    all_to_all x1 -> x2, waiting for transfers between devices: 7.17 us -> 22.5 us  [the longest x1 11.8 us: shards(): lax.all_to_all(part, ('z', 'y'), split_axis=0, concat_axis=0, tiled=True)]
    all_gather x2 -> x0, local copies, waits for them, and re-layouts: 12.7 us -> none  [the longest x1 6.37 us: shards(): piece_g = lax.all_gather(recv_g, 'tensor', axis=2, tiled=True)]
    dot_general x7 -> x22, matrix products: 19.1 us -> 9.8 us  [the longest x8 3.92 us: forward(): total_b += jnp.dot(block[i, rows:], w_b[k], preferred_element_type=F32)]
    transpose x0 -> x6, local copies, waits for them, and re-layouts: none -> 8.72 us  [the longest x3 5.58 us: ordered(): w = w.reshape(ny, nx, nc, parts, FINE, hidden).transpose(2, 1, 3, 0, 4, 5)]
    ppermute x0 -> x2, starting transfers between devices: none -> 8.65 us  [the longest x1 6.73 us: shards(): other = lax.ppermute(own, 'c', [(0, 1), (1, 0)])]
  transfers between devices with their start and end apart: 4 -> 4, of which waited for: 4 -> 3; matrix products, arithmetic and copies ran while one was open for 3% -> 12% of each run, Pallas kernels for 0% -> 0%
where the time goes in v1:
time: 132 us; the launch traced here: 130 us
  blocking collectives  50.9 us (39%)
  waiting for transfers between devices  25 us (19%)
  local copies, waits for them, and re-layouts  19.8 us (15%)
  starting transfers between devices  19.4 us (15%)
  matrix products  9.8 us (7%)
  other arithmetic  4.92 us (4%)
    all_to_all x1, blocking collectives, shards(): lax.all_to_all(send, ('z', 'y'), split_axis=0, concat_axis=0, tiled=True)  34.1 us
    all_to_all x1, blocking collectives, shards(): part = lax.all_to_all(part, 'x', split_axis=0, concat_axis=0, tiled=True)  16.8 us
    all_to_all x1, waiting for transfers between devices, shards(): lax.all_to_all(part, ('z', 'y'), split_axis=0, concat_axis=0, tiled=True)  11.8 us
    all_to_all x1, waiting for transfers between devices, shards(): own = lax.all_to_all(copies, 'x', split_axis=0, concat_axis=0, tiled=True)  10.6 us
    all_to_all x1, starting transfers between devices, shards(): lax.all_to_all(part, ('z', 'y'), split_axis=0, concat_axis=0, tiled=True)  6.75 us
    ppermute x1, starting transfers between devices, shards(): other = lax.ppermute(own, 'c', [(0, 1), (1, 0)])  6.73 us
    transpose x3, local copies, waits for them, and re-layouts, ordered(): w = w.reshape(ny, nx, nc, parts, FINE, hidden).transpose(2, 1, 3, 0, 4, 5)  5.58 us
    broadcast_in_dim x3, local copies, waits for them, and re-layouts, shards(): copies = jnp.broadcast_to(mine[None], (nx,) + mine.shape)  4.6 us
  transfers between devices with their start and end apart: 4, of which 3 were waited for; matrix products, arithmetic and copies ran while one was open for 12% of the time, Pallas kernels for 0%

profile of v1, /device:TPU:1, one launch (start us, length us, event | category | flops | bytes accessed | tf_op | source)
XLA Modules:
  0.0 130.3 jit_solution(679479739372721174)
XLA Ops:
  0.0 0.0 copy-start.10
  0.0 0.7 convert_reduce_fusion.1
  0.7 0.2 convolution_convert_fusion.4
  0.9 0.1 copy.46
  1.1 0.1 copy.47
  1.2 0.2 eq.94
  1.4 0.2 and.54
  1.6 0.2 fusion.17
  1.8 0.2 fusion.14
  2.0 0.2 fusion.13
  2.3 0.1 broadcast_in_dim.93
  2.4 34.1 %all_to_all.20 = bf16[64,32,128]{2,1,0:T(8,128)(2,1)S(1)} all-to-all(bf16[64,32,128]{2,1,0:T(8,128)(2,1)S(1)} %bitcast.208), channel_id=1, replica_groups=mesh['z'=8,'y'=8,'x'=4,'c'=2] {'z','y'}, dimensions={0} | all-to-all | bytes 1048576 | tf_op jit(solution)/shard_map/all_to_all | solution.py:52
  36.6 0.8 reshape.199
  37.4 2.4 %copy.50 = bf16[2,8,40,3,8,16]{2,1,0,5,4,3:T(8,128)(2,1)} copy(bf16[2,8,40,3,8,16]{2,3,5,0,4,1:T(4,128)(2,1)S(1)} %bitcast.190) | data formatting | bytes 983040 | tf_op jit(solution)/shard_map/transpose | solution.py:64
  39.8 2.8 %broadcast_in_dim.94 = bf16[640,384]{0,1:T(8,128)(2,1)S(1)} reshape(bf16[2,8,40,3,8,16]{2,1,0,5,4,3:T(8,128)(2,1)} %copy.50) | data formatting | bytes 983040 | tf_op jit(solution)/shard_map/broadcast_in_dim | solution.py:67
  42.7 0.3 copy.51
  43.0 1.5 %broadcast_in_dim.95 = bf16[4,640,384]{2,1,0:T(8,128)(2,1)} broadcast(bf16[640,384]{1,0:T(8,128)(2,1)S(1)} %copy.51), dimensions={1,2} | broadcast | bytes 2457600 | tf_op jit(solution)/shard_map/broadcast_in_dim | solution.py:67
  44.5 4.0 %all-to-all-start.1 = ((bf16[4,640,384]{2,1,0:T(8,128)(2,1)}), bf16[4,640,384]{2,1,0:T(8,128)(2,1)S(1)}, u32[]{:S(2)}, u32[]{:S(2)}) async-start(bf16[4,640,384]{2,1,0:T(8,128)(2,1)} %broadcast_in_dim.95), calls=%async_computation.1 | async-start | bytes 3932160 | tf_op jit(solution)/shard_map/all_to_all | solution.py:68
  48.5 1.7 %copy.52 = bf16[1,256,3072]{1,2,0:T(8,128)(2,1)S(1)} copy(bf16[1,256,3072]{2,1,0:T(8,128)(2,1)} %param.15) | data formatting | bytes 3145728 | tf_op args[7]
  50.2 1.3 %copy.53 = bf16[2,4,3,8,16,256]{5,4,3,2,1,0:T(8,128)(2,1)} copy(bf16[2,4,3,8,16,256]{5,4,2,0,1,3:T(8,128)(2,1)S(1)} %bitcast.191) | data formatting | bytes 3145728 | tf_op jit(solution)/shard_map/transpose | solution.py:55
  51.5 2.9 %copy.54 = bf16[2,4,3,8,16,256]{5,4,3,2,1,0:T(8,128)(2,1)} copy(bf16[2,4,3,8,16,256]{5,4,2,0,1,3:T(8,128)(2,1)} %bitcast.209) | data formatting | bytes 3145728 | tf_op jit(solution)/shard_map/transpose | solution.py:55
  54.4 1.3 %copy.55 = bf16[2,4,3,8,16,256]{5,4,3,2,1,0:T(8,128)(2,1)} copy(bf16[2,4,3,8,16,256]{5,4,2,0,1,3:T(8,128)(2,1)S(1)} %bitcast.210) | data formatting | bytes 3145728 | tf_op jit(solution)/shard_map/transpose | solution.py:55
  55.8 3.2 %fusion.1 = (bf16[1,1536,512]{2,1,0:T(8,128)(2,1)S(1)}, bf16[1,1536,512]{2,1,0:T(8,128)(2,1)}) fusion(s32[]{:T(128)S(6)} %select_n.101, bf16[2,1536,256]{2,1,0:T(8,128)(2,1)} %bitcast.192, bf16[2,1536,256]{2,1,0:T(8,128)(2,1)} %bitcast.193, s32[]{:T(128)S(6)} %select_n.102), kind=kLoop, calls=%fused_computation.7 | loop fusion | flops 6291456 | bytes 6291464 | tf_op jit(solution)/shard_map/concatenate | solution.py:58
  59.0 10.6 %all-to-all-done.1 = bf16[4,640,384]{2,1,0:T(8,128)(2,1)S(1)} async-done(((bf16[4,640,384]{2,1,0:T(8,128)(2,1)}), bf16[4,640,384]{2,1,0:T(8,128)(2,1)S(1)}, u32[]{:S(2)}, u32[]{:S(2)}) %all-to-all-start.1) | async-done | bytes 1966112 | tf_op jit(solution)/shard_map/all_to_all | solution.py:68
  69.7 6.7 %collective-permute-start = (bf16[4,640,384]{2,1,0:T(8,128)(2,1)S(1)}, bf16[4,640,384]{2,1,0:T(8,128)(2,1)S(1)}, u32[]{:S(2)}, u32[]{:S(2)}) collective-permute-start(bf16[4,640,384]{2,1,0:T(8,128)(2,1)S(1)} %all-to-all-done.1), channel_id=1, source_target_pairs={{0,1},{1,0},{2,3},{3,2},{4,5},{5,4},{6,7},{7,6},{8,9},{9,8},{10,11... | collective-permute-start | bytes 5898248 | tf_op jit(solution)/shard_map/ppermute | solution.py:69
  76.4 1.2 fusion.27
  77.6 1.2 convolution_add_fusion.7
  78.8 0.2 convolution_add_fusion.6
  79.0 0.2 convolution_add_fusion.5
  79.3 0.3 fusion.21
  79.6 0.3 convolution_add_fusion.3
  80.0 0.3 convolution_add_fusion.2
  80.3 0.3 convolution_add_fusion.1
  80.6 0.0 collective-permute-done
  80.6 0.7 copy-done.1
  81.4 0.3 fusion.18
  81.7 0.3 fusion.19
  82.0 0.3 fusion.20
  82.3 0.2 fusion.24
  82.6 0.2 fusion.25
  82.8 0.2 fusion.26
  83.1 0.4 fusion.9
  83.5 0.4 fusion.23
  83.8 0.7 convolution_convert_fusion
  84.5 1.9 %collective-permute-start.1 = (bf16[320,1536]{1,0:T(8,128)(2,1)S(1)}, bf16[320,1536]{1,0:T(8,128)(2,1)S(1)}, u32[]{:S(2)}, u32[]{:S(2)}) collective-permute-start(bf16[320,1536]{1,0:T(8,128)(2,1)S(1)} %convolution_convert_fusion), channel_id=1, source_target_pairs={{0,1},{1,0},{2,3},{3,2},{4,5},{5,4},{6,7},{7,6},{8,9},{9,8},{10,11... | collective-permute-start | bytes 2949128 | tf_op jit(solution)/shard_map/ppermute | solution.py:88
  86.5 2.5 %collective-permute-done.1 = bf16[320,1536]{1,0:T(8,128)(2,1)S(1)} collective-permute-done((bf16[320,1536]{1,0:T(8,128)(2,1)S(1)}, bf16[320,1536]{1,0:T(8,128)(2,1)S(1)}, u32[]{:S(2)}, u32[]{:S(2)}) %collective-permute-start.1) | collective-permute-done | bytes 983072 | tf_op jit(solution)/shard_map/ppermute | solution.py:88
  89.0 0.7 add_convert_fusion
  89.7 0.1 copy.82
  89.8 16.8 %all_to_all.21 = bf16[4,320,384]{2,1,0:T(8,128)(2,1)S(1)} all-to-all(bf16[4,320,384]{2,1,0:T(8,128)(2,1)S(1)} %bitcast.202), channel_id=1, replica_groups=mesh['z'=8,'y'=8,'x'=4,'c'=2] {'x'}, dimensions={0} | all-to-all | bytes 1966080 | tf_op jit(solution)/shard_map/all_to_all | solution.py:91
  106.6 0.2 reduce_sum.67
  106.8 0.2 copy.58
  107.1 0.7 reshape.205
  107.7 0.7 copy.59
  108.4 0.0 copy-start.9
  108.4 0.0 copy-start.12
  108.4 0.0 copy-start.13
  108.5 0.0 copy-start.11
  108.5 0.5 reshape.206
  109.0 0.8 pad.4
  109.8 6.8 %all-to-all-start.3 = ((bf16[64,16,128]{2,1,0:T(8,128)(2,1)}), bf16[64,16,128]{2,1,0:T(8,128)(2,1)S(1)}, u32[]{:S(2)}, u32[]{:S(2)}) async-start(bf16[64,16,128]{2,1,0:T(8,128)(2,1)} %pad.4), calls=%async_computation.3 | async-start | bytes 524288 | tf_op jit(solution)/shard_map/all_to_all | solution.py:97
  116.6 0.1 copy.48
  116.7 0.5 and_select_fusion
  117.2 11.8 %all-to-all-done.3 = bf16[64,16,128]{2,1,0:T(8,128)(2,1)S(1)} async-done(((bf16[64,16,128]{2,1,0:T(8,128)(2,1)}), bf16[64,16,128]{2,1,0:T(8,128)(2,1)S(1)}, u32[]{:S(2)}, u32[]{:S(2)}) %all-to-all-start.3) | async-done | bytes 262176 | tf_op jit(solution)/shard_map/all_to_all | solution.py:97
  129.1 1.3 convolution_convert_fusion.3
  (37 shorter events, 0.3 us)
Async XLA Ops:
  0.0 1.8 %copy-start = (bf16[128,48]{0,1:T(8,128)(2,1)S(1)}, bf16[128,48]{0,1:T(8,128)(2,1)}, u32[]{:S(2)}) copy-start(bf16[128,48]{0,1:T(8,128)(2,1)} %param.9) | copy-start | bytes 36868
  0.0 2.0 %copy-start.8 = (bf16[128,48]{0,1:T(8,128)(2,1)S(1)}, bf16[128,48]{0,1:T(8,128)(2,1)}, u32[]{:S(2)}) copy-start(bf16[128,48]{0,1:T(8,128)(2,1)} %param.8) | copy-start | bytes 36868
  0.0 2.4 %copy-start.10 = (s32[128]{0:T(128)}, s32[128]{0:T(128)S(1)}, u32[]{:S(2)}) copy-start(s32[128]{0:T(128)S(1)} %get-tuple-element.11) | copy-start | bytes 1540
  1.1 1.4 %copy-start.4 = (s32[128,8]{1,0:T(8,128)}, s32[128,8]{1,0:T(8,128)S(1)}, u32[]{:S(2)}) copy-start(s32[128,8]{1,0:T(8,128)S(1)} %copy.46) | copy-start | bytes 12292
  1.2 1.2 copy-start.6
  44.5 25.2 %all-to-all-start.1 = ((bf16[4,640,384]{2,1,0:T(8,128)(2,1)}), bf16[4,640,384]{2,1,0:T(8,128)(2,1)S(1)}, u32[]{:S(2)}, u32[]{:S(2)}) async-start(bf16[4,640,384]{2,1,0:T(8,128)(2,1)} %broadcast_in_dim.95), calls=%async_computation.1 | async-start | bytes 3932160 | tf_op jit(solution)/shard_map/all_to_all | solution.py:68
  51.5 2.9 %copy-start.3 = (bf16[1,3072,256]{2,1,0:T(8,128)(2,1)S(1)}, bf16[1,3072,256]{2,1,0:T(8,128)(2,1)}, u32[]{:S(2)}) copy-start(bf16[1,3072,256]{2,1,0:T(8,128)(2,1)} %param.14) | copy-start | bytes 4718596
  69.7 9.1 %copy-start.2 = (bf16[2,4,3,8,16,256]{5,4,3,2,1,0:T(8,128)(2,1)S(1)}, bf16[2,4,3,8,16,256]{5,4,3,2,1,0:T(8,128)(2,1)}, u32[]{:S(2)}) copy-start(bf16[2,4,3,8,16,256]{5,4,3,2,1,0:T(8,128)(2,1)} %copy.53) | copy-start | bytes 4718596
  69.7 11.0 %collective-permute-start = (bf16[4,640,384]{2,1,0:T(8,128)(2,1)S(1)}, bf16[4,640,384]{2,1,0:T(8,128)(2,1)S(1)}, u32[]{:S(2)}, u32[]{:S(2)}) collective-permute-start(bf16[4,640,384]{2,1,0:T(8,128)(2,1)S(1)} %all-to-all-done.1), channel_id=1, source_target_pairs={{0,1},{1,0},{2,3},{3,2},{4,5},{5,4},{6,7},{7,6},{8,9},{9,8},{10,11... | collective-permute-start | bytes 5898248 | tf_op jit(solution)/shard_map/ppermute | solution.py:69
  79.9 1.4 %copy-start.1 = (bf16[1,1536,512]{2,1,0:T(8,128)(2,1)S(1)}, bf16[1,1536,512]{2,1,0:T(8,128)(2,1)}, u32[]{:S(2)}) copy-start(bf16[1,1536,512]{2,1,0:T(8,128)(2,1)} %get-tuple-element.8) | copy-start | bytes 4718596
  84.5 4.5 %collective-permute-start.1 = (bf16[320,1536]{1,0:T(8,128)(2,1)S(1)}, bf16[320,1536]{1,0:T(8,128)(2,1)S(1)}, u32[]{:S(2)}, u32[]{:S(2)}) collective-permute-start(bf16[320,1536]{1,0:T(8,128)(2,1)S(1)} %convolution_convert_fusion), channel_id=1, source_target_pairs={{0,1},{1,0},{2,3},{3,2},{4,5},{5,4},{6,7},{7,6},{8,9},{9,8},{10,11... | collective-permute-start | bytes 2949128 | tf_op jit(solution)/shard_map/ppermute | solution.py:88
  108.4 8.1 %copy-start.9 = (s32[128,2]{0,1:T(2,128)S(1)}, s32[128,2]{0,1:T(2,128)}, u32[]{:S(2)}) copy-start(s32[128,2]{0,1:T(2,128)} %param.12) | copy-start | bytes 3076
  108.4 8.1 %copy-start.12 = (f32[128,2]{0,1:T(2,128)S(1)}, f32[128,2]{0,1:T(2,128)}, u32[]{:S(2)}) copy-start(f32[128,2]{0,1:T(2,128)} %param.11) | copy-start | bytes 3076
  108.4 8.1 %copy-start.13 = (f32[128]{0:T(128)S(1)}, f32[128]{0:T(128)}, u32[]{:S(2)}) copy-start(f32[128]{0:T(128)} %param.10) | copy-start | bytes 1540
  108.4 8.2 %copy-start.5 = (s32[128,8]{1,0:T(8,128)S(1)}, s32[128,8]{1,0:T(8,128)}, u32[]{:S(2)}) copy-start(s32[128,8]{1,0:T(8,128)} %copy-done.4) | copy-start | bytes 12292
  108.4 8.2 %copy-start.7 = (pred[128,8]{1,0:T(8,128)(4,1)S(1)}, pred[128,8]{1,0:T(8,128)(4,1)}, u32[]{:S(2)}) copy-start(pred[128,8]{1,0:T(8,128)(4,1)} %copy-done.6) | copy-start | bytes 3076
  108.5 8.2 %copy-start.11 = (s32[128]{0:T(128)S(1)}, s32[128]{0:T(128)}, u32[]{:S(2)}) copy-start(s32[128]{0:T(128)} %copy-done.10) | copy-start | bytes 1540
  109.8 19.2 %all-to-all-start.3 = ((bf16[64,16,128]{2,1,0:T(8,128)(2,1)}), bf16[64,16,128]{2,1,0:T(8,128)(2,1)S(1)}, u32[]{:S(2)}, u32[]{:S(2)}) async-start(bf16[64,16,128]{2,1,0:T(8,128)(2,1)} %pad.4), calls=%async_computation.3 | async-start | bytes 524288 | tf_op jit(solution)/shard_map/all_to_all | solution.py:97

commit v2 on v1

v2 whole, which is shorter than its diff:
```python
import functools
import math

import jax
import jax.numpy as jnp
from jax import lax
from jax.experimental import pallas as pl
from jax.experimental.pallas import tpu as pltpu
from jax.sharding import Mesh, PartitionSpec as P

BF16 = jnp.bfloat16
F32 = jnp.float32
LANES = 128
FINE = 16


def backward_tail(gate, upper, back):
    sigmoid_g = jax.nn.sigmoid(gate)
    slope = sigmoid_g * (1.0 + gate * (1.0 - sigmoid_g))
    d_gate = (back * upper * slope).astype(BF16)
    d_upper = (back * gate * sigmoid_g).astype(BF16)
    return d_gate, d_upper


def lane_layout(shape, capacity, parts):
    lane = lax.broadcasted_iota(jnp.int32, shape, 1)
    expert = lane // LANES
    inner = lane - expert * LANES
    part = inner // capacity
    slot = jnp.where(part < parts, inner - part * capacity, -1)
    return expert, part, slot


def placement(ids_ref, tokens, lanes, capacity, parts):
    expert, _, slot = lane_layout((tokens, lanes), capacity, parts)
    first = ids_ref[:, 0:1] == expert
    second = ids_ref[:, 1:2] == expert
    hit = first | second
    row = lax.broadcasted_iota(jnp.int32, (tokens, tokens), 0)
    col = lax.broadcasted_iota(jnp.int32, (tokens, tokens), 1)
    below = jnp.where(col < row, 1.0, 0.0).astype(BF16)
    hit_bf = jnp.where(hit, 1.0, 0.0).astype(BF16)
    before = jnp.dot(below, hit_bf, preferred_element_type=F32)
    return hit & (before == slot.astype(F32)), first, second


def pack_kernel(capacity, ids_ref, x_ref, g_ref, out_ref):
    nz, ny = out_ref.shape[:2]
    tokens, feats = x_ref.shape
    parts = feats // FINE
    lanes = nz * LANES
    place, _, _ = placement(ids_ref, tokens, lanes, capacity, parts)
    place = jnp.where(place, 1.0, 0.0).astype(BF16)
    _, part, _ = lane_layout((FINE, lanes), capacity, parts)
    for kind, ref in enumerate((x_ref, g_ref)):
        spread = lax.dot_general(
            ref[...], place, (((0,), (0,)), ((), ())), preferred_element_type=F32
        )
        block = jnp.zeros((FINE, lanes), F32)
        for p in range(parts):
            block = jnp.where(part == p, spread[p * FINE : (p + 1) * FINE], block)
        block = block.astype(BF16)
        for z in range(nz):
            for y in range(ny):
                out_ref[z, y, kind * FINE : (kind + 1) * FINE, :] = block[
                    :, z * LANES : (z + 1) * LANES
                ]


def unpack_kernel(capacity, parts, ny, in_ref, out_ref):
    nx, _, wide = out_ref.shape
    nz = in_ref.shape[0] // ny
    span = wide // parts
    rows = nz * capacity
    for kind in range(2):
        for pair in range(0, nz, 2):
            turned = []
            for z in (pair, pair + 1):
                block = in_ref[z * ny : (z + 1) * ny, kind * FINE : (kind + 1) * FINE, :]
                turned.append(block.reshape(span, LANES).astype(F32).T)
            start = kind * rows + pair * capacity
            for p in range(parts):
                piece = jnp.concatenate(
                    [t[p * capacity : (p + 1) * capacity] for t in turned], axis=0
                ).astype(BF16)
                for i in range(nx):
                    out_ref[i, start : start + 2 * capacity, p * span : (p + 1) * span] = piece


def repack_kernel(capacity, parts, ny, in_ref, out_ref):
    nx, rows, wide = in_ref.shape
    span = wide // parts
    for pair in range(0, rows // capacity, 2):
        here = slice(pair * capacity, (pair + 2) * capacity)
        total = in_ref[0, here, :].astype(F32)
        for i in range(1, nx):
            total += in_ref[i, here, :].astype(F32)
        for half in range(2):
            block = total[half * capacity : (half + 1) * capacity]
            pieces = [block[:, p * span : (p + 1) * span] for p in range(parts)]
            pieces.append(jnp.zeros((LANES - parts * capacity, span), F32))
            turned = jnp.concatenate(pieces, axis=0).T.astype(BF16)
            z = pair + half
            out_ref[z * ny : (z + 1) * ny] = turned.reshape(ny, FINE, LANES)


def combine_kernel(capacity, parts, ids_ref, prob_ref, scale_ref, out_ref):
    tokens, lanes = out_ref.shape
    place, first, _ = placement(ids_ref, tokens, lanes, capacity, parts)
    prob = jnp.where(first, prob_ref[:, 0:1], prob_ref[:, 1:2])
    out_ref[...] = jnp.where(place, prob * scale_ref[...], 0.0)


def final_kernel(capacity, parts, ny, combine_ref, in_ref, out_ref):
    lanes = combine_ref.shape[1]
    nz = lanes // LANES
    sums = []
    for z in range(nz):
        total = in_ref[z * ny].astype(F32)
        for y in range(1, ny):
            total += in_ref[z * ny + y].astype(F32)
        sums.append(total)
    sums = jnp.concatenate(sums, axis=1)
    _, part, _ = lane_layout(sums.shape, capacity, parts)
    spread = jnp.concatenate([jnp.where(part == p, sums, 0.0) for p in range(parts)], axis=0)
    out_ref[...] = lax.dot_general(
        combine_ref[...],
        spread,
        (((1,), (1,)), ((), ())),
        precision=lax.Precision.HIGHEST,
        preferred_element_type=F32,
    ).astype(out_ref.dtype)


def call(kernel, shape, dtype, *operands, flops=0):
    moved = sum(o.size * o.dtype.itemsize for o in operands)
    moved += math.prod(shape) * jnp.dtype(dtype).itemsize
    return pl.pallas_call(
        kernel,
        out_shape=jax.ShapeDtypeStruct(shape, dtype),
        in_specs=[pl.BlockSpec(memory_space=pltpu.VMEM)] * len(operands),
        out_specs=pl.BlockSpec(memory_space=pltpu.VMEM),
        compiler_params=pltpu.CompilerParams(vmem_limit_bytes=32 * 1024 * 1024),
        cost_estimate=pl.CostEstimate(flops=flops, bytes_accessed=moved, transcendentals=0),
    )(*operands)


def shards(activations, out_grad, token_scale, route_prob, route_ids, w_gate, w_up, w_down):
    nz, ny, nx, nc = (lax.axis_size(a) for a in ("z", "y", "x", "c"))
    core = lax.axis_index("c")
    tokens, feats = activations.shape
    capacity = min(tokens, 5 * tokens // (2 * nz))
    parts = feats // FINE
    hidden = w_gate.shape[2]
    rows = nz * capacity
    wide = feats * ny

    send = call(
        functools.partial(pack_kernel, capacity),
        (nz, ny, 2 * FINE, LANES),
        BF16,
        route_ids,
        activations,
        out_grad,
    )
    send = send.reshape(nz * ny, 2 * FINE, LANES)
    got = lax.all_to_all(send, ("z", "y"), split_axis=0, concat_axis=0, tiled=True)

    def ordered(w):
        w = w.reshape(ny, nx, nc, parts, FINE, hidden).transpose(2, 1, 3, 0, 4, 5)
        return w.reshape(nc, nx * wide, hidden)

    w_in = jnp.concatenate([ordered(w_gate[0]), ordered(w_up[0])], axis=2)
    w_dn = ordered(w_down[0].T)
    in_own, in_other = (lax.dynamic_index_in_dim(w_in, i, 0, False) for i in (core, 1 - core))
    dn_own, dn_other = (lax.dynamic_index_in_dim(w_dn, i, 0, False) for i in (core, 1 - core))
    got, in_own, in_other, dn_own, dn_other = lax.optimization_barrier(
        (got, in_own, in_other, dn_own, dn_other)
    )

    copies = call(
        functools.partial(unpack_kernel, capacity, parts, ny), (nx, 2 * rows, wide), BF16, got
    )
    own = lax.all_to_all(copies, "x", split_axis=0, concat_axis=0, tiled=True)
    other = lax.ppermute(own, "c", [(0, 1), (1, 0)])

    def forward(block, w_a, w_b):
        total_a, total_b = 0.0, 0.0
        for i in range(nx):
            k = slice(i * wide, (i + 1) * wide)
            total_a += jnp.dot(block[i, :rows], w_a[k], preferred_element_type=F32)
            total_b += jnp.dot(block[i, rows:], w_b[k], preferred_element_type=F32)
        return total_a, total_b

    in_a, back_a = forward(own, in_own, dn_own)
    in_b, back_b = forward(other, in_other, dn_other)
    both = in_a + in_b
    d_gate, d_upper = backward_tail(both[:, :hidden], both[:, hidden:], back_a + back_b)
    d_both = jnp.concatenate([d_gate, d_upper], axis=1)

    def returned(w):
        return lax.dot_general(d_both, w, (((1,), (1,)), ((), ())), preferred_element_type=F32)

    from_other = lax.ppermute(returned(in_other).astype(BF16), "c", [(0, 1), (1, 0)])
    part = (returned(in_own) + from_other.astype(F32)).astype(BF16)
    part = part.reshape(rows, nx, wide).transpose(1, 0, 2)
    part = lax.all_to_all(part, "x", split_axis=0, concat_axis=0, tiled=True)

    part = call(
        functools.partial(repack_kernel, capacity, parts, ny), (nz * ny, FINE, LANES), BF16, part
    )
    part = lax.all_to_all(part, ("z", "y"), split_axis=0, concat_axis=0, tiled=True)
    combine = call(
        functools.partial(combine_kernel, capacity, parts),
        (tokens, nz * LANES),
        F32,
        route_ids,
        route_prob,
        token_scale.reshape(tokens, 1),
    )
    return call(
        functools.partial(final_kernel, capacity, parts, ny), (tokens, feats), BF16, combine, part
    )


def solution(mesh):
    devices = mesh.devices
    fine = Mesh(devices.reshape(devices.shape[0], 8, 4, 2), ("z", "y", "x", "c"))
    tensor = ("y", "x", "c")
    placed = (
        P("z", tensor),
        P("z", tensor),
        P("z"),
        P("z", None),
        P("z", None),
        P("z", None, tensor),
        P("z", None, tensor),
        P("z", tensor, None),
    )
    return jax.shard_map(
        shards, mesh=fine, in_specs=placed, out_specs=P("z", tensor), check_vma=False
    )
```

time: 132 us -> 122 us (0.924)
  starting transfers between devices: 19.4 us -> 33 us
  blocking collectives: 50.9 us -> 41.2 us
  local copies, waits for them, and re-layouts: 19.8 us -> 13.9 us
  waiting for transfers between devices: 25 us -> 20.6 us
  matrix products: 9.8 us -> 6.09 us
  Pallas kernels: 0 us -> 3.54 us
  other arithmetic: 4.92 us -> 1.41 us
    all_to_all x1, starting transfers between devices: 4.01 us -> 17.3 us  [shards(): lax.all_to_all(send, ('z', 'y'), split_axis=0, concat_axis=0, tiled=True)]
    all_to_all x1, blocking collectives: 34.1 us -> 25 us  [shards(): own = lax.all_to_all(copies, 'x', split_axis=0, concat_axis=0, tiled=True)]
    all_to_all x1, waiting for transfers between devices: 10.6 us -> 5.3 us  [shards(): lax.all_to_all(send, ('z', 'y'), split_axis=0, concat_axis=0, tiled=True)]
    broadcast_in_dim x4 -> x0, local copies, waits for them, and re-layouts: 4.68 us -> none  [the longest x3 4.6 us: shards(): copies = jnp.broadcast_to(mine[None], (nx,) + mine.shape)]
    unnamed x31 -> x19, local copies, waits for them, and re-layouts: 2.52 us -> 6.29 us
    pallas_call x0 -> x5, Pallas kernels: none -> 3.54 us  [call(): pl.pallas_call(kernel, out_shape=jax.ShapeDtypeStruct(shape, dtype), in_s...]
    concatenate x2 -> x0, other arithmetic: 3.25 us -> none  [the longest x1 3.24 us: shards(): w_in = jnp.concatenate([ordered(w_gate[0]), ordered(w_up[0])], axis=2)]
    transpose x3 -> x0, local copies, waits for them, and re-layouts: 3.14 us -> none  [the longest x1 2.44 us: shards(): got.reshape(nz, ny, 2, FINE, parts, capacity).transpose(2, 0, 5, 4, 1, 3)]
  transfers between devices with their start and end apart: 4 -> 4, of which waited for: 3 -> 4; matrix products, arithmetic and copies ran while one was open for 12% -> 11% of each run, Pallas kernels for 0% -> 0%
where the time goes in v2:
time: 122 us; the launch traced here: 120 us
  blocking collectives  41.2 us (34%)
  starting transfers between devices  33 us (27%)
  waiting for transfers between devices  20.6 us (17%)
  local copies, waits for them, and re-layouts  13.9 us (11%)
  matrix products  6.09 us (5%)
  Pallas kernels  3.54 us (3%)
  other arithmetic  1.41 us (1%)
    all_to_all x1, blocking collectives, shards(): own = lax.all_to_all(copies, 'x', split_axis=0, concat_axis=0, tiled=True)  25 us
    all_to_all x1, starting transfers between devices, shards(): lax.all_to_all(send, ('z', 'y'), split_axis=0, concat_axis=0, tiled=True)  17.3 us
    all_to_all x1, blocking collectives, shards(): part = lax.all_to_all(part, 'x', split_axis=0, concat_axis=0, tiled=True)  16.2 us
    all_to_all x1, waiting for transfers between devices, shards(): lax.all_to_all(part, ('z', 'y'), split_axis=0, concat_axis=0, tiled=True)  11.9 us
    all_to_all x1, starting transfers between devices, shards(): lax.all_to_all(part, ('z', 'y'), split_axis=0, concat_axis=0, tiled=True)  6.85 us
    ppermute x1, starting transfers between devices, shards(): other = lax.ppermute(own, 'c', [(0, 1), (1, 0)])  6.6 us
    unnamed x19, local copies, waits for them, and re-layouts  6.29 us
    transpose x3, local copies, waits for them, and re-layouts, ordered(): w = w.reshape(ny, nx, nc, parts, FINE, hidden).transpose(2, 1, 3, 0, 4, 5)  5.69 us
  transfers between devices with their start and end apart: 4, of which 4 were waited for; matrix products, arithmetic and copies ran while one was open for 11% of the time, Pallas kernels for 0%

profile of v2, /device:TPU:1, one launch (start us, length us, event | category | flops | bytes accessed | tf_op | source)
XLA Modules:
  0.0 120.0 jit_solution(1968126146662755030)
XLA Ops:
  0.0 0.8 copy.30.x_ref
  0.8 0.8 copy.31.g_ref
  1.6 0.8 copy.26.ids_ref
  2.4 1.3 %shard_map.83 = bf16[8,8,32,128]{3,2,1,0:T(8,128)(2,1)} custom-call(s32[128,2]{1,0:T(8,128)S(1)} %copy.26.ids_ref, bf16[128,48]{1,0:T(8,128)(2,1)S(1)} %copy.30.x_ref, bf16[128,48]{1,0:T(8,128)(2,1)S(1)} %copy.31.g_ref), custom_call_target="tpu_custom_call" | custom-call | bytes 549888 | tf_op jit(solution)/shard_map/pallas_call | solution.py:138
  3.8 0.0 copy-start.4
  3.8 17.3 %all-to-all-start = ((bf16[64,32,128]{2,1,0:T(8,128)(2,1)}), bf16[64,32,128]{2,1,0:T(8,128)(2,1)S(1)}, u32[]{:S(2)}, u32[]{:S(2)}) async-start(bf16[64,32,128]{2,1,0:T(8,128)(2,1)} %bitcast.1), calls=%async_computation | async-start | bytes 1048576 | tf_op jit(solution)/shard_map/all_to_all | solution.py:167
  21.1 2.8 %copy.32 = bf16[2,4,3,8,16,256]{5,4,3,2,1,0:T(8,128)(2,1)} copy(bf16[2,4,3,8,16,256]{5,4,2,0,1,3:T(8,128)(2,1)} %bitcast.91) | data formatting | bytes 3145728 | tf_op jit(solution)/shard_map/transpose | solution.py:170
  23.8 0.0 copy-done.4
  23.8 1.3 %copy.33 = bf16[2,4,3,8,16,256]{5,4,3,2,1,0:T(8,128)(2,1)} copy(bf16[2,4,3,8,16,256]{5,4,2,0,1,3:T(8,128)(2,1)S(1)} %bitcast.92) | data formatting | bytes 3145728 | tf_op jit(solution)/shard_map/transpose | solution.py:170
  25.2 2.6 %copy.34 = bf16[1,256,3072]{1,2,0:T(8,128)(2,1)} copy(bf16[1,256,3072]{2,1,0:T(8,128)(2,1)} %param.15) | data formatting | bytes 3145728 | tf_op args[7]
  27.7 1.6 %copy.35 = bf16[2,4,3,8,16,256]{5,4,3,2,1,0:T(8,128)(2,1)S(1)} copy(bf16[2,4,3,8,16,256]{5,4,2,0,1,3:T(8,128)(2,1)} %bitcast.86) | data formatting | bytes 3145728 | tf_op jit(solution)/shard_map/transpose | solution.py:170
  29.3 0.0 copy-start
  29.4 0.0 copy-start.1
  29.4 1.0 dynamic-slice_bitcast_fusion
  30.4 0.7 copy-done
  31.0 0.5 copy-done.1
  31.5 1.4 %fusion.1 = (bf16[1536,512]{1,0:T(8,128)(2,1)}, bf16[1536,512]{1,0:T(8,128)(2,1)S(1)}) fusion(s32[]{:T(128)S(6)} %select_n.11, bf16[2,1536,256]{2,1,0:T(8,128)(2,1)S(1)} %bitcast.87, bf16[2,1536,256]{2,1,0:T(8,128)(2,1)S(1)} %bitcast.88, s32[]{:T(128)S(6)} %select_n.10), kind=kLoop, calls=%fused_computation.7 | loop fusion | flops 6291456 | bytes 6291464 | tf_op jit(solution)/shard_map/jit(dynamic_index_in_dim)/squeeze | solution.py:175
  32.9 5.3 %all-to-all-done.in_ref = bf16[64,32,128]{2,1,0:T(8,128)(2,1)S(1)} async-done(((bf16[64,32,128]{2,1,0:T(8,128)(2,1)}), bf16[64,32,128]{2,1,0:T(8,128)(2,1)S(1)}, u32[]{:S(2)}, u32[]{:S(2)}) %all-to-all-start) | async-done | bytes 524320 | tf_op jit(solution)/shard_map/all_to_all | solution.py:167
  38.2 0.3 shard_map.84
  38.6 25.0 %all_to_all.20 = bf16[4,640,384]{2,1,0:T(8,128)(2,1)S(1)} all-to-all(bf16[4,640,384]{2,1,0:T(8,128)(2,1)S(1)} %shard_map.84), channel_id=1, replica_groups=mesh['z'=8,'y'=8,'x'=4,'c'=2] {'x'}, dimensions={0} | all-to-all | bytes 3932160 | tf_op jit(solution)/shard_map/all_to_all | solution.py:184
  63.6 6.6 %collective-permute-start = (bf16[4,640,384]{2,1,0:T(8,128)(2,1)S(1)}, bf16[4,640,384]{2,1,0:T(8,128)(2,1)S(1)}, u32[]{:S(2)}, u32[]{:S(2)}) collective-permute-start(bf16[4,640,384]{2,1,0:T(8,128)(2,1)S(1)} %all_to_all.20), channel_id=1, source_target_pairs={{0,1},{1,0},{2,3},{3,2},{4,5},{5,4},{6,7},{7,6},{8,9},{9,8},{10,11... | collective-permute-start | bytes 5898248 | tf_op jit(solution)/shard_map/ppermute | solution.py:185
  70.2 0.2 fusion.27
  70.4 0.2 convolution_add_fusion.7
  70.7 0.2 convolution_add_fusion.6
  70.9 0.2 convolution_add_fusion.5
  71.1 0.3 fusion.20
  71.5 0.3 convolution_add_fusion.3
  71.8 0.0 copy-start.3
  71.8 0.3 convolution_add_fusion.2
  72.2 0.0 copy-start.2
  72.2 0.3 convolution_add_fusion.1
  72.5 1.2 %collective-permute-done = bf16[4,640,384]{2,1,0:T(8,128)(2,1)S(1)} collective-permute-done((bf16[4,640,384]{2,1,0:T(8,128)(2,1)S(1)}, bf16[4,640,384]{2,1,0:T(8,128)(2,1)S(1)}, u32[]{:S(2)}, u32[]{:S(2)}) %collective-permute-start) | collective-permute-done | bytes 1966112 | tf_op jit(solution)/shard_map/ppermute | solution.py:185
  73.7 0.0 copy-done.3
  73.7 0.2 fusion.24
  74.0 0.2 fusion.25
  74.2 0.2 fusion.26
  74.5 0.0 copy-done.2
  74.5 0.3 fusion.10
  74.8 0.3 fusion.12
  75.1 0.3 fusion.14
  75.5 0.4 fusion.6
  75.8 0.4 fusion.23
  76.2 0.7 convolution_convert_fusion
  76.9 2.3 %collective-permute-start.1 = (bf16[320,1536]{1,0:T(8,128)(2,1)S(1)}, bf16[320,1536]{1,0:T(8,128)(2,1)S(1)}, u32[]{:S(2)}, u32[]{:S(2)}) collective-permute-start(bf16[320,1536]{1,0:T(8,128)(2,1)S(1)} %convolution_convert_fusion), channel_id=1, source_target_pairs={{0,1},{1,0},{2,3},{3,2},{4,5},{5,4},{6,7},{7,6},{8,9},{9,8},{10,11... | collective-permute-start | bytes 2949128 | tf_op jit(solution)/shard_map/ppermute | solution.py:204
  79.2 2.2 %collective-permute-done.1 = bf16[320,1536]{1,0:T(8,128)(2,1)S(1)} collective-permute-done((bf16[320,1536]{1,0:T(8,128)(2,1)S(1)}, bf16[320,1536]{1,0:T(8,128)(2,1)S(1)}, u32[]{:S(2)}, u32[]{:S(2)}) %collective-permute-start.1) | collective-permute-done | bytes 983072 | tf_op jit(solution)/shard_map/ppermute | solution.py:204
  81.4 0.7 add_convert_fusion
  82.1 0.1 copy.40
  82.2 0.0 copy-start.6
  82.2 0.0 copy-start.5
  82.2 16.2 %all_to_all.21.in_ref = bf16[4,320,384]{2,1,0:T(8,128)(2,1)S(1)} all-to-all(bf16[4,320,384]{2,1,0:T(8,128)(2,1)S(1)} %bitcast.89), channel_id=1, replica_groups=mesh['z'=8,'y'=8,'x'=4,'c'=2] {'x'}, dimensions={0} | all-to-all | bytes 1966080 | tf_op jit(solution)/shard_map/all_to_all | solution.py:207
  98.5 0.9 shard_map.85
  99.4 6.8 %all-to-all-start.3 = ((bf16[64,16,128]{2,1,0:T(8,128)(2,1)}), bf16[64,16,128]{2,1,0:T(8,128)(2,1)S(1)}, u32[]{:S(2)}, u32[]{:S(2)}) async-start(bf16[64,16,128]{2,1,0:T(8,128)(2,1)} %shard_map.85), calls=%async_computation.3 | async-start | bytes 524288 | tf_op jit(solution)/shard_map/all_to_all | solution.py:212
  106.2 0.0 copy-done.6
  106.2 0.1 copy.28.scale_ref
  106.4 0.0 copy-done.5
  106.4 0.1 copy.27.prob_ref
  106.5 0.4 shard_map.82.combine_ref
  106.9 11.9 %all-to-all-done.3.in_ref = bf16[64,16,128]{2,1,0:T(8,128)(2,1)S(1)} async-done(((bf16[64,16,128]{2,1,0:T(8,128)(2,1)}), bf16[64,16,128]{2,1,0:T(8,128)(2,1)S(1)}, u32[]{:S(2)}, u32[]{:S(2)}) %all-to-all-start.3) | async-done | bytes 262176 | tf_op jit(solution)/shard_map/all_to_all | solution.py:212
  118.8 0.6 shard_map.86
  119.4 0.7 copy.37
Async XLA Ops:
  3.8 20.1 %copy-start.4 = (bf16[1,3072,256]{2,1,0:T(8,128)(2,1)S(1)}, bf16[1,3072,256]{2,1,0:T(8,128)(2,1)}, u32[]{:S(2)}) copy-start(bf16[1,3072,256]{2,1,0:T(8,128)(2,1)} %param.14) | copy-start | bytes 4718596
  3.8 34.4 %all-to-all-start = ((bf16[64,32,128]{2,1,0:T(8,128)(2,1)}), bf16[64,32,128]{2,1,0:T(8,128)(2,1)S(1)}, u32[]{:S(2)}, u32[]{:S(2)}) async-start(bf16[64,32,128]{2,1,0:T(8,128)(2,1)} %bitcast.1), calls=%async_computation | async-start | bytes 1048576 | tf_op jit(solution)/shard_map/all_to_all | solution.py:167
  29.3 1.7 %copy-start = (bf16[2,4,3,8,16,256]{5,4,3,2,1,0:T(8,128)(2,1)S(1)}, bf16[2,4,3,8,16,256]{5,4,3,2,1,0:T(8,128)(2,1)}, u32[]{:S(2)}) copy-start(bf16[2,4,3,8,16,256]{5,4,3,2,1,0:T(8,128)(2,1)} %copy.32) | copy-start | bytes 4718596
  29.4 2.2 %copy-start.1 = (bf16[2,4,3,8,16,256]{5,4,3,2,1,0:T(8,128)(2,1)S(1)}, bf16[2,4,3,8,16,256]{5,4,3,2,1,0:T(8,128)(2,1)}, u32[]{:S(2)}) copy-start(bf16[2,4,3,8,16,256]{5,4,3,2,1,0:T(8,128)(2,1)} %copy.33) | copy-start | bytes 4718596
  63.6 10.2 %collective-permute-start = (bf16[4,640,384]{2,1,0:T(8,128)(2,1)S(1)}, bf16[4,640,384]{2,1,0:T(8,128)(2,1)S(1)}, u32[]{:S(2)}, u32[]{:S(2)}) collective-permute-start(bf16[4,640,384]{2,1,0:T(8,128)(2,1)S(1)} %all_to_all.20), channel_id=1, source_target_pairs={{0,1},{1,0},{2,3},{3,2},{4,5},{5,4},{6,7},{7,6},{8,9},{9,8},{10,11... | collective-permute-start | bytes 5898248 | tf_op jit(solution)/shard_map/ppermute | solution.py:185
  71.8 1.9 %copy-start.3 = (bf16[1536,256]{1,0:T(8,128)(2,1)S(1)}, bf16[1536,256]{1,0:T(8,128)(2,1)}, u32[]{:S(2)}) copy-start(bf16[1536,256]{1,0:T(8,128)(2,1)} %get-tuple-element.12) | copy-start | bytes 2359300
  72.2 2.3 %copy-start.2 = (bf16[1536,512]{1,0:T(8,128)(2,1)S(1)}, bf16[1536,512]{1,0:T(8,128)(2,1)}, u32[]{:S(2)}) copy-start(bf16[1536,512]{1,0:T(8,128)(2,1)} %get-tuple-element.14) | copy-start | bytes 4718596
  76.9 4.5 %collective-permute-start.1 = (bf16[320,1536]{1,0:T(8,128)(2,1)S(1)}, bf16[320,1536]{1,0:T(8,128)(2,1)S(1)}, u32[]{:S(2)}, u32[]{:S(2)}) collective-permute-start(bf16[320,1536]{1,0:T(8,128)(2,1)S(1)} %convolution_convert_fusion), channel_id=1, source_target_pairs={{0,1},{1,0},{2,3},{3,2},{4,5},{5,4},{6,7},{7,6},{8,9},{9,8},{10,11... | collective-permute-start | bytes 2949128 | tf_op jit(solution)/shard_map/ppermute | solution.py:204
  82.2 24.0 %copy-start.6 = (f32[128]{0:T(128)S(1)}, f32[128]{0:T(128)}, u32[]{:S(2)}) copy-start(f32[128]{0:T(128)} %param.10) | copy-start | bytes 1540
  82.2 24.1 %copy-start.5 = (f32[128,2]{0,1:T(2,128)S(1)}, f32[128,2]{0,1:T(2,128)}, u32[]{:S(2)}) copy-start(f32[128,2]{0,1:T(2,128)} %param.11) | copy-start | bytes 3076
  99.4 19.4 %all-to-all-start.3 = ((bf16[64,16,128]{2,1,0:T(8,128)(2,1)}), bf16[64,16,128]{2,1,0:T(8,128)(2,1)S(1)}, u32[]{:S(2)}, u32[]{:S(2)}) async-start(bf16[64,16,128]{2,1,0:T(8,128)(2,1)} %shard_map.85), calls=%async_computation.3 | async-start | bytes 524288 | tf_op jit(solution)/shard_map/all_to_all | solution.py:212

commit v3 on v2

--- a/solution.py
+++ b/solution.py
@@ -12,6 +12,7 @@
 F32 = jnp.float32
 LANES = 128
 FINE = 16
+AXES = ("z", "y", "x", "c")
 
 
 def backward_tail(gate, upper, back):
@@ -22,8 +23,8 @@
     return d_gate, d_upper
 
 
-def lane_layout(shape, capacity, parts):
-    lane = lax.broadcasted_iota(jnp.int32, shape, 1)
+def lane_layout(shape, axis, capacity, parts):
+    lane = lax.broadcasted_iota(jnp.int32, shape, axis)
     expert = lane // LANES
     inner = lane - expert * LANES
     part = inner // capacity
@@ -31,30 +32,31 @@
     return expert, part, slot
 
 
-def placement(ids_ref, tokens, lanes, capacity, parts):
-    expert, _, slot = lane_layout((tokens, lanes), capacity, parts)
-    first = ids_ref[:, 0:1] == expert
-    second = ids_ref[:, 1:2] == expert
+def placement(ids_ref, lanes, capacity, parts):
+    tokens = ids_ref.shape[1]
+    expert, _, slot = lane_layout((lanes, tokens), 0, capacity, parts)
+    first = ids_ref[0:1, :] == expert
+    second = ids_ref[1:2, :] == expert
     hit = first | second
     row = lax.broadcasted_iota(jnp.int32, (tokens, tokens), 0)
     col = lax.broadcasted_iota(jnp.int32, (tokens, tokens), 1)
-    below = jnp.where(col < row, 1.0, 0.0).astype(BF16)
+    earlier = jnp.where(row < col, 1.0, 0.0).astype(BF16)
     hit_bf = jnp.where(hit, 1.0, 0.0).astype(BF16)
-    before = jnp.dot(below, hit_bf, preferred_element_type=F32)
-    return hit & (before == slot.astype(F32)), first, second
+    before = jnp.dot(hit_bf, earlier, preferred_element_type=F32)
+    return hit & (before == slot.astype(F32)), first
 
 
 def pack_kernel(capacity, ids_ref, x_ref, g_ref, out_ref):
     nz, ny = out_ref.shape[:2]
-    tokens, feats = x_ref.shape
+    feats = x_ref.shape[0]
     parts = feats // FINE
     lanes = nz * LANES
-    place, _, _ = placement(ids_ref, tokens, lanes, capacity, parts)
+    place, _ = placement(ids_ref, lanes, capacity, parts)
     place = jnp.where(place, 1.0, 0.0).astype(BF16)
-    _, part, _ = lane_layout((FINE, lanes), capacity, parts)
+    _, part, _ = lane_layout((FINE, lanes), 1, capacity, parts)
     for kind, ref in enumerate((x_ref, g_ref)):
         spread = lax.dot_general(
-            ref[...], place, (((0,), (0,)), ((), ())), preferred_element_type=F32
+            ref[...], place, (((1,), (1,)), ((), ())), preferred_element_type=F32
         )
         block = jnp.zeros((FINE, lanes), F32)
         for p in range(parts):
@@ -105,14 +107,14 @@
 
 
 def combine_kernel(capacity, parts, ids_ref, prob_ref, scale_ref, out_ref):
-    tokens, lanes = out_ref.shape
-    place, first, _ = placement(ids_ref, tokens, lanes, capacity, parts)
-    prob = jnp.where(first, prob_ref[:, 0:1], prob_ref[:, 1:2])
+    lanes = out_ref.shape[0]
+    place, first = placement(ids_ref, lanes, capacity, parts)
+    prob = jnp.where(first, prob_ref[0:1, :], prob_ref[1:2, :])
     out_ref[...] = jnp.where(place, prob * scale_ref[...], 0.0)
 
 
 def final_kernel(capacity, parts, ny, combine_ref, in_ref, out_ref):
-    lanes = combine_ref.shape[1]
+    lanes = combine_ref.shape[0]
     nz = lanes // LANES
     sums = []
     for z in range(nz):
@@ -121,12 +123,12 @@
             total += in_ref[z * ny + y].astype(F32)
         sums.append(total)
     sums = jnp.concatenate(sums, axis=1)
-    _, part, _ = lane_layout(sums.shape, capacity, parts)
+    _, part, _ = lane_layout(sums.shape, 1, capacity, parts)
     spread = jnp.concatenate([jnp.where(part == p, sums, 0.0) for p in range(parts)], axis=0)
     out_ref[...] = lax.dot_general(
+        spread,
         combine_ref[...],
-        spread,
-        (((1,), (1,)), ((), ())),
+        (((1,), (0,)), ((), ())),
         precision=lax.Precision.HIGHEST,
         preferred_element_type=F32,
     ).astype(out_ref.dtype)
@@ -145,30 +147,58 @@
     )(*operands)
 
 
+def exchange_groups(nz, ny, nx, nc):
+    def index(z, y, x, c):
+        return ((z * ny + y % ny) * nx + x % nx) * nc + c
+
+    halves = [(yb, xb) for yb in range(2) for xb in range(2)]
+    places = [(2 * ya, 2 * xa) for ya in range(ny // 2) for xa in range(nx // 2)]
+    far = [
+        [index(z, y + yb, x + xb, c) for z in range(nz) for y, x in places]
+        for c in range(nc)
+        for yb, xb in halves
+    ]
+    near = [
+        [index(z, y + c + (yb + c) % 2, x + c + (xb + c) % 2, c) for yb, xb in halves]
+        for z in range(nz)
+        for c in range(nc)
+        for y, x in places
+    ]
+    return far, near
+
+
+def swap(blocks, groups):
+    return lax.all_to_all(
+        blocks, AXES, split_axis=0, concat_axis=0, axis_index_groups=groups, tiled=True
+    )
+
+
 def shards(activations, out_grad, token_scale, route_prob, route_ids, w_gate, w_up, w_down):
-    nz, ny, nx, nc = (lax.axis_size(a) for a in ("z", "y", "x", "c"))
+    nz, ny, nx, nc = (lax.axis_size(a) for a in AXES)
+    far, near = exchange_groups(nz, ny, nx, nc)
+    spread = ny * nx // 4
+    members = 4
     core = lax.axis_index("c")
     tokens, feats = activations.shape
     capacity = min(tokens, 5 * tokens // (2 * nz))
     parts = feats // FINE
     hidden = w_gate.shape[2]
     rows = nz * capacity
-    wide = feats * ny
+    wide = feats * spread
 
     send = call(
         functools.partial(pack_kernel, capacity),
-        (nz, ny, 2 * FINE, LANES),
-        BF16,
-        route_ids,
-        activations,
-        out_grad,
-    )
-    send = send.reshape(nz * ny, 2 * FINE, LANES)
-    got = lax.all_to_all(send, ("z", "y"), split_axis=0, concat_axis=0, tiled=True)
+        (nz, spread, 2 * FINE, LANES),
+        BF16,
+        route_ids.T,
+        activations.T,
+        out_grad.T,
+    )
+    got = swap(send.reshape(nz * spread, 2 * FINE, LANES), far)
 
     def ordered(w):
-        w = w.reshape(ny, nx, nc, parts, FINE, hidden).transpose(2, 1, 3, 0, 4, 5)
-        return w.reshape(nc, nx * wide, hidden)
+        w = w.reshape(ny // 2, 2, nx // 2, 2, nc, parts, FINE, hidden)
+        return w.transpose(4, 1, 3, 5, 0, 2, 6, 7).reshape(nc, members * wide, hidden)
 
     w_in = jnp.concatenate([ordered(w_gate[0]), ordered(w_up[0])], axis=2)
     w_dn = ordered(w_down[0].T)
@@ -179,14 +209,17 @@
     )
 
     copies = call(
-        functools.partial(unpack_kernel, capacity, parts, ny), (nx, 2 * rows, wide), BF16, got
-    )
-    own = lax.all_to_all(copies, "x", split_axis=0, concat_axis=0, tiled=True)
+        functools.partial(unpack_kernel, capacity, parts, spread),
+        (members, 2 * rows, wide),
+        BF16,
+        got,
+    )
+    own = swap(copies, near)
     other = lax.ppermute(own, "c", [(0, 1), (1, 0)])
 
     def forward(block, w_a, w_b):
         total_a, total_b = 0.0, 0.0
-        for i in range(nx):
+        for i in range(members):
             k = slice(i * wide, (i + 1) * wide)
             total_a += jnp.dot(block[i, :rows], w_a[k], preferred_element_type=F32)
             total_b += jnp.dot(block[i, rows:], w_b[k], preferred_element_type=F32)
@@ -203,29 +236,34 @@
 
     from_other = lax.ppermute(returned(in_other).astype(BF16), "c", [(0, 1), (1, 0)])
     part = (returned(in_own) + from_other.astype(F32)).astype(BF16)
-    part = part.reshape(rows, nx, wide).transpose(1, 0, 2)
-    part = lax.all_to_all(part, "x", split_axis=0, concat_axis=0, tiled=True)
-
+    part = swap(part.reshape(rows, members, wide).transpose(1, 0, 2), near)
     part = call(
-        functools.partial(repack_kernel, capacity, parts, ny), (nz * ny, FINE, LANES), BF16, part
-    )
-    part = lax.all_to_all(part, ("z", "y"), split_axis=0, concat_axis=0, tiled=True)
+        functools.partial(repack_kernel, capacity, parts, spread),
+        (nz * spread, FINE, LANES),
+        BF16,
+        part,
+    )
+    part = swap(part, far)
     combine = call(
         functools.partial(combine_kernel, capacity, parts),
-        (tokens, nz * LANES),
+        (nz * LANES, tokens),
         F32,
-        route_ids,
-        route_prob,
-        token_scale.reshape(tokens, 1),
+        route_ids.T,
+        route_prob.T,
+        token_scale.reshape(1, tokens),
     )
     return call(
-        functools.partial(final_kernel, capacity, parts, ny), (tokens, feats), BF16, combine, part
-    )
+        functools.partial(final_kernel, capacity, parts, spread),
+        (feats, tokens),
+        BF16,
+        combine,
+        part,
+    ).T
 
 
 def solution(mesh):
     devices = mesh.devices
-    fine = Mesh(devices.reshape(devices.shape[0], 8, 4, 2), ("z", "y", "x", "c"))
+    fine = Mesh(devices.reshape(devices.shape[0], 8, 4, 2), AXES)
     tensor = ("y", "x", "c")
     placed = (
         P("z", tensor),

time: 122 us -> 117 us (0.959); the launches traced: 120 us -> 116 us
  waiting for transfers between devices: 20.6 us -> 30.2 us
  blocking collectives: 41.2 us -> 32.2 us
  local copies, waits for them, and re-layouts: 13.9 us -> 10.8 us
  starting transfers between devices: 33 us -> 30.8 us
    all_to_all x2, waiting for transfers between devices: 17.2 us -> 26.8 us  [swap(): lax.all_to_all(blocks, AXES, split_axis=0, concat_axis=0, axis_index_grou...]
    all_to_all x2, blocking collectives: 41.2 us -> 32.2 us  [swap(): lax.all_to_all(blocks, AXES, split_axis=0, concat_axis=0, axis_index_grou...]
    ppermute x1, starting transfers between devices: 6.6 us -> 2.56 us  [shards(): other = lax.ppermute(own, 'c', [(0, 1), (1, 0)])]
    all_to_all x2, starting transfers between devices: 24.1 us -> 26 us  [swap(): lax.all_to_all(blocks, AXES, split_axis=0, concat_axis=0, axis_index_grou...]
    transpose x3, local copies, waits for them, and re-layouts: 5.69 us -> 4.37 us  [ordered(): w.transpose(4, 1, 3, 5, 0, 2, 6, 7).reshape(nc, members * wide, hidden)]
    unnamed x19 -> x27, local copies, waits for them, and re-layouts: 6.29 us -> 5.33 us
  transfers between devices with their start and end apart: 4 -> 4, of which waited for: 4 -> 4; matrix products, arithmetic and copies ran while one was open for 11% -> 9% of each run, Pallas kernels for 0% -> 1%
where the time goes in v3:
time: 117 us; the launch traced here: 116 us
  blocking collectives  32.2 us (28%)
  starting transfers between devices  30.8 us (26%)
  waiting for transfers between devices  30.2 us (26%)
  local copies, waits for them, and re-layouts  10.8 us (9%)
  matrix products  6.08 us (5%)
  Pallas kernels  4.61 us (4%)
  other arithmetic  1.42 us (1%)
    all_to_all x2, blocking collectives, swap(): lax.all_to_all(blocks, AXES, split_axis=0, concat_axis=0, axis_index_grou...  32.2 us
    all_to_all x2, waiting for transfers between devices, swap(): lax.all_to_all(blocks, AXES, split_axis=0, concat_axis=0, axis_index_grou...  26.8 us
    all_to_all x2, starting transfers between devices, swap(): lax.all_to_all(blocks, AXES, split_axis=0, concat_axis=0, axis_index_grou...  26 us
    unnamed x27, local copies, waits for them, and re-layouts  5.33 us
    pallas_call x5, Pallas kernels, call(): pl.pallas_call(kernel, out_shape=jax.ShapeDtypeStruct(shape, dtype), in_s...  4.61 us
    transpose x3, local copies, waits for them, and re-layouts, ordered(): w.transpose(4, 1, 3, 5, 0, 2, 6, 7).reshape(nc, members * wide, hidden)  4.37 us
    dot_general x8, matrix products, forward(): total_a += jnp.dot(block[i, :rows], w_a[k], preferred_element_type=F32)  2.65 us
    ppermute x1, starting transfers between devices, shards(): other = lax.ppermute(own, 'c', [(0, 1), (1, 0)])  2.56 us
  transfers between devices with their start and end apart: 4, of which 4 were waited for; matrix products, arithmetic and copies ran while one was open for 9% of the time, Pallas kernels for 1%

profile of v3, /device:TPU:1, one launch (start us, length us, event | category | flops | bytes accessed | tf_op | source)
XLA Modules:
  0.0 116.4 jit_solution(14170228415002475240)
XLA Ops:
  0.0 0.0 copy-start
  0.0 0.7 copy-done
  0.7 0.0 copy-start.1
  0.7 0.7 copy-done.1
  1.4 0.0 copy-start.2
  1.4 0.7 copy-done.2
  2.1 1.6 %shard_map.83 = bf16[8,8,32,128]{3,2,1,0:T(8,128)(2,1)} custom-call(s32[2,128]{1,0:T(2,128)S(1)} %bitcast.92, bf16[48,128]{1,0:T(8,128)(2,1)S(1)} %bitcast.90, bf16[48,128]{1,0:T(8,128)(2,1)S(1)} %bitcast.91), custom_call_target="tpu_custom_call" | custom-call | bytes 549888 | tf_op jit(solution)/shard_map/pallas_call | solution.py:140
  3.7 19.6 %all-to-all-start = ((bf16[64,32,128]{2,1,0:T(8,128)(2,1)}), bf16[64,32,128]{2,1,0:T(8,128)(2,1)S(1)}, u32[]{:S(2)}, u32[]{:S(2)}) async-start(bf16[64,32,128]{2,1,0:T(8,128)(2,1)} %bitcast.5), calls=%async_computation | async-start | bytes 1048576 | tf_op jit(solution)/shard_map/all_to_all | solution.py:171
  23.3 0.0 copy-start.11
  23.3 0.0 copy-done.10
  23.4 1.4 %copy.12 = bf16[2,2,2,3,4,2,16,256]{7,6,5,4,3,2,1,0:T(8,128)(2,1)} copy(bf16[2,2,2,3,4,2,16,256]{7,6,3,0,2,5,1,4:T(8,128)(2,1)S(1)} %bitcast.102) | data formatting | bytes 3145728 | tf_op jit(solution)/shard_map/transpose | solution.py:201
  24.8 0.5 copy-done.11
  25.2 1.3 %copy.13 = bf16[2,2,2,3,4,2,16,256]{7,6,5,4,3,2,1,0:T(8,128)(2,1)} copy(bf16[2,2,2,3,4,2,16,256]{7,6,3,0,2,5,1,4:T(8,128)(2,1)S(1)} %bitcast.103) | data formatting | bytes 3145728 | tf_op jit(solution)/shard_map/transpose | solution.py:201
  26.6 0.0 copy-done.12
  26.6 1.6 %copy.14 = bf16[1,256,3072]{1,2,0:T(8,128)(2,1)} copy(bf16[1,256,3072]{2,1,0:T(8,128)(2,1)S(1)} %copy-done.12) | data formatting | bytes 3145728 | tf_op args[7]
  28.1 1.6 %copy.15 = bf16[2,2,2,3,4,2,16,256]{7,6,5,4,3,2,1,0:T(8,128)(2,1)S(1)} copy(bf16[2,2,2,3,4,2,16,256]{7,6,3,0,2,5,1,4:T(8,128)(2,1)} %bitcast.97) | data formatting | bytes 3145728 | tf_op jit(solution)/shard_map/transpose | solution.py:201
  29.8 0.0 copy-start.6
  29.8 0.0 copy-start.7
  29.8 1.0 dynamic-slice_bitcast_fusion
  30.8 0.7 copy-done.6
  31.5 0.5 copy-done.7
  32.0 1.4 %fusion.1 = (bf16[1536,512]{1,0:T(8,128)(2,1)}, bf16[1536,512]{1,0:T(8,128)(2,1)S(1)}) fusion(s32[]{:T(128)S(6)} %select_n.11, bf16[2,1536,256]{2,1,0:T(8,128)(2,1)S(1)} %bitcast.98, bf16[2,1536,256]{2,1,0:T(8,128)(2,1)S(1)} %bitcast.99, s32[]{:T(128)S(6)} %select_n.10), kind=kLoop, calls=%fused_computation.7 | loop fusion | flops 6291456 | bytes 6291464 | tf_op jit(solution)/shard_map/jit(dynamic_index_in_dim)/squeeze | solution.py:205
  33.4 11.4 %all-to-all-done.in_ref = bf16[64,32,128]{2,1,0:T(8,128)(2,1)S(1)} async-done(((bf16[64,32,128]{2,1,0:T(8,128)(2,1)}), bf16[64,32,128]{2,1,0:T(8,128)(2,1)S(1)}, u32[]{:S(2)}, u32[]{:S(2)}) %all-to-all-start) | async-done | bytes 524320 | tf_op jit(solution)/shard_map/all_to_all | solution.py:171
  44.8 0.3 shard_map.84
  45.1 18.6 %all_to_all.20 = bf16[4,640,384]{2,1,0:T(8,128)(2,1)S(1)} all-to-all(bf16[4,640,384]{2,1,0:T(8,128)(2,1)S(1)} %shard_map.84), channel_id=1, replica_groups={{0,2,8,10},{4,6,12,14},{16,18,24,26},{20,22,28,30},{32,34,40,42},{36,38..., dimensions={0} | all-to-all | bytes 3932160 | tf_op jit(solution)/shard_map/all_to_all | solution.py:171
  63.7 2.6 %collective-permute-start = (bf16[4,640,384]{2,1,0:T(8,128)(2,1)S(1)}, bf16[4,640,384]{2,1,0:T(8,128)(2,1)S(1)}, u32[]{:S(2)}, u32[]{:S(2)}) collective-permute-start(bf16[4,640,384]{2,1,0:T(8,128)(2,1)S(1)} %all_to_all.20), channel_id=1, source_target_pairs={{0,1},{1,0},{2,3},{3,2},{4,5},{5,4},{6,7},{7,6},{8,9},{9,8},{10,11... | collective-permute-start | bytes 5898248 | tf_op jit(solution)/shard_map/ppermute | solution.py:218
  66.2 0.2 fusion.27
  66.5 0.2 convolution_add_fusion.7
  66.7 0.2 convolution_add_fusion.6
  67.0 0.2 convolution_add_fusion.5
  67.2 0.3 fusion.20
  67.6 0.3 convolution_add_fusion.3
  67.9 0.0 copy-start.9
  67.9 0.3 convolution_add_fusion.2
  68.2 0.0 copy-start.8
  68.3 0.3 convolution_add_fusion.1
  68.6 1.2 %collective-permute-done = bf16[4,640,384]{2,1,0:T(8,128)(2,1)S(1)} collective-permute-done((bf16[4,640,384]{2,1,0:T(8,128)(2,1)S(1)}, bf16[4,640,384]{2,1,0:T(8,128)(2,1)S(1)}, u32[]{:S(2)}, u32[]{:S(2)}) %collective-permute-start) | collective-permute-done | bytes 1966112 | tf_op jit(solution)/shard_map/ppermute | solution.py:218
  69.8 0.0 copy-done.9
  69.8 0.2 fusion.24
  70.1 0.2 fusion.25
  70.3 0.2 fusion.26
  70.6 0.0 copy-done.8
  70.6 0.3 fusion.10
  70.9 0.3 fusion.12
  71.2 0.3 fusion.14
  71.6 0.4 fusion.6
  71.9 0.3 fusion.23
  72.3 0.7 convolution_convert_fusion
  73.0 2.3 %collective-permute-start.1 = (bf16[320,1536]{1,0:T(8,128)(2,1)S(1)}, bf16[320,1536]{1,0:T(8,128)(2,1)S(1)}, u32[]{:S(2)}, u32[]{:S(2)}) collective-permute-start(bf16[320,1536]{1,0:T(8,128)(2,1)S(1)} %convolution_convert_fusion), channel_id=1, source_target_pairs={{0,1},{1,0},{2,3},{3,2},{4,5},{5,4},{6,7},{7,6},{8,9},{9,8},{10,11... | collective-permute-start | bytes 2949128 | tf_op jit(solution)/shard_map/ppermute | solution.py:237
  75.3 2.2 %collective-permute-done.1 = bf16[320,1536]{1,0:T(8,128)(2,1)S(1)} collective-permute-done((bf16[320,1536]{1,0:T(8,128)(2,1)S(1)}, bf16[320,1536]{1,0:T(8,128)(2,1)S(1)}, u32[]{:S(2)}, u32[]{:S(2)}) %collective-permute-start.1) | collective-permute-done | bytes 983072 | tf_op jit(solution)/shard_map/ppermute | solution.py:237
  77.4 0.7 add_convert_fusion
  78.2 0.1 copy.19
  78.3 0.0 copy-start.3
  78.3 0.0 copy-start.4
  78.3 0.0 copy-start.5
  78.3 13.6 %all_to_all.21.in_ref = bf16[4,320,384]{2,1,0:T(8,128)(2,1)S(1)} all-to-all(bf16[4,320,384]{2,1,0:T(8,128)(2,1)S(1)} %bitcast.100), channel_id=1, replica_groups={{0,2,8,10},{4,6,12,14},{16,18,24,26},{20,22,28,30},{32,34,40,42},{36,38..., dimensions={0} | all-to-all | bytes 1966080 | tf_op jit(solution)/shard_map/all_to_all | solution.py:171
  91.9 0.9 shard_map.85
  92.8 6.4 %all-to-all-start.3 = ((bf16[64,16,128]{2,1,0:T(8,128)(2,1)}), bf16[64,16,128]{2,1,0:T(8,128)(2,1)S(1)}, u32[]{:S(2)}, u32[]{:S(2)}) async-start(bf16[64,16,128]{2,1,0:T(8,128)(2,1)} %shard_map.85), calls=%async_computation.3 | async-start | bytes 524288 | tf_op jit(solution)/shard_map/all_to_all | solution.py:171
  99.1 0.0 copy-done.3
  99.2 0.0 copy-done.4
  99.2 0.0 copy-done.5
  99.2 0.7 shard_map.82.combine_ref
  99.9 15.5 %all-to-all-done.3.in_ref = bf16[64,16,128]{2,1,0:T(8,128)(2,1)S(1)} async-done(((bf16[64,16,128]{2,1,0:T(8,128)(2,1)}), bf16[64,16,128]{2,1,0:T(8,128)(2,1)S(1)}, u32[]{:S(2)}, u32[]{:S(2)}) %all-to-all-start.3) | async-done | bytes 262176 | tf_op jit(solution)/shard_map/all_to_all | solution.py:171
  115.4 1.0 shard_map.86
  (2 shorter events, 0.0 us)
Async XLA Ops:
  0.0 0.7 copy-start
  0.7 0.7 copy-start.1
  1.4 0.7 copy-start.2
  2.1 21.3 %copy-start.10 = (bf16[1,3072,256]{2,1,0:T(8,128)(2,1)S(1)}, bf16[1,3072,256]{2,1,0:T(8,128)(2,1)}, u32[]{:S(2)}) copy-start(bf16[1,3072,256]{2,1,0:T(8,128)(2,1)} %param.13) | copy-start | bytes 4718596
  3.7 41.0 %all-to-all-start = ((bf16[64,32,128]{2,1,0:T(8,128)(2,1)}), bf16[64,32,128]{2,1,0:T(8,128)(2,1)S(1)}, u32[]{:S(2)}, u32[]{:S(2)}) async-start(bf16[64,32,128]{2,1,0:T(8,128)(2,1)} %bitcast.5), calls=%async_computation | async-start | bytes 1048576 | tf_op jit(solution)/shard_map/all_to_all | solution.py:171
  23.3 1.9 %copy-start.11 = (bf16[1,3072,256]{2,1,0:T(8,128)(2,1)S(1)}, bf16[1,3072,256]{2,1,0:T(8,128)(2,1)}, u32[]{:S(2)}) copy-start(bf16[1,3072,256]{2,1,0:T(8,128)(2,1)} %param.14) | copy-start | bytes 4718596
  24.8 1.8 %copy-start.12 = (bf16[1,256,3072]{2,1,0:T(8,128)(2,1)S(1)}, bf16[1,256,3072]{2,1,0:T(8,128)(2,1)}, u32[]{:S(2)}) copy-start(bf16[1,256,3072]{2,1,0:T(8,128)(2,1)} %param.15) | copy-start | bytes 4718596
  29.8 1.7 %copy-start.6 = (bf16[2,2,2,3,4,2,16,256]{7,6,5,4,3,2,1,0:T(8,128)(2,1)S(1)}, bf16[2,2,2,3,4,2,16,256]{7,6,5,4,3,2,1,0:T(8,128)(2,1)}, u32[]{:S(2)}) copy-start(bf16[2,2,2,3,4,2,16,256]{7,6,5,4,3,2,1,0:T(8,128)(2,1)} %copy.12) | copy-start | bytes 4718596
  29.8 2.2 %copy-start.7 = (bf16[2,2,2,3,4,2,16,256]{7,6,5,4,3,2,1,0:T(8,128)(2,1)S(1)}, bf16[2,2,2,3,4,2,16,256]{7,6,5,4,3,2,1,0:T(8,128)(2,1)}, u32[]{:S(2)}) copy-start(bf16[2,2,2,3,4,2,16,256]{7,6,5,4,3,2,1,0:T(8,128)(2,1)} %copy.13) | copy-start | bytes 4718596
  63.7 6.1 %collective-permute-start = (bf16[4,640,384]{2,1,0:T(8,128)(2,1)S(1)}, bf16[4,640,384]{2,1,0:T(8,128)(2,1)S(1)}, u32[]{:S(2)}, u32[]{:S(2)}) collective-permute-start(bf16[4,640,384]{2,1,0:T(8,128)(2,1)S(1)} %all_to_all.20), channel_id=1, source_target_pairs={{0,1},{1,0},{2,3},{3,2},{4,5},{5,4},{6,7},{7,6},{8,9},{9,8},{10,11... | collective-permute-start | bytes 5898248 | tf_op jit(solution)/shard_map/ppermute | solution.py:218
  67.9 1.9 %copy-start.9 = (bf16[1536,256]{1,0:T(8,128)(2,1)S(1)}, bf16[1536,256]{1,0:T(8,128)(2,1)}, u32[]{:S(2)}) copy-start(bf16[1536,256]{1,0:T(8,128)(2,1)} %get-tuple-element.12) | copy-start | bytes 2359300
  68.2 2.3 %copy-start.8 = (bf16[1536,512]{1,0:T(8,128)(2,1)S(1)}, bf16[1536,512]{1,0:T(8,128)(2,1)}, u32[]{:S(2)}) copy-start(bf16[1536,512]{1,0:T(8,128)(2,1)} %get-tuple-element.14) | copy-start | bytes 4718596
  73.0 4.5 %collective-permute-start.1 = (bf16[320,1536]{1,0:T(8,128)(2,1)S(1)}, bf16[320,1536]{1,0:T(8,128)(2,1)S(1)}, u32[]{:S(2)}, u32[]{:S(2)}) collective-permute-start(bf16[320,1536]{1,0:T(8,128)(2,1)S(1)} %convolution_convert_fusion), channel_id=1, source_target_pairs={{0,1},{1,0},{2,3},{3,2},{4,5},{5,4},{6,7},{7,6},{8,9},{9,8},{10,11... | collective-permute-start | bytes 2949128 | tf_op jit(solution)/shard_map/ppermute | solution.py:237
  78.3 20.9 %copy-start.3 = (s32[128,2]{0,1:T(2,128)S(1)}, s32[128,2]{0,1:T(2,128)}, u32[]{:S(2)}) copy-start(s32[128,2]{0,1:T(2,128)} %param.12) | copy-start | bytes 3076
  78.3 20.9 %copy-start.4 = (f32[128,2]{0,1:T(2,128)S(1)}, f32[128,2]{0,1:T(2,128)}, u32[]{:S(2)}) copy-start(f32[128,2]{0,1:T(2,128)} %param.11) | copy-start | bytes 3076
  78.3 20.9 %copy-start.5 = (f32[128]{0:T(128)S(1)}, f32[128]{0:T(128)}, u32[]{:S(2)}) copy-start(f32[128]{0:T(128)} %param.10) | copy-start | bytes 1540
  92.8 22.6 %all-to-all-start.3 = ((bf16[64,16,128]{2,1,0:T(8,128)(2,1)}), bf16[64,16,128]{2,1,0:T(8,128)(2,1)S(1)}, u32[]{:S(2)}, u32[]{:S(2)}) async-start(bf16[64,16,128]{2,1,0:T(8,128)(2,1)} %shard_map.85), calls=%async_computation.3 | async-start | bytes 524288 | tf_op jit(solution)/shard_map/all_to_all | solution.py:171

commit v4 on v3

--- a/solution.py
+++ b/solution.py
@@ -23,38 +23,51 @@
     return d_gate, d_upper
 
 
-def lane_layout(shape, axis, capacity, parts):
-    lane = lax.broadcasted_iota(jnp.int32, shape, axis)
-    expert = lane // LANES
-    inner = lane - expert * LANES
+def lane_parts(shape, axis, capacity):
+    inner = lax.broadcasted_iota(jnp.int32, shape, axis) % LANES
+    return inner // capacity
+
+
+def lane_slots(tokens, capacity, parts):
+    inner = lax.broadcasted_iota(jnp.int32, (LANES, tokens), 0)
     part = inner // capacity
-    slot = jnp.where(part < parts, inner - part * capacity, -1)
-    return expert, part, slot
-
-
-def placement(ids_ref, lanes, capacity, parts):
-    tokens = ids_ref.shape[1]
-    expert, _, slot = lane_layout((lanes, tokens), 0, capacity, parts)
-    first = ids_ref[0:1, :] == expert
-    second = ids_ref[1:2, :] == expert
-    hit = first | second
+    return jnp.where(part < parts, inner - part * capacity, -1).astype(F32)
+
+
+def token_slots(ids, experts):
+    tokens = ids.shape[1]
+    expert = lax.broadcasted_iota(jnp.int32, (experts, tokens), 0)
+    first = ids[0:1, :] == expert
+    hit = first | (ids[1:2, :] == expert)
     row = lax.broadcasted_iota(jnp.int32, (tokens, tokens), 0)
     col = lax.broadcasted_iota(jnp.int32, (tokens, tokens), 1)
     earlier = jnp.where(row < col, 1.0, 0.0).astype(BF16)
     hit_bf = jnp.where(hit, 1.0, 0.0).astype(BF16)
     before = jnp.dot(hit_bf, earlier, preferred_element_type=F32)
-    return hit & (before == slot.astype(F32)), first
-
-
-def pack_kernel(capacity, ids_ref, x_ref, g_ref, out_ref):
-    nz, ny = out_ref.shape[:2]
-    feats = x_ref.shape[0]
+    return jnp.where(hit, before, -2.0), first
+
+
+def pack_kernel(capacity, ids_hbm, x_hbm, g_hbm, out_ref, ids_ref, x_ref, g_ref, sems):
+    copies = [
+        pltpu.make_async_copy(src, dst, sems.at[i])
+        for i, (src, dst) in enumerate(((ids_hbm, ids_ref), (x_hbm, x_ref), (g_hbm, g_ref)))
+    ]
+    for copy in copies:
+        copy.start()
+    nz, members = out_ref.shape[:2]
+    feats, tokens = x_ref.shape
     parts = feats // FINE
     lanes = nz * LANES
-    place, _ = placement(ids_ref, lanes, capacity, parts)
-    place = jnp.where(place, 1.0, 0.0).astype(BF16)
-    _, part, _ = lane_layout((FINE, lanes), 1, capacity, parts)
+    part = lane_parts((FINE, lanes), 1, capacity)
+    slot_of_lane = lane_slots(tokens, capacity, parts)
+    copies[0].wait()
+    slots, _ = token_slots(ids_ref[...], nz)
+    place = jnp.concatenate(
+        [jnp.where(slots[z : z + 1] == slot_of_lane, 1.0, 0.0).astype(BF16) for z in range(nz)],
+        axis=0,
+    )
     for kind, ref in enumerate((x_ref, g_ref)):
+        copies[1 + kind].wait()
         spread = lax.dot_general(
             ref[...], place, (((1,), (1,)), ((), ())), preferred_element_type=F32
         )
@@ -63,8 +76,8 @@
             block = jnp.where(part == p, spread[p * FINE : (p + 1) * FINE], block)
         block = block.astype(BF16)
         for z in range(nz):
-            for y in range(ny):
-                out_ref[z, y, kind * FINE : (kind + 1) * FINE, :] = block[
+            for m in range(members):
+                out_ref[z, m, kind * FINE : (kind + 1) * FINE, :] = block[
                     :, z * LANES : (z + 1) * LANES
                 ]
 
@@ -106,11 +119,82 @@
             out_ref[z * ny : (z + 1) * ny] = turned.reshape(ny, FINE, LANES)
 
 
+def order_kernel(gate_hbm, up_hbm, down_hbm, own_ref, sent_ref, sems):
+    core = lax.axis_index("c")
+    hidden = gate_hbm.shape[-1]
+    copies = []
+    for out_ref, c in ((own_ref, core), (sent_ref, 1 - core)):
+        for k, src in enumerate((gate_hbm, up_hbm, down_hbm)):
+            lanes = pl.ds(k * hidden, hidden)
+            for yb in range(2):
+                for xb in range(2):
+                    for p in range(src.shape[5]):
+                        copies.append(
+                            pltpu.make_async_copy(
+                                src.at[:, yb, :, xb, c, p],
+                                out_ref.at[2 * yb + xb, p, :, :, :, lanes],
+                                sems.at[len(copies)],
+                            )
+                        )
+    for copy in copies:
+        copy.start()
+    for copy in copies:
+        copy.wait()
+
+
+def project_kernel(in_ref, w_ref, out_ref):
+    members = in_ref.shape[0]
+    rows, wide = out_ref.shape
+    split = wide // 3 * 2
+    x = jnp.concatenate([in_ref[i, :rows, :] for i in range(members)], axis=1)
+    out_ref[:, :split] = jnp.dot(x, w_ref[:, :split], preferred_element_type=F32)
+    g = jnp.concatenate([in_ref[i, rows:, :] for i in range(members)], axis=1)
+    out_ref[:, split:] = jnp.dot(g, w_ref[:, split:], preferred_element_type=F32)
+
+
+def tail_kernel(a_ref, b_ref, out_ref):
+    hidden = a_ref.shape[1] // 3
+    gate, upper, back = (
+        a_ref[:, k * hidden : (k + 1) * hidden] + b_ref[:, k * hidden : (k + 1) * hidden]
+        for k in range(3)
+    )
+    d_gate, d_upper = backward_tail(gate, upper, back)
+    out_ref[:, :hidden] = d_gate
+    out_ref[:, hidden:] = d_upper
+
+
+def return_kernel(d_ref, w_ref, out_ref):
+    out_ref[...] = lax.dot_general(
+        d_ref[...],
+        w_ref[:, : d_ref.shape[1]],
+        (((1,), (1,)), ((), ())),
+        preferred_element_type=F32,
+    )
+
+
+def return_add_kernel(d_ref, w_ref, sum_ref, out_ref):
+    members, _, wide = out_ref.shape
+    for i in range(members):
+        here = slice(i * wide, (i + 1) * wide)
+        total = lax.dot_general(
+            d_ref[...],
+            w_ref[here, : d_ref.shape[1]],
+            (((1,), (1,)), ((), ())),
+            preferred_element_type=F32,
+        )
+        out_ref[i] = (total + sum_ref[:, here]).astype(out_ref.dtype)
+
+
 def combine_kernel(capacity, parts, ids_ref, prob_ref, scale_ref, out_ref):
-    lanes = out_ref.shape[0]
-    place, first = placement(ids_ref, lanes, capacity, parts)
-    prob = jnp.where(first, prob_ref[0:1, :], prob_ref[1:2, :])
-    out_ref[...] = jnp.where(place, prob * scale_ref[...], 0.0)
+    lanes, tokens = out_ref.shape
+    experts = lanes // LANES
+    slots, first = token_slots(ids_ref[...], experts)
+    weights = jnp.where(first, prob_ref[0:1, :], prob_ref[1:2, :]) * scale_ref[...]
+    slot_of_lane = lane_slots(tokens, capacity, parts)
+    for z in range(experts):
+        out_ref[z * LANES : (z + 1) * LANES, :] = jnp.where(
+            slots[z : z + 1] == slot_of_lane, weights[z : z + 1], 0.0
+        )
 
 
 def final_kernel(capacity, parts, ny, combine_ref, in_ref, out_ref):
@@ -123,7 +207,7 @@
             total += in_ref[z * ny + y].astype(F32)
         sums.append(total)
     sums = jnp.concatenate(sums, axis=1)
-    _, part, _ = lane_layout(sums.shape, 1, capacity, parts)
+    part = lane_parts(sums.shape, 1, capacity)
     spread = jnp.concatenate([jnp.where(part == p, sums, 0.0) for p in range(parts)], axis=0)
     out_ref[...] = lax.dot_general(
         spread,
@@ -134,14 +218,15 @@
     ).astype(out_ref.dtype)
 
 
-def call(kernel, shape, dtype, *operands, flops=0):
+def call(kernel, shape, dtype, *operands, flops=0, spaces=pltpu.VMEM, scratch=()):
     moved = sum(o.size * o.dtype.itemsize for o in operands)
     moved += math.prod(shape) * jnp.dtype(dtype).itemsize
     return pl.pallas_call(
         kernel,
         out_shape=jax.ShapeDtypeStruct(shape, dtype),
-        in_specs=[pl.BlockSpec(memory_space=pltpu.VMEM)] * len(operands),
+        in_specs=[pl.BlockSpec(memory_space=spaces)] * len(operands),
         out_specs=pl.BlockSpec(memory_space=pltpu.VMEM),
+        scratch_shapes=scratch,
         compiler_params=pltpu.CompilerParams(vmem_limit_bytes=32 * 1024 * 1024),
         cost_estimate=pl.CostEstimate(flops=flops, bytes_accessed=moved, transcendentals=0),
     )(*operands)
@@ -173,6 +258,10 @@
     )
 
 
+def other_core(values):
+    return lax.ppermute(values, "c", [(0, 1), (1, 0)])
+
+
 def shards(activations, out_grad, token_scale, route_prob, route_ids, w_gate, w_up, w_down):
     nz, ny, nx, nc = (lax.axis_size(a) for a in AXES)
     far, near = exchange_groups(nz, ny, nx, nc)
@@ -193,20 +282,29 @@
         route_ids.T,
         activations.T,
         out_grad.T,
+        spaces=pl.ANY,
+        scratch=(
+            pltpu.VMEM(route_ids.T.shape, route_ids.dtype),
+            pltpu.VMEM((feats, tokens), BF16),
+            pltpu.VMEM((feats, tokens), BF16),
+            pltpu.SemaphoreType.DMA((3,)),
+        ),
     )
     got = swap(send.reshape(nz * spread, 2 * FINE, LANES), far)
 
-    def ordered(w):
-        w = w.reshape(ny // 2, 2, nx // 2, 2, nc, parts, FINE, hidden)
-        return w.transpose(4, 1, 3, 5, 0, 2, 6, 7).reshape(nc, members * wide, hidden)
-
-    w_in = jnp.concatenate([ordered(w_gate[0]), ordered(w_up[0])], axis=2)
-    w_dn = ordered(w_down[0].T)
-    in_own, in_other = (lax.dynamic_index_in_dim(w_in, i, 0, False) for i in (core, 1 - core))
-    dn_own, dn_other = (lax.dynamic_index_in_dim(w_dn, i, 0, False) for i in (core, 1 - core))
-    got, in_own, in_other, dn_own, dn_other = lax.optimization_barrier(
-        (got, in_own, in_other, dn_own, dn_other)
-    )
+    views = (ny // 2, 2, nx // 2, 2, nc, parts, FINE, hidden)
+    ordered = (members, parts, ny // 2, nx // 2, FINE, 3 * hidden)
+    own, sent = pl.pallas_call(
+        order_kernel,
+        out_shape=[jax.ShapeDtypeStruct(ordered, BF16)] * 2,
+        in_specs=[pl.BlockSpec(memory_space=pl.ANY)] * 3,
+        out_specs=[pl.BlockSpec(memory_space=pltpu.VMEM)] * 2,
+        scratch_shapes=[pltpu.SemaphoreType.DMA((2 * 3 * members * parts,))],
+        compiler_params=pltpu.CompilerParams(vmem_limit_bytes=32 * 1024 * 1024),
+        cost_estimate=pl.CostEstimate(flops=0, bytes_accessed=12 * 1024 * 1024, transcendentals=0),
+    )(w_gate.reshape(views), w_up.reshape(views), w_down[0].T.reshape(views))
+    own, sent = (w.reshape(members * wide, 3 * hidden) for w in (own, sent))
+    got, own = lax.optimization_barrier((got, own))
 
     copies = call(
         functools.partial(unpack_kernel, capacity, parts, spread),
@@ -214,29 +312,21 @@
         BF16,
         got,
     )
-    own = swap(copies, near)
-    other = lax.ppermute(own, "c", [(0, 1), (1, 0)])
-
-    def forward(block, w_a, w_b):
-        total_a, total_b = 0.0, 0.0
-        for i in range(members):
-            k = slice(i * wide, (i + 1) * wide)
-            total_a += jnp.dot(block[i, :rows], w_a[k], preferred_element_type=F32)
-            total_b += jnp.dot(block[i, rows:], w_b[k], preferred_element_type=F32)
-        return total_a, total_b
-
-    in_a, back_a = forward(own, in_own, dn_own)
-    in_b, back_b = forward(other, in_other, dn_other)
-    both = in_a + in_b
-    d_gate, d_upper = backward_tail(both[:, :hidden], both[:, hidden:], back_a + back_b)
-    d_both = jnp.concatenate([d_gate, d_upper], axis=1)
-
-    def returned(w):
-        return lax.dot_general(d_both, w, (((1,), (1,)), ((), ())), preferred_element_type=F32)
-
-    from_other = lax.ppermute(returned(in_other).astype(BF16), "c", [(0, 1), (1, 0)])
-    part = (returned(in_own) + from_other.astype(F32)).astype(BF16)
-    part = swap(part.reshape(rows, members, wide).transpose(1, 0, 2), near)
+    block = swap(copies, near)
+
+    other = other_core(sent)
+    flops = 2 * rows * members * wide * 3 * hidden
+
+    def project(w):
+        return call(project_kernel, (rows, 3 * hidden), F32, block, w, flops=flops)
+
+    theirs = other_core(project(other))
+    d_own = call(tail_kernel, (rows, 2 * hidden), BF16, project(own), theirs)
+    d_other = other_core(d_own)
+    flops = flops // 3 * 2
+    part = call(return_kernel, (rows, members * wide), F32, d_own, own, flops=flops)
+    part = call(return_add_kernel, (members, rows, wide), BF16, d_other, other, part, flops=flops)
+    part = swap(part, near)
     part = call(
         functools.partial(repack_kernel, capacity, parts, spread),
         (nz * spread, FINE, LANES),

time: 117 us -> 117 us (level)
  blocking collectives: 32.2 us -> 13.6 us
  waiting for transfers between devices: 30.2 us -> 39.7 us
  starting transfers between devices: 30.8 us -> 40.2 us
  matrix products: 6.08 us -> 0 us
  Pallas kernels: 4.61 us -> 8.63 us
  local copies, waits for them, and re-layouts: 10.8 us -> 13.9 us
  other arithmetic: 1.42 us -> 0 us
    all_to_all x2 -> x1, blocking collectives: 32.2 us -> 13.6 us  [swap(): lax.all_to_all(blocks, AXES, split_axis=0, concat_axis=0, axis_index_grou...]
    unnamed x27 -> x30, local copies, waits for them, and re-layouts: 5.33 us -> 12.2 us
    all_to_all x2 -> x3, waiting for transfers between devices: 26.8 us -> 33.6 us  [swap(): lax.all_to_all(blocks, AXES, split_axis=0, concat_axis=0, axis_index_grou...]
    dot_general x18 -> x0, matrix products: 6.08 us -> none  [the longest x8 2.65 us: forward(): total_a += jnp.dot(block[i, :rows], w_a[k], preferred_element_type=F32)]
    ppermute x2 -> x3, starting transfers between devices: 4.84 us -> 10 us  [other_core(): return lax.ppermute(values, 'c', [(0, 1), (1, 0)])]
    all_to_all x2 -> x3, starting transfers between devices: 26 us -> 30.1 us  [swap(): lax.all_to_all(blocks, AXES, split_axis=0, concat_axis=0, axis_index_grou...]
    pallas_call x5 -> x10, Pallas kernels: 4.61 us -> 7.42 us  [call(): pl.pallas_call(kernel, out_shape=jax.ShapeDtypeStruct(shape, dtype), in_s...]
    ppermute x2 -> x3, waiting for transfers between devices: 3.39 us -> 6.11 us  [other_core(): return lax.ppermute(values, 'c', [(0, 1), (1, 0)])]
  transfers between devices with their start and end apart: 4 -> 6, of which waited for: 4 -> 6; matrix products, arithmetic and copies ran while one was open for 9% -> 1% of each run, Pallas kernels for 1% -> 3%
where the time goes in v4:
time: 117 us; the launch traced here: 116 us
  starting transfers between devices  40.2 us (34%)
  waiting for transfers between devices  39.7 us (34%)
  local copies, waits for them, and re-layouts  13.9 us (12%)
  blocking collectives  13.6 us (12%)
  Pallas kernels  8.63 us (7%)
    all_to_all x3, waiting for transfers between devices, swap(): lax.all_to_all(blocks, AXES, split_axis=0, concat_axis=0, axis_index_grou...  33.6 us
    all_to_all x3, starting transfers between devices, swap(): lax.all_to_all(blocks, AXES, split_axis=0, concat_axis=0, axis_index_grou...  30.1 us
    all_to_all x1, blocking collectives, swap(): lax.all_to_all(blocks, AXES, split_axis=0, concat_axis=0, axis_index_grou...  13.6 us
    unnamed x30, local copies, waits for them, and re-layouts  12.2 us
    ppermute x3, starting transfers between devices, other_core(): return lax.ppermute(values, 'c', [(0, 1), (1, 0)])  10 us
    pallas_call x10, Pallas kernels, call(): pl.pallas_call(kernel, out_shape=jax.ShapeDtypeStruct(shape, dtype), in_s...  7.42 us
    ppermute x3, waiting for transfers between devices, other_core(): return lax.ppermute(values, 'c', [(0, 1), (1, 0)])  6.11 us
  transfers between devices with their start and end apart: 6, of which 6 were waited for; matrix products, arithmetic and copies ran while one was open for 1% of the time, Pallas kernels for 3%

profile of v4, /device:TPU:1, one launch (start us, length us, event | category | flops | bytes accessed | tf_op | source)
XLA Modules:
  0.0 116.1 jit_solution(11915756340106327215)
XLA Ops:
  0.0 0.0 copy-start.8
  0.0 0.7 copy-done.8
  0.7 0.0 copy-start.9
  0.7 0.7 copy-done.9
  1.4 0.0 copy-start.10
  1.4 0.7 copy-done.10
  2.1 1.4 %shard_map.83 = bf16[8,8,32,128]{3,2,1,0:T(8,128)(2,1)} custom-call(s32[2,128]{1,0:T(2,128)S(1)} %bitcast.22, bf16[48,128]{1,0:T(8,128)(2,1)S(1)} %bitcast.20, bf16[48,128]{1,0:T(8,128)(2,1)S(1)} %bitcast.21), custom_call_target="tpu_custom_call" | custom-call | bytes 549888 | tf_op jit(solution)/shard_map/pallas_call | solution.py:224
  3.5 19.6 %all-to-all-start = ((bf16[64,32,128]{2,1,0:T(8,128)(2,1)}), bf16[64,32,128]{2,1,0:T(8,128)(2,1)S(1)}, u32[]{:S(2)}, u32[]{:S(2)}) async-start(bf16[64,32,128]{2,1,0:T(8,128)(2,1)} %bitcast.5), calls=%async_computation | async-start | bytes 1048576 | tf_op jit(solution)/shard_map/all_to_all | solution.py:256
  23.2 1.7 %copy.9 = bf16[3072,256]{1,0:T(8,128)(2,1)S(1)} copy(bf16[3072,256]{0,1:T(8,128)(2,1)} %bitcast.27) | data formatting | bytes 3145728 | tf_op jit(solution)/shard_map/transpose | solution.py:305
  24.9 0.0 copy-start.6
  24.9 1.4 %copy-done.6 = bf16[1,3072,256]{2,1,0:T(8,128)(2,1)S(1)} copy-done((bf16[1,3072,256]{2,1,0:T(8,128)(2,1)S(1)}, bf16[1,3072,256]{2,1,0:T(8,128)(2,1)}, u32[]{:S(2)}) %copy-start.6) | copy-done | bytes 1572888
  26.3 0.0 copy-start.7
  26.3 1.4 %copy-done.7 = bf16[1,3072,256]{2,1,0:T(8,128)(2,1)S(1)} copy-done((bf16[1,3072,256]{2,1,0:T(8,128)(2,1)S(1)}, bf16[1,3072,256]{2,1,0:T(8,128)(2,1)}, u32[]{:S(2)}) %copy-start.7) | copy-done | bytes 1572888
  27.7 1.2 %shard_map.84 = (bf16[4,3,4,2,16,768]{5,4,3,2,1,0:T(8,128)(2,1)S(1)}, bf16[4,3,4,2,16,768]{5,4,3,2,1,0:T(8,128)(2,1)S(1)}) custom-call(bf16[4,2,2,2,2,3,16,256]{7,6,5,4,3,2,1,0:T(8,128)(2,1)S(1)} %bitcast.18, bf16[4,2,2,2,2,3,16,256]{7,6,5,4,3,2,1,0:T(8,128)(2,1)S(1)} %bitcast.19, bf16[4,2,2,2,2,3,16,256]{7,6,5,4,3,2,1,0:T(8,128)(2,1)S(1)} %bitcast.17), custom_call_target="tpu_custom_call" | custom-call | bytes 12582912 | tf_op jit(solution)/shard_map/pallas_call | solution.py:297
  28.9 0.0 copy-start
  28.9 1.4 %copy-done = bf16[4,3,4,2,16,768]{5,4,3,2,1,0:T(8,128)(2,1)} copy-done((bf16[4,3,4,2,16,768]{5,4,3,2,1,0:T(8,128)(2,1)}, bf16[4,3,4,2,16,768]{5,4,3,2,1,0:T(8,128)(2,1)S(1)}, u32[]{:S(2)}) %copy-start) | copy-done | bytes 2359320
  30.3 0.0 copy-start.14
  30.3 1.4 %copy-done.14 = bf16[4,3,4,2,16,768]{5,4,3,2,1,0:T(8,128)(2,1)} copy-done((bf16[4,3,4,2,16,768]{5,4,3,2,1,0:T(8,128)(2,1)}, bf16[4,3,4,2,16,768]{5,4,3,2,1,0:T(8,128)(2,1)S(1)}, u32[]{:S(2)}) %copy-start.14) | copy-done | bytes 2359320
  31.8 12.8 %all-to-all-done.in_ref = bf16[64,32,128]{2,1,0:T(8,128)(2,1)S(1)} async-done(((bf16[64,32,128]{2,1,0:T(8,128)(2,1)}), bf16[64,32,128]{2,1,0:T(8,128)(2,1)S(1)}, u32[]{:S(2)}, u32[]{:S(2)}) %all-to-all-start) | async-done | bytes 524320 | tf_op jit(solution)/shard_map/all_to_all | solution.py:256
  44.6 0.3 shard_map.85
  44.9 0.0 copy-start.5
  44.9 1.3 %copy-done.5 = bf16[4,640,384]{2,1,0:T(8,128)(2,1)} copy-done((bf16[4,640,384]{2,1,0:T(8,128)(2,1)}, bf16[4,640,384]{2,1,0:T(8,128)(2,1)S(1)}, u32[]{:S(2)}) %copy-start.5) | copy-done | bytes 1966104
  46.2 3.6 %all-to-all-start.1 = ((bf16[4,640,384]{2,1,0:T(8,128)(2,1)}), bf16[4,640,384]{2,1,0:T(8,128)(2,1)S(1)}, u32[]{:S(2)}, u32[]{:S(2)}) async-start(bf16[4,640,384]{2,1,0:T(8,128)(2,1)} %copy-done.5), calls=%async_computation.1 | async-start | bytes 3932160 | tf_op jit(solution)/shard_map/all_to_all | solution.py:256
  49.8 3.8 %collective-permute-start = (bf16[1536,768]{1,0:T(8,128)(2,1)}, bf16[1536,768]{1,0:T(8,128)(2,1)S(1)}, u32[]{:S(2)}, u32[]{:S(2)}) collective-permute-start(bf16[1536,768]{1,0:T(8,128)(2,1)} %bitcast.26), channel_id=1, source_target_pairs={{0,1},{1,0},{2,3},{3,2},{4,5},{5,4},{6,7},{7,6},{8,9},{9,8},{10,11... | collective-permute-start | bytes 7077896 | tf_op jit(solution)/shard_map/ppermute | solution.py:262
  53.7 4.3 %collective-permute-done.w_ref = bf16[1536,768]{1,0:T(8,128)(2,1)S(1)} collective-permute-done((bf16[1536,768]{1,0:T(8,128)(2,1)}, bf16[1536,768]{1,0:T(8,128)(2,1)S(1)}, u32[]{:S(2)}, u32[]{:S(2)}) %collective-permute-start) | collective-permute-done | bytes 2359328 | tf_op jit(solution)/shard_map/ppermute | solution.py:262
  58.0 0.0 copy-start.2
  58.0 1.4 %copy-done.2 = bf16[1536,768]{1,0:T(8,128)(2,1)} copy-done((bf16[1536,768]{1,0:T(8,128)(2,1)}, bf16[1536,768]{1,0:T(8,128)(2,1)S(1)}, u32[]{:S(2)}) %copy-start.2) | copy-done | bytes 2359320
  59.5 4.7 %all-to-all-done.1.in_ref = bf16[4,640,384]{2,1,0:T(8,128)(2,1)S(1)} async-done(((bf16[4,640,384]{2,1,0:T(8,128)(2,1)}), bf16[4,640,384]{2,1,0:T(8,128)(2,1)S(1)}, u32[]{:S(2)}, u32[]{:S(2)}) %all-to-all-start.1) | async-done | bytes 1966112 | tf_op jit(solution)/shard_map/all_to_all | solution.py:256
  64.2 0.0 copy-start.3
  64.2 1.7 %copy-done.3 = bf16[1536,768]{1,0:T(8,128)(2,1)S(1)} copy-done((bf16[1536,768]{1,0:T(8,128)(2,1)S(1)}, bf16[1536,768]{1,0:T(8,128)(2,1)}, u32[]{:S(2)}) %copy-start.3) | copy-done | bytes 2359320
  65.9 0.0 copy-start.1
  65.9 0.9 shard_map.87
  66.8 3.8 %collective-permute-start.1 = (f32[320,768]{1,0:T(8,128)S(1)}, f32[320,768]{1,0:T(8,128)S(1)}, u32[]{:S(2)}, u32[]{:S(2)}) collective-permute-start(f32[320,768]{1,0:T(8,128)S(1)} %shard_map.87), channel_id=1, source_target_pairs={{0,1},{1,0},{2,3},{3,2},{4,5},{5,4},{6,7},{7,6},{8,9},{9,8},{10,11... | collective-permute-start | bytes 2949128 | tf_op jit(solution)/shard_map/ppermute | solution.py:262
  70.6 0.0 copy-done.1
  70.6 0.9 shard_map.86.a_ref
  71.5 1.2 %collective-permute-done.1.b_ref = f32[320,768]{1,0:T(8,128)S(1)} collective-permute-done((f32[320,768]{1,0:T(8,128)S(1)}, f32[320,768]{1,0:T(8,128)S(1)}, u32[]{:S(2)}, u32[]{:S(2)}) %collective-permute-start.1) | collective-permute-done | bytes 983072 | tf_op jit(solution)/shard_map/ppermute | solution.py:262
  72.8 0.2 shard_map.88.d_ref
  73.0 0.0 copy-start.4
  73.0 2.4 %collective-permute-start.2 = (bf16[320,512]{1,0:T(8,128)(2,1)S(1)}, bf16[320,512]{1,0:T(8,128)(2,1)S(1)}, u32[]{:S(2)}, u32[]{:S(2)}) collective-permute-start(bf16[320,512]{1,0:T(8,128)(2,1)S(1)} %shard_map.88.d_ref), channel_id=1, source_target_pairs={{0,1},{1,0},{2,3},{3,2},{4,5},{5,4},{6,7},{7,6},{8,9},{9,8},{10,11... | collective-permute-start | bytes 983048 | tf_op jit(solution)/shard_map/ppermute | solution.py:262
  75.4 0.7 shard_map.89.sum_ref
  76.1 0.5 collective-permute-done.2.d_ref
  76.6 0.0 copy-done.4
  76.6 0.8 shard_map.90
  77.5 0.0 copy-start.11
  77.5 0.0 copy-start.12
  77.5 0.0 copy-start.13
  77.5 13.6 %all_to_all.20.in_ref = bf16[4,320,384]{2,1,0:T(8,128)(2,1)S(1)} all-to-all(bf16[4,320,384]{2,1,0:T(8,128)(2,1)S(1)} %shard_map.90), channel_id=1, replica_groups={{0,2,8,10},{4,6,12,14},{16,18,24,26},{20,22,28,30},{32,34,40,42},{36,38..., dimensions={0} | all-to-all | bytes 1966080 | tf_op jit(solution)/shard_map/all_to_all | solution.py:256
  91.1 0.9 shard_map.91
  92.0 6.9 %all-to-all-start.3 = ((bf16[64,16,128]{2,1,0:T(8,128)(2,1)}), bf16[64,16,128]{2,1,0:T(8,128)(2,1)S(1)}, u32[]{:S(2)}, u32[]{:S(2)}) async-start(bf16[64,16,128]{2,1,0:T(8,128)(2,1)} %shard_map.91), calls=%async_computation.3 | async-start | bytes 524288 | tf_op jit(solution)/shard_map/all_to_all | solution.py:256
  98.9 0.0 copy-done.11
  98.9 0.0 copy-done.12
  98.9 0.0 copy-done.13
  98.9 0.2 shard_map.82.combine_ref
  99.1 16.0 %all-to-all-done.3.in_ref = bf16[64,16,128]{2,1,0:T(8,128)(2,1)S(1)} async-done(((bf16[64,16,128]{2,1,0:T(8,128)(2,1)}), bf16[64,16,128]{2,1,0:T(8,128)(2,1)S(1)}, u32[]{:S(2)}, u32[]{:S(2)}) %all-to-all-start.3) | async-done | bytes 262176 | tf_op jit(solution)/shard_map/all_to_all | solution.py:256
  115.1 1.0 shard_map.92
Async XLA Ops:
  0.0 0.7 copy-start.8
  0.7 0.7 copy-start.9
  1.4 0.7 copy-start.10
  3.5 41.0 %all-to-all-start = ((bf16[64,32,128]{2,1,0:T(8,128)(2,1)}), bf16[64,32,128]{2,1,0:T(8,128)(2,1)S(1)}, u32[]{:S(2)}, u32[]{:S(2)}) async-start(bf16[64,32,128]{2,1,0:T(8,128)(2,1)} %bitcast.5), calls=%async_computation | async-start | bytes 1048576 | tf_op jit(solution)/shard_map/all_to_all | solution.py:256
  24.9 1.4 %copy-start.6 = (bf16[1,3072,256]{2,1,0:T(8,128)(2,1)S(1)}, bf16[1,3072,256]{2,1,0:T(8,128)(2,1)}, u32[]{:S(2)}) copy-start(bf16[1,3072,256]{2,1,0:T(8,128)(2,1)} %param.13) | copy-start | bytes 4718596
  26.3 1.4 %copy-start.7 = (bf16[1,3072,256]{2,1,0:T(8,128)(2,1)S(1)}, bf16[1,3072,256]{2,1,0:T(8,128)(2,1)}, u32[]{:S(2)}) copy-start(bf16[1,3072,256]{2,1,0:T(8,128)(2,1)} %param.14) | copy-start | bytes 4718596
  28.9 1.4 %copy-start = (bf16[4,3,4,2,16,768]{5,4,3,2,1,0:T(8,128)(2,1)}, bf16[4,3,4,2,16,768]{5,4,3,2,1,0:T(8,128)(2,1)S(1)}, u32[]{:S(2)}) copy-start(bf16[4,3,4,2,16,768]{5,4,3,2,1,0:T(8,128)(2,1)S(1)} %get-tuple-element.9) | copy-start | bytes 7077892
  30.3 1.4 %copy-start.14 = (bf16[4,3,4,2,16,768]{5,4,3,2,1,0:T(8,128)(2,1)}, bf16[4,3,4,2,16,768]{5,4,3,2,1,0:T(8,128)(2,1)S(1)}, u32[]{:S(2)}) copy-start(bf16[4,3,4,2,16,768]{5,4,3,2,1,0:T(8,128)(2,1)S(1)} %get-tuple-element.12) | copy-start | bytes 7077892
  44.9 1.3 %copy-start.5 = (bf16[4,640,384]{2,1,0:T(8,128)(2,1)}, bf16[4,640,384]{2,1,0:T(8,128)(2,1)S(1)}, u32[]{:S(2)}) copy-start(bf16[4,640,384]{2,1,0:T(8,128)(2,1)S(1)} %shard_map.85) | copy-start | bytes 5898244
  46.2 18.0 %all-to-all-start.1 = ((bf16[4,640,384]{2,1,0:T(8,128)(2,1)}), bf16[4,640,384]{2,1,0:T(8,128)(2,1)S(1)}, u32[]{:S(2)}, u32[]{:S(2)}) async-start(bf16[4,640,384]{2,1,0:T(8,128)(2,1)} %copy-done.5), calls=%async_computation.1 | async-start | bytes 3932160 | tf_op jit(solution)/shard_map/all_to_all | solution.py:256
  49.8 8.2 %collective-permute-start = (bf16[1536,768]{1,0:T(8,128)(2,1)}, bf16[1536,768]{1,0:T(8,128)(2,1)S(1)}, u32[]{:S(2)}, u32[]{:S(2)}) collective-permute-start(bf16[1536,768]{1,0:T(8,128)(2,1)} %bitcast.26), channel_id=1, source_target_pairs={{0,1},{1,0},{2,3},{3,2},{4,5},{5,4},{6,7},{7,6},{8,9},{9,8},{10,11... | collective-permute-start | bytes 7077896 | tf_op jit(solution)/shard_map/ppermute | solution.py:262
  58.0 1.4 %copy-start.2 = (bf16[1536,768]{1,0:T(8,128)(2,1)}, bf16[1536,768]{1,0:T(8,128)(2,1)S(1)}, u32[]{:S(2)}) copy-start(bf16[1536,768]{1,0:T(8,128)(2,1)S(1)} %collective-permute-done.w_ref) | copy-start | bytes 7077892
  64.2 1.7 %copy-start.3 = (bf16[1536,768]{1,0:T(8,128)(2,1)S(1)}, bf16[1536,768]{1,0:T(8,128)(2,1)}, u32[]{:S(2)}) copy-start(bf16[1536,768]{1,0:T(8,128)(2,1)} %copy-done.2) | copy-start | bytes 7077892
  65.9 4.7 %copy-start.1 = (bf16[4,3,4,2,16,768]{5,4,3,2,1,0:T(8,128)(2,1)S(1)}, bf16[4,3,4,2,16,768]{5,4,3,2,1,0:T(8,128)(2,1)}, u32[]{:S(2)}) copy-start(bf16[4,3,4,2,16,768]{5,4,3,2,1,0:T(8,128)(2,1)} %copy-done) | copy-start | bytes 7077892
  66.8 6.0 %collective-permute-start.1 = (f32[320,768]{1,0:T(8,128)S(1)}, f32[320,768]{1,0:T(8,128)S(1)}, u32[]{:S(2)}, u32[]{:S(2)}) collective-permute-start(f32[320,768]{1,0:T(8,128)S(1)} %shard_map.87), channel_id=1, source_target_pairs={{0,1},{1,0},{2,3},{3,2},{4,5},{5,4},{6,7},{7,6},{8,9},{9,8},{10,11... | collective-permute-start | bytes 2949128 | tf_op jit(solution)/shard_map/ppermute | solution.py:262
  73.0 3.7 %copy-start.4 = (bf16[1536,768]{1,0:T(8,128)(2,1)S(1)}, bf16[1536,768]{1,0:T(8,128)(2,1)}, u32[]{:S(2)}) copy-start(bf16[1536,768]{1,0:T(8,128)(2,1)} %copy-done.2) | copy-start | bytes 7077892
  73.0 3.7 %collective-permute-start.2 = (bf16[320,512]{1,0:T(8,128)(2,1)S(1)}, bf16[320,512]{1,0:T(8,128)(2,1)S(1)}, u32[]{:S(2)}, u32[]{:S(2)}) collective-permute-start(bf16[320,512]{1,0:T(8,128)(2,1)S(1)} %shard_map.88.d_ref), channel_id=1, source_target_pairs={{0,1},{1,0},{2,3},{3,2},{4,5},{5,4},{6,7},{7,6},{8,9},{9,8},{10,11... | collective-permute-start | bytes 983048 | tf_op jit(solution)/shard_map/ppermute | solution.py:262
  77.5 21.4 %copy-start.11 = (s32[128,2]{0,1:T(2,128)S(1)}, s32[128,2]{0,1:T(2,128)}, u32[]{:S(2)}) copy-start(s32[128,2]{0,1:T(2,128)} %param.12) | copy-start | bytes 3076
  77.5 21.4 %copy-start.12 = (f32[128,2]{0,1:T(2,128)S(1)}, f32[128,2]{0,1:T(2,128)}, u32[]{:S(2)}) copy-start(f32[128,2]{0,1:T(2,128)} %param.11) | copy-start | bytes 3076
  77.5 21.4 %copy-start.13 = (f32[128]{0:T(128)S(1)}, f32[128]{0:T(128)}, u32[]{:S(2)}) copy-start(f32[128]{0:T(128)} %param.10) | copy-start | bytes 1540
  92.0 23.2 %all-to-all-start.3 = ((bf16[64,16,128]{2,1,0:T(8,128)(2,1)}), bf16[64,16,128]{2,1,0:T(8,128)(2,1)S(1)}, u32[]{:S(2)}, u32[]{:S(2)}) async-start(bf16[64,16,128]{2,1,0:T(8,128)(2,1)} %shard_map.91), calls=%async_computation.3 | async-start | bytes 524288 | tf_op jit(solution)/shard_map/all_to_all | solution.py:256

commit v5 on v4

--- a/solution.py
+++ b/solution.py
@@ -36,7 +36,7 @@
 
 def token_slots(ids, experts):
     tokens = ids.shape[1]
-    expert = lax.broadcasted_iota(jnp.int32, (experts, tokens), 0)
+    expert = lax.broadcasted_iota(jnp.int32, (experts, tokens), 0).astype(F32)
     first = ids[0:1, :] == expert
     hit = first | (ids[1:2, :] == expert)
     row = lax.broadcasted_iota(jnp.int32, (tokens, tokens), 0)
@@ -47,29 +47,24 @@
     return jnp.where(hit, before, -2.0), first
 
 
-def pack_kernel(capacity, ids_hbm, x_hbm, g_hbm, out_ref, ids_ref, x_ref, g_ref, sems):
-    copies = [
-        pltpu.make_async_copy(src, dst, sems.at[i])
-        for i, (src, dst) in enumerate(((ids_hbm, ids_ref), (x_hbm, x_ref), (g_hbm, g_ref)))
-    ]
-    for copy in copies:
-        copy.start()
+def pack_kernel(capacity, feats, head_ref, out_ref):
     nz, members = out_ref.shape[:2]
-    feats, tokens = x_ref.shape
+    tokens = head_ref.shape[1]
     parts = feats // FINE
     lanes = nz * LANES
     part = lane_parts((FINE, lanes), 1, capacity)
     slot_of_lane = lane_slots(tokens, capacity, parts)
-    copies[0].wait()
-    slots, _ = token_slots(ids_ref[...], nz)
+    slots, _ = token_slots(head_ref[2 * feats :, :].astype(F32), nz)
     place = jnp.concatenate(
         [jnp.where(slots[z : z + 1] == slot_of_lane, 1.0, 0.0).astype(BF16) for z in range(nz)],
         axis=0,
     )
-    for kind, ref in enumerate((x_ref, g_ref)):
-        copies[1 + kind].wait()
+    for kind in range(2):
         spread = lax.dot_general(
-            ref[...], place, (((1,), (1,)), ((), ())), preferred_element_type=F32
+            head_ref[kind * feats : (kind + 1) * feats, :],
+            place,
+            (((1,), (1,)), ((), ())),
+            preferred_element_type=F32,
         )
         block = jnp.zeros((FINE, lanes), F32)
         for p in range(parts):
@@ -119,20 +114,19 @@
             out_ref[z * ny : (z + 1) * ny] = turned.reshape(ny, FINE, LANES)
 
 
-def order_kernel(gate_hbm, up_hbm, down_hbm, own_ref, sent_ref, sems):
+def order_kernel(*refs):
     core = lax.axis_index("c")
-    hidden = gate_hbm.shape[-1]
+    srcs, own, sent, sems = refs[:3], refs[3:6], refs[6:9], refs[9]
     copies = []
-    for out_ref, c in ((own_ref, core), (sent_ref, 1 - core)):
-        for k, src in enumerate((gate_hbm, up_hbm, down_hbm)):
-            lanes = pl.ds(k * hidden, hidden)
+    for outs, c in ((own, core), (sent, 1 - core)):
+        for src, out_ref in zip(srcs, outs):
             for yb in range(2):
                 for xb in range(2):
                     for p in range(src.shape[5]):
                         copies.append(
                             pltpu.make_async_copy(
                                 src.at[:, yb, :, xb, c, p],
-                                out_ref.at[2 * yb + xb, p, :, :, :, lanes],
+                                out_ref.at[2 * yb + xb, p],
                                 sems.at[len(copies)],
                             )
                         )
@@ -142,14 +136,15 @@
         copy.wait()
 
 
-def project_kernel(in_ref, w_ref, out_ref):
+def project_kernel(in_ref, gate_ref, up_ref, down_ref, out_ref):
     members = in_ref.shape[0]
-    rows, wide = out_ref.shape
-    split = wide // 3 * 2
+    rows = out_ref.shape[0]
+    hidden = gate_ref.shape[1]
     x = jnp.concatenate([in_ref[i, :rows, :] for i in range(members)], axis=1)
-    out_ref[:, :split] = jnp.dot(x, w_ref[:, :split], preferred_element_type=F32)
+    out_ref[:, :hidden] = jnp.dot(x, gate_ref[...], preferred_element_type=F32)
+    out_ref[:, hidden : 2 * hidden] = jnp.dot(x, up_ref[...], preferred_element_type=F32)
     g = jnp.concatenate([in_ref[i, rows:, :] for i in range(members)], axis=1)
-    out_ref[:, split:] = jnp.dot(g, w_ref[:, split:], preferred_element_type=F32)
+    out_ref[:, 2 * hidden :] = jnp.dot(g, down_ref[...], preferred_element_type=F32)
 
 
 def tail_kernel(a_ref, b_ref, out_ref):
@@ -163,32 +158,33 @@
     out_ref[:, hidden:] = d_upper
 
 
-def return_kernel(d_ref, w_ref, out_ref):
-    out_ref[...] = lax.dot_general(
-        d_ref[...],
-        w_ref[:, : d_ref.shape[1]],
-        (((1,), (1,)), ((), ())),
-        preferred_element_type=F32,
-    )
-
-
-def return_add_kernel(d_ref, w_ref, sum_ref, out_ref):
+def return_part(d_ref, gate_ref, up_ref, here):
+    hidden = gate_ref.shape[1]
+    across = (((1,), (1,)), ((), ()))
+    part = lax.dot_general(
+        d_ref[:, :hidden], gate_ref[here, :], across, preferred_element_type=F32
+    )
+    return part + lax.dot_general(
+        d_ref[:, hidden:], up_ref[here, :], across, preferred_element_type=F32
+    )
+
+
+def return_kernel(d_ref, gate_ref, up_ref, out_ref):
+    out_ref[...] = return_part(d_ref, gate_ref, up_ref, slice(None))
+
+
+def return_add_kernel(d_ref, gate_ref, up_ref, sum_ref, out_ref):
     members, _, wide = out_ref.shape
     for i in range(members):
         here = slice(i * wide, (i + 1) * wide)
-        total = lax.dot_general(
-            d_ref[...],
-            w_ref[here, : d_ref.shape[1]],
-            (((1,), (1,)), ((), ())),
-            preferred_element_type=F32,
-        )
-        out_ref[i] = (total + sum_ref[:, here]).astype(out_ref.dtype)
+        part = return_part(d_ref, gate_ref, up_ref, here)
+        out_ref[i] = (part + sum_ref[:, here]).astype(out_ref.dtype)
 
 
 def combine_kernel(capacity, parts, ids_ref, prob_ref, scale_ref, out_ref):
     lanes, tokens = out_ref.shape
     experts = lanes // LANES
-    slots, first = token_slots(ids_ref[...], experts)
+    slots, first = token_slots(ids_ref[...].astype(F32), experts)
     weights = jnp.where(first, prob_ref[0:1, :], prob_ref[1:2, :]) * scale_ref[...]
     slot_of_lane = lane_slots(tokens, capacity, parts)
     for z in range(experts):
@@ -218,15 +214,14 @@
     ).astype(out_ref.dtype)
 
 
-def call(kernel, shape, dtype, *operands, flops=0, spaces=pltpu.VMEM, scratch=()):
+def call(kernel, shape, dtype, *operands, flops=0):
     moved = sum(o.size * o.dtype.itemsize for o in operands)
     moved += math.prod(shape) * jnp.dtype(dtype).itemsize
     return pl.pallas_call(
         kernel,
         out_shape=jax.ShapeDtypeStruct(shape, dtype),
-        in_specs=[pl.BlockSpec(memory_space=spaces)] * len(operands),
+        in_specs=[pl.BlockSpec(memory_space=pltpu.VMEM)] * len(operands),
         out_specs=pl.BlockSpec(memory_space=pltpu.VMEM),
-        scratch_shapes=scratch,
         compiler_params=pltpu.CompilerParams(vmem_limit_bytes=32 * 1024 * 1024),
         cost_estimate=pl.CostEstimate(flops=flops, bytes_accessed=moved, transcendentals=0),
     )(*operands)
@@ -275,36 +270,30 @@
     rows = nz * capacity
     wide = feats * spread
 
+    ids = jnp.pad(route_ids.T.astype(BF16), ((0, FINE - route_ids.shape[1]), (0, 0)))
+    head = jnp.concatenate([activations.T, out_grad.T, ids], axis=0)
     send = call(
-        functools.partial(pack_kernel, capacity),
+        functools.partial(pack_kernel, capacity, feats),
         (nz, spread, 2 * FINE, LANES),
         BF16,
-        route_ids.T,
-        activations.T,
-        out_grad.T,
-        spaces=pl.ANY,
-        scratch=(
-            pltpu.VMEM(route_ids.T.shape, route_ids.dtype),
-            pltpu.VMEM((feats, tokens), BF16),
-            pltpu.VMEM((feats, tokens), BF16),
-            pltpu.SemaphoreType.DMA((3,)),
-        ),
+        head,
     )
     got = swap(send.reshape(nz * spread, 2 * FINE, LANES), far)
 
     views = (ny // 2, 2, nx // 2, 2, nc, parts, FINE, hidden)
-    ordered = (members, parts, ny // 2, nx // 2, FINE, 3 * hidden)
-    own, sent = pl.pallas_call(
+    ordered = (members, parts, ny // 2, nx // 2, FINE, hidden)
+    weights = pl.pallas_call(
         order_kernel,
-        out_shape=[jax.ShapeDtypeStruct(ordered, BF16)] * 2,
-        in_specs=[pl.BlockSpec(memory_space=pl.ANY)] * 3,
-        out_specs=[pl.BlockSpec(memory_space=pltpu.VMEM)] * 2,
+        out_shape=[jax.ShapeDtypeStruct(ordered, BF16)] * 6,
+        in_specs=[pl.BlockSpec(memory_space=pltpu.HBM)] * 3,
+        out_specs=[pl.BlockSpec(memory_space=pltpu.VMEM)] * 6,
         scratch_shapes=[pltpu.SemaphoreType.DMA((2 * 3 * members * parts,))],
         compiler_params=pltpu.CompilerParams(vmem_limit_bytes=32 * 1024 * 1024),
         cost_estimate=pl.CostEstimate(flops=0, bytes_accessed=12 * 1024 * 1024, transcendentals=0),
     )(w_gate.reshape(views), w_up.reshape(views), w_down[0].T.reshape(views))
-    own, sent = (w.reshape(members * wide, 3 * hidden) for w in (own, sent))
-    got, own = lax.optimization_barrier((got, own))
+    weights = [w.reshape(members * wide, hidden) for w in weights]
+    own, other = weights[:3], [other_core(w) for w in weights[3:]]
+    got, own, other = lax.optimization_barrier((got, own, other))
 
     copies = call(
         functools.partial(unpack_kernel, capacity, parts, spread),
@@ -314,18 +303,25 @@
     )
     block = swap(copies, near)
 
-    other = other_core(sent)
     flops = 2 * rows * members * wide * 3 * hidden
 
     def project(w):
-        return call(project_kernel, (rows, 3 * hidden), F32, block, w, flops=flops)
-
-    theirs = other_core(project(other))
-    d_own = call(tail_kernel, (rows, 2 * hidden), BF16, project(own), theirs)
-    d_other = other_core(d_own)
+        return call(project_kernel, (rows, 3 * hidden), F32, block, *w, flops=flops)
+
+    def tail(a, b):
+        return call(tail_kernel, (rows, 2 * hidden), BF16, a, b)
+
+    part_other = project(other)
+    rest_own = other_core(part_other)
+    part_own = project(own)
+    rest_other = other_core(part_own)
+    d_own = tail(part_own, rest_own)
     flops = flops // 3 * 2
-    part = call(return_kernel, (rows, members * wide), F32, d_own, own, flops=flops)
-    part = call(return_add_kernel, (members, rows, wide), BF16, d_other, other, part, flops=flops)
+    part = call(return_kernel, (rows, members * wide), F32, d_own, *own[:2], flops=flops)
+    d_other = tail(part_other, rest_other)
+    part = call(
+        return_add_kernel, (members, rows, wide), BF16, d_other, *other[:2], part, flops=flops
+    )
     part = swap(part, near)
     part = call(
         functools.partial(repack_kernel, capacity, parts, spread),

time: 117 us -> 114 us (0.974)
  blocking collectives: 13.6 us -> 32.3 us
  waiting for transfers between devices: 39.7 us -> 25.1 us
  local copies, waits for them, and re-layouts: 13.9 us -> 5.32 us
  other arithmetic: 0 us -> 1.53 us
  Pallas kernels: 8.63 us -> 10 us
    all_to_all x1 -> x2, blocking collectives: 13.6 us -> 32.3 us  [swap(): lax.all_to_all(blocks, AXES, split_axis=0, concat_axis=0, axis_index_grou...]
    all_to_all x3 -> x2, waiting for transfers between devices: 33.6 us -> 21.6 us  [swap(): lax.all_to_all(blocks, AXES, split_axis=0, concat_axis=0, axis_index_grou...]
    unnamed x30 -> x20, local copies, waits for them, and re-layouts: 12.2 us -> 4.63 us
    all_to_all x3 -> x2, starting transfers between devices: 30.1 us -> 27.5 us  [swap(): lax.all_to_all(blocks, AXES, split_axis=0, concat_axis=0, axis_index_grou...]
    ppermute x3 -> x5, waiting for transfers between devices: 6.11 us -> 3.5 us  [other_core(): return lax.ppermute(values, 'c', [(0, 1), (1, 0)])]
    ppermute x3 -> x5, starting transfers between devices: 10 us -> 11.6 us  [other_core(): return lax.ppermute(values, 'c', [(0, 1), (1, 0)])]
    pallas_call x10 -> x11, Pallas kernels: 7.42 us -> 8.41 us  [call(): pl.pallas_call(kernel, out_shape=jax.ShapeDtypeStruct(shape, dtype), in_s...]
  transfers between devices with their start and end apart: 6 -> 7, of which waited for: 6 -> 4; matrix products, arithmetic and copies ran while one was open for 1% -> 1% of each run, Pallas kernels for 3% -> 3%
where the time goes in v5:
time: 114 us
  starting transfers between devices  39.1 us (34%)
  blocking collectives  32.3 us (28%)
  waiting for transfers between devices  25.1 us (22%)
  Pallas kernels  10 us (9%)
  local copies, waits for them, and re-layouts  5.32 us (5%)
  other arithmetic  1.53 us (1%)
    all_to_all x2, blocking collectives, swap(): lax.all_to_all(blocks, AXES, split_axis=0, concat_axis=0, axis_index_grou...  32.3 us
    all_to_all x2, starting transfers between devices, swap(): lax.all_to_all(blocks, AXES, split_axis=0, concat_axis=0, axis_index_grou...  27.5 us
    all_to_all x2, waiting for transfers between devices, swap(): lax.all_to_all(blocks, AXES, split_axis=0, concat_axis=0, axis_index_grou...  21.6 us
    ppermute x5, starting transfers between devices, other_core(): return lax.ppermute(values, 'c', [(0, 1), (1, 0)])  11.6 us
    pallas_call x11, Pallas kernels, call(): pl.pallas_call(kernel, out_shape=jax.ShapeDtypeStruct(shape, dtype), in_s...  8.41 us
    unnamed x20, local copies, waits for them, and re-layouts  4.63 us
    ppermute x5, waiting for transfers between devices, other_core(): return lax.ppermute(values, 'c', [(0, 1), (1, 0)])  3.5 us
  transfers between devices with their start and end apart: 7, of which 4 were waited for; matrix products, arithmetic and copies ran while one was open for 1% of the time, Pallas kernels for 3%

profile of v5, /device:TPU:1, one launch (start us, length us, event | category | flops | bytes accessed | tf_op | source)
XLA Modules:
  0.0 113.6 jit_solution(3335687425765214102)
XLA Ops:
  0.0 0.0 copy-start.9
  0.0 0.8 bitcast_convert_fusion
  0.8 0.7 fusion.1.head_ref
  1.5 1.2 %shard_map.83 = bf16[8,8,32,128]{3,2,1,0:T(8,128)(2,1)} custom-call(bf16[112,128]{1,0:T(8,128)(2,1)S(1)} %fusion.1.head_ref), custom_call_target="tpu_custom_call" | custom-call | bytes 552960 | tf_op jit(solution)/shard_map/pallas_call | solution.py:220
  2.8 19.9 %all-to-all-start = ((bf16[64,32,128]{2,1,0:T(8,128)(2,1)}), bf16[64,32,128]{2,1,0:T(8,128)(2,1)}, u32[]{:S(2)}, u32[]{:S(2)}) async-start(bf16[64,32,128]{2,1,0:T(8,128)(2,1)} %bitcast.5), calls=%async_computation | async-start | bytes 1048576 | tf_op jit(solution)/shard_map/all_to_all | solution.py:251
  22.6 0.0 copy-done.9
  22.6 0.7 copy.9
  23.3 0.0 copy-start
  23.4 1.4 %copy-done = bf16[1,3072,256]{2,1,0:T(8,128)(2,1)S(1)} copy-done((bf16[1,3072,256]{2,1,0:T(8,128)(2,1)S(1)}, bf16[1,3072,256]{2,1,0:T(8,128)(2,1)}, u32[]{:S(2)}) %copy-start) | copy-done | bytes 1572888
  24.8 0.0 copy-start.1
  24.8 1.4 %copy-done.1 = bf16[1,3072,256]{2,1,0:T(8,128)(2,1)S(1)} copy-done((bf16[1,3072,256]{2,1,0:T(8,128)(2,1)S(1)}, bf16[1,3072,256]{2,1,0:T(8,128)(2,1)}, u32[]{:S(2)}) %copy-start.1) | copy-done | bytes 1572888
  26.2 1.6 %shard_map.84 = (bf16[4,3,4,2,16,256]{5,4,3,2,1,0:T(8,128)(2,1)S(1)}, bf16[4,3,4,2,16,256]{5,4,3,2,1,0:T(8,128)(2,1)S(1)}, bf16[4,3,4,2,16,256]{5,4,3,2,1,0:T(8,...) custom-call(bf16[4,2,2,2,2,3,16,256]{7,6,5,4,3,2,1,0:T(8,128)(2,1)S(, ...), custom_call_target="tpu_custom_call" | custom-call | bytes 12582912 | tf_op jit(solution)/shard_map/pallas_call | solution.py:285
  27.8 0.0 copy-start.2
  27.8 0.9 copy-done.2
  28.7 2.9 %collective-permute-start = (bf16[1536,256]{1,0:T(8,128)(2,1)S(1)}, bf16[1536,256]{1,0:T(8,128)(2,1)S(1)}, u32[]{:S(2)}, u32[]{:S(2)}) collective-permute-start(bf16[1536,256]{1,0:T(8,128)(2,1)S(1)} %bitcast.33), channel_id=1, source_target_pairs={{0,1},{1,0},{2,3},{3,2},{4,5},{5,4},{6,7},{7,6},{8,9},{9,8},{10,11... | collective-permute-start | bytes 2359304 | tf_op jit(solution)/shard_map/ppermute | solution.py:257
  31.5 1.9 %collective-permute-start.1 = (bf16[1536,256]{1,0:T(8,128)(2,1)S(1)}, bf16[1536,256]{1,0:T(8,128)(2,1)S(1)}, u32[]{:S(2)}, u32[]{:S(2)}) collective-permute-start(bf16[1536,256]{1,0:T(8,128)(2,1)S(1)} %bitcast.32), channel_id=1, source_target_pairs={{0,1},{1,0},{2,3},{3,2},{4,5},{5,4},{6,7},{7,6},{8,9},{9,8},{10,11... | collective-permute-start | bytes 2359304 | tf_op jit(solution)/shard_map/ppermute | solution.py:257
  33.4 2.4 %collective-permute-start.2 = (bf16[1536,256]{1,0:T(8,128)(2,1)S(1)}, bf16[1536,256]{1,0:T(8,128)(2,1)S(1)}, u32[]{:S(2)}, u32[]{:S(2)}) collective-permute-start(bf16[1536,256]{1,0:T(8,128)(2,1)S(1)} %bitcast.31), channel_id=1, source_target_pairs={{0,1},{1,0},{2,3},{3,2},{4,5},{5,4},{6,7},{7,6},{8,9},{9,8},{10,11... | collective-permute-start | bytes 2359304 | tf_op jit(solution)/shard_map/ppermute | solution.py:257
  35.9 0.0 collective-permute-done.gate_ref
  35.9 0.0 collective-permute-done.1.up_ref
  35.9 1.9 %collective-permute-done.2.down_ref = bf16[1536,256]{1,0:T(8,128)(2,1)S(1)} collective-permute-done((bf16[1536,256]{1,0:T(8,128)(2,1)S(1)}, bf16[1536,256]{1,0:T(8,128)(2,1)S(1)}, u32[]{:S(2)}, u32[]{:S(2)}) %collective-permute-start.2) | collective-permute-done | bytes 786464 | tf_op jit(solution)/shard_map/ppermute | solution.py:257
  37.7 0.0 copy-start.4
  37.8 0.9 copy-done.4
  38.7 5.3 %all-to-all-done.in_ref = bf16[64,32,128]{2,1,0:T(8,128)(2,1)} async-done(((bf16[64,32,128]{2,1,0:T(8,128)(2,1)}), bf16[64,32,128]{2,1,0:T(8,128)(2,1)}, u32[]{:S(2)}, u32[]{:S(2)}) %all-to-all-start) | async-done | bytes 524320 | tf_op jit(solution)/shard_map/all_to_all | solution.py:251
  43.9 1.4 %shard_map.85 = bf16[4,640,384]{2,1,0:T(8,128)(2,1)S(1)} custom-call(bf16[64,32,128]{2,1,0:T(8,128)(2,1)} %all-to-all-done.in_ref), custom_call_target="tpu_custom_call" | custom-call | bytes 2490368 | tf_op jit(solution)/shard_map/pallas_call | solution.py:220
  45.3 0.0 copy-start.5
  45.3 18.7 %all_to_all.20.in_ref = bf16[4,640,384]{2,1,0:T(8,128)(2,1)S(1)} all-to-all(bf16[4,640,384]{2,1,0:T(8,128)(2,1)S(1)} %shard_map.85), channel_id=1, replica_groups={{0,2,8,10},{4,6,12,14},{16,18,24,26},{20,22,28,30},{32,34,40,42},{36,38..., dimensions={0} | all-to-all | bytes 3932160 | tf_op jit(solution)/shard_map/all_to_all | solution.py:251
  64.0 0.0 copy-done.5
  64.0 0.0 copy-start.3
  64.0 0.9 shard_map.86.a_ref
  64.9 2.5 %collective-permute-start.4 = (f32[320,768]{1,0:T(8,128)S(1)}, f32[320,768]{1,0:T(8,128)S(1)}, u32[]{:S(2)}, u32[]{:S(2)}) collective-permute-start(f32[320,768]{1,0:T(8,128)S(1)} %shard_map.86.a_ref), channel_id=1, source_target_pairs={{0,1},{1,0},{2,3},{3,2},{4,5},{5,4},{6,7},{7,6},{8,9},{9,8},{10,11... | collective-permute-start | bytes 2949128 | tf_op jit(solution)/shard_map/ppermute | solution.py:257
  67.5 0.0 copy-done.3
  67.5 0.9 shard_map.87.a_ref
  68.4 1.9 %collective-permute-start.3 = (f32[320,768]{1,0:T(8,128)S(1)}, f32[320,768]{1,0:T(8,128)S(1)}, u32[]{:S(2)}, u32[]{:S(2)}) collective-permute-start(f32[320,768]{1,0:T(8,128)S(1)} %shard_map.87.a_ref), channel_id=1, source_target_pairs={{0,1},{1,0},{2,3},{3,2},{4,5},{5,4},{6,7},{7,6},{8,9},{9,8},{10,11... | collective-permute-start | bytes 2949128 | tf_op jit(solution)/shard_map/ppermute | solution.py:257
  70.4 0.0 collective-permute-done.4.b_ref
  70.4 0.2 shard_map.89.d_ref
  70.6 0.7 shard_map.90.sum_ref
  71.3 1.6 %collective-permute-done.3.b_ref = f32[320,768]{1,0:T(8,128)S(1)} collective-permute-done((f32[320,768]{1,0:T(8,128)S(1)}, f32[320,768]{1,0:T(8,128)S(1)}, u32[]{:S(2)}, u32[]{:S(2)}) %collective-permute-start.3) | collective-permute-done | bytes 983072 | tf_op jit(solution)/shard_map/ppermute | solution.py:257
  72.9 0.2 shard_map.88.d_ref
  73.1 0.9 shard_map.91
  73.9 0.0 copy-start.6
  74.0 0.0 copy-start.7
  74.0 0.0 copy-start.8
  74.0 13.6 %all_to_all.21.in_ref = bf16[4,320,384]{2,1,0:T(8,128)(2,1)S(1)} all-to-all(bf16[4,320,384]{2,1,0:T(8,128)(2,1)S(1)} %shard_map.91), channel_id=1, replica_groups={{0,2,8,10},{4,6,12,14},{16,18,24,26},{20,22,28,30},{32,34,40,42},{36,38..., dimensions={0} | all-to-all | bytes 1966080 | tf_op jit(solution)/shard_map/all_to_all | solution.py:251
  87.5 0.9 shard_map.92
  88.4 7.6 %all-to-all-start.3 = ((bf16[64,16,128]{2,1,0:T(8,128)(2,1)}), bf16[64,16,128]{2,1,0:T(8,128)(2,1)S(1)}, u32[]{:S(2)}, u32[]{:S(2)}) async-start(bf16[64,16,128]{2,1,0:T(8,128)(2,1)} %shard_map.92), calls=%async_computation.3 | async-start | bytes 524288 | tf_op jit(solution)/shard_map/all_to_all | solution.py:251
  96.1 0.0 copy-done.6
  96.1 0.0 copy-done.7
  96.1 0.0 copy-done.8
  96.1 0.2 shard_map.82.combine_ref
  96.3 16.3 %all-to-all-done.3.in_ref = bf16[64,16,128]{2,1,0:T(8,128)(2,1)S(1)} async-done(((bf16[64,16,128]{2,1,0:T(8,128)(2,1)}), bf16[64,16,128]{2,1,0:T(8,128)(2,1)S(1)}, u32[]{:S(2)}, u32[]{:S(2)}) %all-to-all-start.3) | async-done | bytes 262176 | tf_op jit(solution)/shard_map/all_to_all | solution.py:251
  112.6 1.0 shard_map.93
Async XLA Ops:
  0.0 22.6 %copy-start.9 = (bf16[1,256,3072]{2,1,0:T(8,128)(2,1)S(1)}, bf16[1,256,3072]{2,1,0:T(8,128)(2,1)}, u32[]{:S(2)}) copy-start(bf16[1,256,3072]{2,1,0:T(8,128)(2,1)} %param.15) | copy-start | bytes 4718596
  2.8 41.1 %all-to-all-start = ((bf16[64,32,128]{2,1,0:T(8,128)(2,1)}), bf16[64,32,128]{2,1,0:T(8,128)(2,1)}, u32[]{:S(2)}, u32[]{:S(2)}) async-start(bf16[64,32,128]{2,1,0:T(8,128)(2,1)} %bitcast.5), calls=%async_computation | async-start | bytes 1048576 | tf_op jit(solution)/shard_map/all_to_all | solution.py:251
  23.3 1.4 %copy-start = (bf16[1,3072,256]{2,1,0:T(8,128)(2,1)S(1)}, bf16[1,3072,256]{2,1,0:T(8,128)(2,1)}, u32[]{:S(2)}) copy-start(bf16[1,3072,256]{2,1,0:T(8,128)(2,1)} %param.13) | copy-start | bytes 4718596
  24.8 1.4 %copy-start.1 = (bf16[1,3072,256]{2,1,0:T(8,128)(2,1)S(1)}, bf16[1,3072,256]{2,1,0:T(8,128)(2,1)}, u32[]{:S(2)}) copy-start(bf16[1,3072,256]{2,1,0:T(8,128)(2,1)} %param.14) | copy-start | bytes 4718596
  27.8 0.9 copy-start.2
  28.7 7.2 %collective-permute-start = (bf16[1536,256]{1,0:T(8,128)(2,1)S(1)}, bf16[1536,256]{1,0:T(8,128)(2,1)S(1)}, u32[]{:S(2)}, u32[]{:S(2)}) collective-permute-start(bf16[1536,256]{1,0:T(8,128)(2,1)S(1)} %bitcast.33), channel_id=1, source_target_pairs={{0,1},{1,0},{2,3},{3,2},{4,5},{5,4},{6,7},{7,6},{8,9},{9,8},{10,11... | collective-permute-start | bytes 2359304 | tf_op jit(solution)/shard_map/ppermute | solution.py:257
  31.5 4.4 %collective-permute-start.1 = (bf16[1536,256]{1,0:T(8,128)(2,1)S(1)}, bf16[1536,256]{1,0:T(8,128)(2,1)S(1)}, u32[]{:S(2)}, u32[]{:S(2)}) collective-permute-start(bf16[1536,256]{1,0:T(8,128)(2,1)S(1)} %bitcast.32), channel_id=1, source_target_pairs={{0,1},{1,0},{2,3},{3,2},{4,5},{5,4},{6,7},{7,6},{8,9},{9,8},{10,11... | collective-permute-start | bytes 2359304 | tf_op jit(solution)/shard_map/ppermute | solution.py:257
  33.4 4.3 %collective-permute-start.2 = (bf16[1536,256]{1,0:T(8,128)(2,1)S(1)}, bf16[1536,256]{1,0:T(8,128)(2,1)S(1)}, u32[]{:S(2)}, u32[]{:S(2)}) collective-permute-start(bf16[1536,256]{1,0:T(8,128)(2,1)S(1)} %bitcast.31), channel_id=1, source_target_pairs={{0,1},{1,0},{2,3},{3,2},{4,5},{5,4},{6,7},{7,6},{8,9},{9,8},{10,11... | collective-permute-start | bytes 2359304 | tf_op jit(solution)/shard_map/ppermute | solution.py:257
  37.7 0.9 copy-start.4
  45.3 18.7 %copy-start.5 = (bf16[1536,256]{1,0:T(8,128)(2,1)S(1)}, bf16[1536,256]{1,0:T(8,128)(2,1)}, u32[]{:S(2)}) copy-start(bf16[1536,256]{1,0:T(8,128)(2,1)} %copy-done.4) | copy-start | bytes 2359300
  64.0 3.5 %copy-start.3 = (bf16[4,3,4,2,16,256]{5,4,3,2,1,0:T(8,128)(2,1)S(1)}, bf16[4,3,4,2,16,256]{5,4,3,2,1,0:T(8,128)(2,1)}, u32[]{:S(2)}) copy-start(bf16[4,3,4,2,16,256]{5,4,3,2,1,0:T(8,128)(2,1)} %copy-done.2) | copy-start | bytes 2359300
  64.9 5.4 %collective-permute-start.4 = (f32[320,768]{1,0:T(8,128)S(1)}, f32[320,768]{1,0:T(8,128)S(1)}, u32[]{:S(2)}, u32[]{:S(2)}) collective-permute-start(f32[320,768]{1,0:T(8,128)S(1)} %shard_map.86.a_ref), channel_id=1, source_target_pairs={{0,1},{1,0},{2,3},{3,2},{4,5},{5,4},{6,7},{7,6},{8,9},{9,8},{10,11... | collective-permute-start | bytes 2949128 | tf_op jit(solution)/shard_map/ppermute | solution.py:257
  68.4 4.5 %collective-permute-start.3 = (f32[320,768]{1,0:T(8,128)S(1)}, f32[320,768]{1,0:T(8,128)S(1)}, u32[]{:S(2)}, u32[]{:S(2)}) collective-permute-start(f32[320,768]{1,0:T(8,128)S(1)} %shard_map.87.a_ref), channel_id=1, source_target_pairs={{0,1},{1,0},{2,3},{3,2},{4,5},{5,4},{6,7},{7,6},{8,9},{9,8},{10,11... | collective-permute-start | bytes 2949128 | tf_op jit(solution)/shard_map/ppermute | solution.py:257
  73.9 22.1 %copy-start.6 = (s32[128,2]{0,1:T(2,128)S(1)}, s32[128,2]{0,1:T(2,128)}, u32[]{:S(2)}) copy-start(s32[128,2]{0,1:T(2,128)} %param.12) | copy-start | bytes 3076
  74.0 22.1 %copy-start.7 = (f32[128,2]{0,1:T(2,128)S(1)}, f32[128,2]{0,1:T(2,128)}, u32[]{:S(2)}) copy-start(f32[128,2]{0,1:T(2,128)} %param.11) | copy-start | bytes 3076
  74.0 22.1 %copy-start.8 = (f32[128]{0:T(128)S(1)}, f32[128]{0:T(128)}, u32[]{:S(2)}) copy-start(f32[128]{0:T(128)} %param.10) | copy-start | bytes 1540
  88.4 24.1 %all-to-all-start.3 = ((bf16[64,16,128]{2,1,0:T(8,128)(2,1)}), bf16[64,16,128]{2,1,0:T(8,128)(2,1)S(1)}, u32[]{:S(2)}, u32[]{:S(2)}) async-start(bf16[64,16,128]{2,1,0:T(8,128)(2,1)} %shard_map.92), calls=%async_computation.3 | async-start | bytes 524288 | tf_op jit(solution)/shard_map/all_to_all | solution.py:251

commit v6 on v5

--- a/solution.py
+++ b/solution.py
@@ -12,6 +12,7 @@
 F32 = jnp.float32
 LANES = 128
 FINE = 16
+VMEM_LIMIT = 16 * 1024 * 1024
 AXES = ("z", "y", "x", "c")
 
 
@@ -222,7 +223,7 @@
         out_shape=jax.ShapeDtypeStruct(shape, dtype),
         in_specs=[pl.BlockSpec(memory_space=pltpu.VMEM)] * len(operands),
         out_specs=pl.BlockSpec(memory_space=pltpu.VMEM),
-        compiler_params=pltpu.CompilerParams(vmem_limit_bytes=32 * 1024 * 1024),
+        compiler_params=pltpu.CompilerParams(vmem_limit_bytes=VMEM_LIMIT),
         cost_estimate=pl.CostEstimate(flops=flops, bytes_accessed=moved, transcendentals=0),
     )(*operands)
 
@@ -285,12 +286,16 @@
     weights = pl.pallas_call(
         order_kernel,
         out_shape=[jax.ShapeDtypeStruct(ordered, BF16)] * 6,
-        in_specs=[pl.BlockSpec(memory_space=pltpu.HBM)] * 3,
+        in_specs=[pl.BlockSpec(memory_space=pl.ANY)] * 3,
         out_specs=[pl.BlockSpec(memory_space=pltpu.VMEM)] * 6,
         scratch_shapes=[pltpu.SemaphoreType.DMA((2 * 3 * members * parts,))],
-        compiler_params=pltpu.CompilerParams(vmem_limit_bytes=32 * 1024 * 1024),
+        compiler_params=pltpu.CompilerParams(vmem_limit_bytes=VMEM_LIMIT),
         cost_estimate=pl.CostEstimate(flops=0, bytes_accessed=12 * 1024 * 1024, transcendentals=0),
-    )(w_gate.reshape(views), w_up.reshape(views), w_down[0].T.reshape(views))
+    )(
+        pltpu.with_memory_space_constraint(w_gate.reshape(views), pltpu.HBM),
+        pltpu.with_memory_space_constraint(w_up.reshape(views), pltpu.HBM),
+        w_down[0].T.reshape(views),
+    )
     weights = [w.reshape(members * wide, hidden) for w in weights]
     own, other = weights[:3], [other_core(w) for w in weights[3:]]
     got, own, other = lax.optimization_barrier((got, own, other))
@@ -318,18 +323,6 @@
     d_own = tail(part_own, rest_own)
     flops = flops // 3 * 2
     part = call(return_kernel, (rows, members * wide), F32, d_own, *own[:2], flops=flops)
-    d_other = tail(part_other, rest_other)
-    part = call(
-        return_add_kernel, (members, rows, wide), BF16, d_other, *other[:2], part, flops=flops
-    )
-    part = swap(part, near)
-    part = call(
-        functools.partial(repack_kernel, capacity, parts, spread),
-        (nz * spread, FINE, LANES),
-        BF16,
-        part,
-    )
-    part = swap(part, far)
     combine = call(
         functools.partial(combine_kernel, capacity, parts),
         (nz * LANES, tokens),
@@ -338,6 +331,19 @@
         route_prob.T,
         token_scale.reshape(1, tokens),
     )
+    part, combine = lax.optimization_barrier((part, combine))
+    d_other = tail(part_other, rest_other)
+    part = call(
+        return_add_kernel, (members, rows, wide), BF16, d_other, *other[:2], part, flops=flops
+    )
+    part = swap(part, near)
+    part = call(
+        functools.partial(repack_kernel, capacity, parts, spread),
+        (nz * spread, FINE, LANES),
+        BF16,
+        part,
+    )
+    part = swap(part, far)
     return call(
         functools.partial(final_kernel, capacity, parts, spread),
         (feats, tokens),

time: 114 us -> 112 us (0.982)
  blocking collectives: 32.3 us -> 54.6 us
  waiting for transfers between devices: 25.1 us -> 10.3 us
  starting transfers between devices: 39.1 us -> 31.6 us
  local copies, waits for them, and re-layouts: 5.32 us -> 2.55 us
    all_to_all x2 -> x3, blocking collectives: 32.3 us -> 54.6 us  [swap(): lax.all_to_all(blocks, AXES, split_axis=0, concat_axis=0, axis_index_grou...]
    all_to_all x2 -> x1, waiting for transfers between devices: 21.6 us -> 7 us  [swap(): lax.all_to_all(blocks, AXES, split_axis=0, concat_axis=0, axis_index_grou...]
    all_to_all x2 -> x1, starting transfers between devices: 27.5 us -> 19.9 us  [swap(): lax.all_to_all(blocks, AXES, split_axis=0, concat_axis=0, axis_index_grou...]
    unnamed x20 -> x16, local copies, waits for them, and re-layouts: 4.63 us -> 1.85 us
  transfers between devices with their start and end apart: 7 -> 6, of which waited for: 4 -> 3; matrix products, arithmetic and copies ran while one was open for 1% -> 1% of each run, Pallas kernels for 3% -> 4%
where the time goes in v6:
time: 112 us; the launch traced here: 111 us
  blocking collectives  54.6 us (49%)
  starting transfers between devices  31.6 us (28%)
  Pallas kernels  10.4 us (9%)
  waiting for transfers between devices  10.3 us (9%)
  local copies, waits for them, and re-layouts  2.55 us (2%)
  other arithmetic  1.53 us (1%)
    all_to_all x3, blocking collectives, swap(): lax.all_to_all(blocks, AXES, split_axis=0, concat_axis=0, axis_index_grou...  54.6 us
    all_to_all x1, starting transfers between devices, swap(): lax.all_to_all(blocks, AXES, split_axis=0, concat_axis=0, axis_index_grou...  19.9 us
    ppermute x5, starting transfers between devices, other_core(): return lax.ppermute(values, 'c', [(0, 1), (1, 0)])  11.8 us
    pallas_call x11, Pallas kernels, call(): pl.pallas_call(kernel, out_shape=jax.ShapeDtypeStruct(shape, dtype), in_s...  7.74 us
    all_to_all x1, waiting for transfers between devices, swap(): lax.all_to_all(blocks, AXES, split_axis=0, concat_axis=0, axis_index_grou...  7 us
    ppermute x5, waiting for transfers between devices, other_core(): return lax.ppermute(values, 'c', [(0, 1), (1, 0)])  3.29 us
    pallas_call x1, Pallas kernels, shards(): pl.pallas_call(order_kernel, out_shape=[jax.ShapeDtypeStruct(ordered, BF1...  2.63 us
  transfers between devices with their start and end apart: 6, of which 3 were waited for; matrix products, arithmetic and copies ran while one was open for 1% of the time, Pallas kernels for 4%

profile of v6, /device:TPU:1, one launch (start us, length us, event | category | flops | bytes accessed | tf_op | source)
XLA Modules:
  0.0 111.2 jit_solution(14149039420307482086)
XLA Ops:
  0.0 0.0 copy-start.7
  0.0 0.8 bitcast_convert_fusion
  0.8 0.7 fusion.1.head_ref
  1.5 1.2 %shard_map.82 = bf16[8,8,32,128]{3,2,1,0:T(8,128)(2,1)} custom-call(bf16[112,128]{1,0:T(8,128)(2,1)S(1)} %fusion.1.head_ref), custom_call_target="tpu_custom_call" | custom-call | bytes 552960 | tf_op jit(solution)/shard_map/pallas_call | solution.py:221
  2.8 19.9 %all-to-all-start = ((bf16[64,32,128]{2,1,0:T(8,128)(2,1)}), bf16[64,32,128]{2,1,0:T(8,128)(2,1)}, u32[]{:S(2)}, u32[]{:S(2)}) async-start(bf16[64,32,128]{2,1,0:T(8,128)(2,1)} %bitcast.3), calls=%async_computation | async-start | bytes 1048576 | tf_op jit(solution)/shard_map/all_to_all | solution.py:252
  22.6 0.0 copy-done.7
  22.7 0.7 copy.9
  23.4 2.6 %shard_map.83 = (bf16[4,3,4,2,16,256]{5,4,3,2,1,0:T(8,128)(2,1)S(1)}, bf16[4,3,4,2,16,256]{5,4,3,2,1,0:T(8,128)(2,1)S(1)}, bf16[4,3,4,2,16,256]{5,4,3,2,1,0:T(8,...) custom-call(bf16[4,2,2,2,2,3,16,256]{7,6,5,4,3,2,1,0:T(8,128)(2,1)} , ...), custom_call_target="tpu_custom_call" | custom-call | bytes 12582912 | tf_op jit(solution)/shard_map/pallas_call | solution.py:286
  26.0 0.0 copy-start
  26.0 0.9 copy-done
  26.9 2.9 %collective-permute-start = (bf16[1536,256]{1,0:T(8,128)(2,1)S(1)}, bf16[1536,256]{1,0:T(8,128)(2,1)S(1)}, u32[]{:S(2)}, u32[]{:S(2)}) collective-permute-start(bf16[1536,256]{1,0:T(8,128)(2,1)S(1)} %bitcast.31), channel_id=1, source_target_pairs={{0,1},{1,0},{2,3},{3,2},{4,5},{5,4},{6,7},{7,6},{8,9},{9,8},{10,11... | collective-permute-start | bytes 2359304 | tf_op jit(solution)/shard_map/ppermute | solution.py:258
  29.8 1.9 %collective-permute-start.1 = (bf16[1536,256]{1,0:T(8,128)(2,1)S(1)}, bf16[1536,256]{1,0:T(8,128)(2,1)S(1)}, u32[]{:S(2)}, u32[]{:S(2)}) collective-permute-start(bf16[1536,256]{1,0:T(8,128)(2,1)S(1)} %bitcast.30), channel_id=1, source_target_pairs={{0,1},{1,0},{2,3},{3,2},{4,5},{5,4},{6,7},{7,6},{8,9},{9,8},{10,11... | collective-permute-start | bytes 2359304 | tf_op jit(solution)/shard_map/ppermute | solution.py:258
  31.7 2.4 %collective-permute-start.2 = (bf16[1536,256]{1,0:T(8,128)(2,1)S(1)}, bf16[1536,256]{1,0:T(8,128)(2,1)S(1)}, u32[]{:S(2)}, u32[]{:S(2)}) collective-permute-start(bf16[1536,256]{1,0:T(8,128)(2,1)S(1)} %bitcast.29), channel_id=1, source_target_pairs={{0,1},{1,0},{2,3},{3,2},{4,5},{5,4},{6,7},{7,6},{8,9},{9,8},{10,11... | collective-permute-start | bytes 2359304 | tf_op jit(solution)/shard_map/ppermute | solution.py:258
  34.1 0.0 collective-permute-done.gate_ref
  34.1 0.0 collective-permute-done.1.up_ref
  34.1 1.9 %collective-permute-done.2.down_ref = bf16[1536,256]{1,0:T(8,128)(2,1)S(1)} collective-permute-done((bf16[1536,256]{1,0:T(8,128)(2,1)S(1)}, bf16[1536,256]{1,0:T(8,128)(2,1)S(1)}, u32[]{:S(2)}, u32[]{:S(2)}) %collective-permute-start.2) | collective-permute-done | bytes 786464 | tf_op jit(solution)/shard_map/ppermute | solution.py:258
  36.0 0.0 copy-start.2
  36.0 0.9 copy-done.2
  36.9 7.0 %all-to-all-done.in_ref = bf16[64,32,128]{2,1,0:T(8,128)(2,1)} async-done(((bf16[64,32,128]{2,1,0:T(8,128)(2,1)}), bf16[64,32,128]{2,1,0:T(8,128)(2,1)}, u32[]{:S(2)}, u32[]{:S(2)}) %all-to-all-start) | async-done | bytes 524320 | tf_op jit(solution)/shard_map/all_to_all | solution.py:252
  43.9 1.4 %shard_map.84 = bf16[4,640,384]{2,1,0:T(8,128)(2,1)S(1)} custom-call(bf16[64,32,128]{2,1,0:T(8,128)(2,1)} %all-to-all-done.in_ref), custom_call_target="tpu_custom_call" | custom-call | bytes 2490368 | tf_op jit(solution)/shard_map/pallas_call | solution.py:221
  45.3 0.0 copy-start.3
  45.3 18.7 %all_to_all.20.in_ref = bf16[4,640,384]{2,1,0:T(8,128)(2,1)S(1)} all-to-all(bf16[4,640,384]{2,1,0:T(8,128)(2,1)S(1)} %shard_map.84), channel_id=1, replica_groups={{0,2,8,10},{4,6,12,14},{16,18,24,26},{20,22,28,30},{32,34,40,42},{36,38..., dimensions={0} | all-to-all | bytes 3932160 | tf_op jit(solution)/shard_map/all_to_all | solution.py:252
  64.0 0.0 copy-done.3
  64.0 0.0 copy-start.1
  64.0 0.9 shard_map.86.a_ref
  65.0 0.0 copy-start.4
  65.0 0.0 copy-start.5
  65.0 0.0 copy-start.6
  65.0 2.7 %collective-permute-start.3 = (f32[320,768]{1,0:T(8,128)S(1)}, f32[320,768]{1,0:T(8,128)S(1)}, u32[]{:S(2)}, u32[]{:S(2)}) collective-permute-start(f32[320,768]{1,0:T(8,128)S(1)} %shard_map.86.a_ref), channel_id=1, source_target_pairs={{0,1},{1,0},{2,3},{3,2},{4,5},{5,4},{6,7},{7,6},{8,9},{9,8},{10,11... | collective-permute-start | bytes 2949128 | tf_op jit(solution)/shard_map/ppermute | solution.py:258
  67.7 0.0 copy-done.1
  67.7 0.9 shard_map.85.a_ref
  68.6 1.9 %collective-permute-start.4 = (f32[320,768]{1,0:T(8,128)S(1)}, f32[320,768]{1,0:T(8,128)S(1)}, u32[]{:S(2)}, u32[]{:S(2)}) collective-permute-start(f32[320,768]{1,0:T(8,128)S(1)} %shard_map.85.a_ref), channel_id=1, source_target_pairs={{0,1},{1,0},{2,3},{3,2},{4,5},{5,4},{6,7},{7,6},{8,9},{9,8},{10,11... | collective-permute-start | bytes 2949128 | tf_op jit(solution)/shard_map/ppermute | solution.py:258
  70.5 0.0 copy-done.4
  70.5 0.0 copy-done.5
  70.6 0.0 copy-done.6
  70.6 0.2 shard_map.89.combine_ref
  70.7 0.0 collective-permute-done.3.b_ref
  70.8 0.2 shard_map.87.d_ref
  70.9 0.7 shard_map.88.sum_ref
  71.7 1.4 %collective-permute-done.4.b_ref = f32[320,768]{1,0:T(8,128)S(1)} collective-permute-done((f32[320,768]{1,0:T(8,128)S(1)}, f32[320,768]{1,0:T(8,128)S(1)}, u32[]{:S(2)}, u32[]{:S(2)}) %collective-permute-start.4) | collective-permute-done | bytes 983072 | tf_op jit(solution)/shard_map/ppermute | solution.py:258
  73.1 0.2 shard_map.90.d_ref
  73.3 0.9 shard_map.91
  74.1 13.4 %all_to_all.21.in_ref = bf16[4,320,384]{2,1,0:T(8,128)(2,1)S(1)} all-to-all(bf16[4,320,384]{2,1,0:T(8,128)(2,1)S(1)} %shard_map.91), channel_id=1, replica_groups={{0,2,8,10},{4,6,12,14},{16,18,24,26},{20,22,28,30},{32,34,40,42},{36,38..., dimensions={0} | all-to-all | bytes 1966080 | tf_op jit(solution)/shard_map/all_to_all | solution.py:252
  87.6 0.2 shard_map.92
  87.8 22.5 %all_to_all.22.in_ref = bf16[64,16,128]{2,1,0:T(8,128)(2,1)S(1)} all-to-all(bf16[64,16,128]{2,1,0:T(8,128)(2,1)S(1)} %shard_map.92), channel_id=1, replica_groups={{0,4,16,20,32,36,48,52,64,68,80,84,96,100,112,116,128,132,144,148,160,1..., dimensions={0} | all-to-all | bytes 524288 | tf_op jit(solution)/shard_map/all_to_all | solution.py:252
  110.2 1.0 shard_map.93
Async XLA Ops:
  0.0 22.6 %copy-start.7 = (bf16[1,256,3072]{2,1,0:T(8,128)(2,1)S(1)}, bf16[1,256,3072]{2,1,0:T(8,128)(2,1)}, u32[]{:S(2)}) copy-start(bf16[1,256,3072]{2,1,0:T(8,128)(2,1)} %param.15) | copy-start | bytes 4718596
  2.8 41.1 %all-to-all-start = ((bf16[64,32,128]{2,1,0:T(8,128)(2,1)}), bf16[64,32,128]{2,1,0:T(8,128)(2,1)}, u32[]{:S(2)}, u32[]{:S(2)}) async-start(bf16[64,32,128]{2,1,0:T(8,128)(2,1)} %bitcast.3), calls=%async_computation | async-start | bytes 1048576 | tf_op jit(solution)/shard_map/all_to_all | solution.py:252
  26.0 0.9 copy-start
  26.9 7.2 %collective-permute-start = (bf16[1536,256]{1,0:T(8,128)(2,1)S(1)}, bf16[1536,256]{1,0:T(8,128)(2,1)S(1)}, u32[]{:S(2)}, u32[]{:S(2)}) collective-permute-start(bf16[1536,256]{1,0:T(8,128)(2,1)S(1)} %bitcast.31), channel_id=1, source_target_pairs={{0,1},{1,0},{2,3},{3,2},{4,5},{5,4},{6,7},{7,6},{8,9},{9,8},{10,11... | collective-permute-start | bytes 2359304 | tf_op jit(solution)/shard_map/ppermute | solution.py:258
  29.8 4.4 %collective-permute-start.1 = (bf16[1536,256]{1,0:T(8,128)(2,1)S(1)}, bf16[1536,256]{1,0:T(8,128)(2,1)S(1)}, u32[]{:S(2)}, u32[]{:S(2)}) collective-permute-start(bf16[1536,256]{1,0:T(8,128)(2,1)S(1)} %bitcast.30), channel_id=1, source_target_pairs={{0,1},{1,0},{2,3},{3,2},{4,5},{5,4},{6,7},{7,6},{8,9},{9,8},{10,11... | collective-permute-start | bytes 2359304 | tf_op jit(solution)/shard_map/ppermute | solution.py:258
  31.7 4.3 %collective-permute-start.2 = (bf16[1536,256]{1,0:T(8,128)(2,1)S(1)}, bf16[1536,256]{1,0:T(8,128)(2,1)S(1)}, u32[]{:S(2)}, u32[]{:S(2)}) collective-permute-start(bf16[1536,256]{1,0:T(8,128)(2,1)S(1)} %bitcast.29), channel_id=1, source_target_pairs={{0,1},{1,0},{2,3},{3,2},{4,5},{5,4},{6,7},{7,6},{8,9},{9,8},{10,11... | collective-permute-start | bytes 2359304 | tf_op jit(solution)/shard_map/ppermute | solution.py:258
  36.0 0.9 copy-start.2
  45.3 18.7 %copy-start.3 = (bf16[1536,256]{1,0:T(8,128)(2,1)S(1)}, bf16[1536,256]{1,0:T(8,128)(2,1)}, u32[]{:S(2)}) copy-start(bf16[1536,256]{1,0:T(8,128)(2,1)} %copy-done.2) | copy-start | bytes 2359300
  64.0 3.7 %copy-start.1 = (bf16[4,3,4,2,16,256]{5,4,3,2,1,0:T(8,128)(2,1)S(1)}, bf16[4,3,4,2,16,256]{5,4,3,2,1,0:T(8,128)(2,1)}, u32[]{:S(2)}) copy-start(bf16[4,3,4,2,16,256]{5,4,3,2,1,0:T(8,128)(2,1)} %copy-done) | copy-start | bytes 2359300
  65.0 5.6 %copy-start.4 = (s32[128,2]{0,1:T(2,128)S(1)}, s32[128,2]{0,1:T(2,128)}, u32[]{:S(2)}) copy-start(s32[128,2]{0,1:T(2,128)} %param.12) | copy-start | bytes 3076
  65.0 5.6 %copy-start.5 = (f32[128,2]{0,1:T(2,128)S(1)}, f32[128,2]{0,1:T(2,128)}, u32[]{:S(2)}) copy-start(f32[128,2]{0,1:T(2,128)} %param.11) | copy-start | bytes 3076
  65.0 5.6 %copy-start.6 = (f32[128]{0:T(128)S(1)}, f32[128]{0:T(128)}, u32[]{:S(2)}) copy-start(f32[128]{0:T(128)} %param.10) | copy-start | bytes 1540
  65.0 5.8 %collective-permute-start.3 = (f32[320,768]{1,0:T(8,128)S(1)}, f32[320,768]{1,0:T(8,128)S(1)}, u32[]{:S(2)}, u32[]{:S(2)}) collective-permute-start(f32[320,768]{1,0:T(8,128)S(1)} %shard_map.86.a_ref), channel_id=1, source_target_pairs={{0,1},{1,0},{2,3},{3,2},{4,5},{5,4},{6,7},{7,6},{8,9},{9,8},{10,11... | collective-permute-start | bytes 2949128 | tf_op jit(solution)/shard_map/ppermute | solution.py:258
  68.6 4.5 %collective-permute-start.4 = (f32[320,768]{1,0:T(8,128)S(1)}, f32[320,768]{1,0:T(8,128)S(1)}, u32[]{:S(2)}, u32[]{:S(2)}) collective-permute-start(f32[320,768]{1,0:T(8,128)S(1)} %shard_map.85.a_ref), channel_id=1, source_target_pairs={{0,1},{1,0},{2,3},{3,2},{4,5},{5,4},{6,7},{7,6},{8,9},{9,8},{10,11... | collective-permute-start | bytes 2949128 | tf_op jit(solution)/shard_map/ppermute | solution.py:258

commit v7 on v6

--- a/solution.py
+++ b/solution.py
@@ -48,21 +48,29 @@
     return jnp.where(hit, before, -2.0), first
 
 
-def pack_kernel(capacity, feats, head_ref, out_ref):
-    nz, members = out_ref.shape[:2]
-    tokens = head_ref.shape[1]
+def pack_kernel(capacity, ids_hbm, x_hbm, g_hbm, out_ref, ids_ref, x_ref, g_ref, sems):
+    copies = [
+        pltpu.make_async_copy(src, dst, sems.at[i])
+        for i, (src, dst) in enumerate(((ids_hbm, ids_ref), (x_hbm, x_ref), (g_hbm, g_ref)))
+    ]
+    for copy in copies:
+        copy.start()
+    nya, nz, nxa = out_ref.shape[:3]
+    feats, tokens = x_ref.shape
     parts = feats // FINE
     lanes = nz * LANES
     part = lane_parts((FINE, lanes), 1, capacity)
     slot_of_lane = lane_slots(tokens, capacity, parts)
-    slots, _ = token_slots(head_ref[2 * feats :, :].astype(F32), nz)
+    copies[0].wait()
+    slots, _ = token_slots(ids_ref[...].astype(F32), nz)
     place = jnp.concatenate(
         [jnp.where(slots[z : z + 1] == slot_of_lane, 1.0, 0.0).astype(BF16) for z in range(nz)],
         axis=0,
     )
-    for kind in range(2):
+    for kind, ref in enumerate((x_ref, g_ref)):
+        copies[1 + kind].wait()
         spread = lax.dot_general(
-            head_ref[kind * feats : (kind + 1) * feats, :],
+            ref[...],
             place,
             (((1,), (1,)), ((), ())),
             preferred_element_type=F32,
@@ -72,22 +80,22 @@
             block = jnp.where(part == p, spread[p * FINE : (p + 1) * FINE], block)
         block = block.astype(BF16)
         for z in range(nz):
-            for m in range(members):
-                out_ref[z, m, kind * FINE : (kind + 1) * FINE, :] = block[
-                    :, z * LANES : (z + 1) * LANES
-                ]
-
-
-def unpack_kernel(capacity, parts, ny, in_ref, out_ref):
+            piece = block[:, z * LANES : (z + 1) * LANES]
+            for ya in range(nya):
+                for xa in range(nxa):
+                    out_ref[ya, z, xa, kind * FINE : (kind + 1) * FINE, :] = piece
+
+
+def unpack_kernel(capacity, parts, in_ref, out_ref):
     nx, _, wide = out_ref.shape
-    nz = in_ref.shape[0] // ny
+    nz = in_ref.shape[1]
     span = wide // parts
     rows = nz * capacity
     for kind in range(2):
         for pair in range(0, nz, 2):
             turned = []
             for z in (pair, pair + 1):
-                block = in_ref[z * ny : (z + 1) * ny, kind * FINE : (kind + 1) * FINE, :]
+                block = in_ref[:, z, :, kind * FINE : (kind + 1) * FINE, :]
                 turned.append(block.reshape(span, LANES).astype(F32).T)
             start = kind * rows + pair * capacity
             for p in range(parts):
@@ -98,7 +106,7 @@
                     out_ref[i, start : start + 2 * capacity, p * span : (p + 1) * span] = piece
 
 
-def repack_kernel(capacity, parts, ny, in_ref, out_ref):
+def repack_kernel(capacity, parts, in_ref, out_ref):
     nx, rows, wide = in_ref.shape
     span = wide // parts
     for pair in range(0, rows // capacity, 2):
@@ -112,7 +120,7 @@
             pieces.append(jnp.zeros((LANES - parts * capacity, span), F32))
             turned = jnp.concatenate(pieces, axis=0).T.astype(BF16)
             z = pair + half
-            out_ref[z * ny : (z + 1) * ny] = turned.reshape(ny, FINE, LANES)
+            out_ref[:, z] = turned.reshape(out_ref.shape[0], out_ref.shape[2], FINE, LANES)
 
 
 def order_kernel(*refs):
@@ -194,14 +202,15 @@
         )
 
 
-def final_kernel(capacity, parts, ny, combine_ref, in_ref, out_ref):
+def final_kernel(capacity, parts, combine_ref, in_ref, out_ref):
     lanes = combine_ref.shape[0]
     nz = lanes // LANES
     sums = []
     for z in range(nz):
-        total = in_ref[z * ny].astype(F32)
-        for y in range(1, ny):
-            total += in_ref[z * ny + y].astype(F32)
+        total = jnp.zeros((FINE, LANES), F32)
+        for ya in range(in_ref.shape[0]):
+            for xa in range(in_ref.shape[2]):
+                total += in_ref[ya, z, xa].astype(F32)
         sums.append(total)
     sums = jnp.concatenate(sums, axis=1)
     part = lane_parts(sums.shape, 1, capacity)
@@ -235,7 +244,12 @@
     halves = [(yb, xb) for yb in range(2) for xb in range(2)]
     places = [(2 * ya, 2 * xa) for ya in range(ny // 2) for xa in range(nx // 2)]
     far = [
-        [index(z, y + yb, x + xb, c) for z in range(nz) for y, x in places]
+        [
+            index(z, 2 * ya + yb, 2 * xa + xb, c)
+            for ya in range(ny // 2)
+            for z in range(nz)
+            for xa in range(nx // 2)
+        ]
         for c in range(nc)
         for yb, xb in halves
     ]
@@ -271,23 +285,25 @@
     rows = nz * capacity
     wide = feats * spread
 
-    ids = jnp.pad(route_ids.T.astype(BF16), ((0, FINE - route_ids.shape[1]), (0, 0)))
-    head = jnp.concatenate([activations.T, out_grad.T, ids], axis=0)
-    send = call(
-        functools.partial(pack_kernel, capacity, feats),
-        (nz, spread, 2 * FINE, LANES),
-        BF16,
-        head,
-    )
+    heads = [route_ids.T, activations.T, out_grad.T]
+    send = pl.pallas_call(
+        functools.partial(pack_kernel, capacity),
+        out_shape=jax.ShapeDtypeStruct((ny // 2, nz, nx // 2, 2 * FINE, LANES), BF16),
+        in_specs=[pl.BlockSpec(memory_space=pl.ANY)] * 3,
+        out_specs=pl.BlockSpec(memory_space=pltpu.VMEM),
+        scratch_shapes=[pltpu.VMEM(h.shape, h.dtype) for h in heads]
+        + [pltpu.SemaphoreType.DMA((3,))],
+        compiler_params=pltpu.CompilerParams(vmem_limit_bytes=VMEM_LIMIT),
+    )(*(pltpu.with_memory_space_constraint(h, pltpu.HBM) for h in heads))
     got = swap(send.reshape(nz * spread, 2 * FINE, LANES), far)
 
     views = (ny // 2, 2, nx // 2, 2, nc, parts, FINE, hidden)
     ordered = (members, parts, ny // 2, nx // 2, FINE, hidden)
     weights = pl.pallas_call(
         order_kernel,
-        out_shape=[jax.ShapeDtypeStruct(ordered, BF16)] * 6,
+        out_shape=[pltpu.HBM(ordered, BF16)] * 3 + [jax.ShapeDtypeStruct(ordered, BF16)] * 3,
         in_specs=[pl.BlockSpec(memory_space=pl.ANY)] * 3,
-        out_specs=[pl.BlockSpec(memory_space=pltpu.VMEM)] * 6,
+        out_specs=[pl.BlockSpec(memory_space=m) for m in [pltpu.HBM] * 3 + [pltpu.VMEM] * 3],
         scratch_shapes=[pltpu.SemaphoreType.DMA((2 * 3 * members * parts,))],
         compiler_params=pltpu.CompilerParams(vmem_limit_bytes=VMEM_LIMIT),
         cost_estimate=pl.CostEstimate(flops=0, bytes_accessed=12 * 1024 * 1024, transcendentals=0),
@@ -301,10 +317,10 @@
     got, own, other = lax.optimization_barrier((got, own, other))
 
     copies = call(
-        functools.partial(unpack_kernel, capacity, parts, spread),
+        functools.partial(unpack_kernel, capacity, parts),
         (members, 2 * rows, wide),
         BF16,
-        got,
+        got.reshape(ny // 2, nz, nx // 2, 2 * FINE, LANES),
     )
     block = swap(copies, near)
 
@@ -338,18 +354,18 @@
     )
     part = swap(part, near)
     part = call(
-        functools.partial(repack_kernel, capacity, parts, spread),
-        (nz * spread, FINE, LANES),
+        functools.partial(repack_kernel, capacity, parts),
+        (ny // 2, nz, nx // 2, FINE, LANES),
         BF16,
         part,
     )
-    part = swap(part, far)
+    part = swap(part.reshape(nz * spread, FINE, LANES), far)
     return call(
-        functools.partial(final_kernel, capacity, parts, spread),
+        functools.partial(final_kernel, capacity, parts),
         (feats, tokens),
         BF16,
         combine,
-        part,
+        part.reshape(ny // 2, nz, nx // 2, FINE, LANES),
     ).T
 
 

time: 112 us -> 154 us (1.38)
  Pallas kernels: 10.4 us -> 57 us
  waiting for transfers between devices: 10.3 us -> 2.94 us
  blocking collectives: 54.6 us -> 60.5 us
    pallas_call x1 -> x2, Pallas kernels: 2.63 us -> 51.5 us  [the longest x1 49.5 us: shards(): pl.pallas_call(order_kernel, out_shape=[pltpu.HBM(ordered, BF16)] * 3 + [...]
    all_to_all x1, waiting for transfers between devices: 7 us -> 0.01 us  [swap(): lax.all_to_all(blocks, AXES, split_axis=0, concat_axis=0, axis_index_grou...]
    all_to_all x3, blocking collectives: 54.6 us -> 60.5 us  [swap(): lax.all_to_all(blocks, AXES, split_axis=0, concat_axis=0, axis_index_grou...]
    pallas_call x11 -> x10, Pallas kernels: 7.74 us -> 5.44 us  [call(): pl.pallas_call(kernel, out_shape=jax.ShapeDtypeStruct(shape, dtype), in_s...]
    unnamed x16 -> x12, local copies, waits for them, and re-layouts: 1.85 us -> 0.03 us
  transfers between devices with their start and end apart: 6 -> 6, of which waited for: 3 -> 2; matrix products, arithmetic and copies ran while one was open for 1% -> 1% of each run, Pallas kernels for 4% -> 33%
where the time goes in v7:
time: 154 us
  blocking collectives  60.5 us (39%)
  Pallas kernels  57 us (37%)
  starting transfers between devices  31.3 us (20%)
  waiting for transfers between devices  2.94 us (2%)
  local copies, waits for them, and re-layouts  1.74 us (1%)
    all_to_all x3, blocking collectives, swap(): lax.all_to_all(blocks, AXES, split_axis=0, concat_axis=0, axis_index_grou...  60.5 us
    pallas_call x1, Pallas kernels, shards(): pl.pallas_call(order_kernel, out_shape=[pltpu.HBM(ordered, BF16)] * 3 + [...  49.5 us
    all_to_all x1, starting transfers between devices, swap(): lax.all_to_all(blocks, AXES, split_axis=0, concat_axis=0, axis_index_grou...  19.6 us
    ppermute x5, starting transfers between devices, other_core(): return lax.ppermute(values, 'c', [(0, 1), (1, 0)])  11.6 us
    pallas_call x10, Pallas kernels, call(): pl.pallas_call(kernel, out_shape=jax.ShapeDtypeStruct(shape, dtype), in_s...  5.44 us
  transfers between devices with their start and end apart: 6, of which 2 were waited for; matrix products, arithmetic and copies ran while one was open for 1% of the time, Pallas kernels for 33%

profile of v7, /device:TPU:1, one launch (start us, length us, event | category | flops | bytes accessed | tf_op | source)
XLA Modules:
  0.0 153.7 jit_solution(1557029511960308525)
XLA Ops:
  0.0 2.1 %shard_map.82 = bf16[4,8,2,32,128]{4,3,2,1,0:T(8,128)(2,1)} custom-call(s32[2,128]{1,0:T(2,128)} %bitcast.31, bf16[48,128]{1,0:T(8,128)(2,1)} %bitcast.41, bf16[48,128]{1,0:T(8,128)(2,1)} %bitcast.42), custom_call_target="tpu_custom_call" | custom-call | tf_op jit(solution)/shard_map/pallas_call | solution.py:289
  2.1 19.6 %all-to-all-start = ((bf16[64,32,128]{2,1,0:T(8,128)(2,1)}), bf16[64,32,128]{2,1,0:T(8,128)(2,1)S(1)}, u32[]{:S(2)}, u32[]{:S(2)}) async-start(bf16[64,32,128]{2,1,0:T(8,128)(2,1)} %bitcast.3), calls=%async_computation | async-start | bytes 1048576 | tf_op jit(solution)/shard_map/all_to_all | solution.py:266
  21.7 1.7 %copy.9 = bf16[3072,256]{1,0:T(8,128)(2,1)S(1)} copy(bf16[3072,256]{0,1:T(8,128)(2,1)} %bitcast.38) | data formatting | bytes 3145728 | tf_op jit(solution)/shard_map/transpose | solution.py:313
  23.4 49.5 %shard_map.83 = (bf16[4,3,4,2,16,256]{5,4,3,2,1,0:T(8,128)(2,1)}, bf16[4,3,4,2,16,256]{5,4,3,2,1,0:T(8,128)(2,1)}, bf16[4,3,4,2,16,256]{5,4,3,2,1,0:T(8,128)(2,1...) custom-call(bf16[4,2,2,2,2,3,16,256]{7,6,5,4,3,2,1,0:T(8,128)(2,1)} , ...), custom_call_target="tpu_custom_call" | custom-call | bytes 12582912 | tf_op jit(solution)/shard_map/pallas_call | solution.py:302
  72.9 2.9 %collective-permute-start = (bf16[1536,256]{1,0:T(8,128)(2,1)S(1)}, bf16[1536,256]{1,0:T(8,128)(2,1)S(1)}, u32[]{:S(2)}, u32[]{:S(2)}) collective-permute-start(bf16[1536,256]{1,0:T(8,128)(2,1)S(1)} %bitcast.37), channel_id=1, source_target_pairs={{0,1},{1,0},{2,3},{3,2},{4,5},{5,4},{6,7},{7,6},{8,9},{9,8},{10,11... | collective-permute-start | bytes 2359304 | tf_op jit(solution)/shard_map/ppermute | solution.py:272
  75.8 1.9 %collective-permute-start.1 = (bf16[1536,256]{1,0:T(8,128)(2,1)S(1)}, bf16[1536,256]{1,0:T(8,128)(2,1)S(1)}, u32[]{:S(2)}, u32[]{:S(2)}) collective-permute-start(bf16[1536,256]{1,0:T(8,128)(2,1)S(1)} %bitcast.36), channel_id=1, source_target_pairs={{0,1},{1,0},{2,3},{3,2},{4,5},{5,4},{6,7},{7,6},{8,9},{9,8},{10,11... | collective-permute-start | bytes 2359304 | tf_op jit(solution)/shard_map/ppermute | solution.py:272
  77.7 2.4 %collective-permute-start.2 = (bf16[1536,256]{1,0:T(8,128)(2,1)S(1)}, bf16[1536,256]{1,0:T(8,128)(2,1)S(1)}, u32[]{:S(2)}, u32[]{:S(2)}) collective-permute-start(bf16[1536,256]{1,0:T(8,128)(2,1)S(1)} %bitcast.35), channel_id=1, source_target_pairs={{0,1},{1,0},{2,3},{3,2},{4,5},{5,4},{6,7},{7,6},{8,9},{9,8},{10,11... | collective-permute-start | bytes 2359304 | tf_op jit(solution)/shard_map/ppermute | solution.py:272
  80.1 0.0 collective-permute-done.gate_ref
  80.1 0.0 collective-permute-done.1.up_ref
  80.1 1.9 %collective-permute-done.2.down_ref = bf16[1536,256]{1,0:T(8,128)(2,1)S(1)} collective-permute-done((bf16[1536,256]{1,0:T(8,128)(2,1)S(1)}, bf16[1536,256]{1,0:T(8,128)(2,1)S(1)}, u32[]{:S(2)}, u32[]{:S(2)}) %collective-permute-start.2) | collective-permute-done | bytes 786464 | tf_op jit(solution)/shard_map/ppermute | solution.py:272
  82.0 0.0 all-to-all-done
  82.0 0.3 shard_map.84
  82.3 22.2 %all_to_all.20.in_ref = bf16[4,640,384]{2,1,0:T(8,128)(2,1)S(1)} all-to-all(bf16[4,640,384]{2,1,0:T(8,128)(2,1)S(1)} %shard_map.84), channel_id=1, replica_groups={{0,2,8,10},{4,6,12,14},{16,18,24,26},{20,22,28,30},{32,34,40,42},{36,38..., dimensions={0} | all-to-all | bytes 3932160 | tf_op jit(solution)/shard_map/all_to_all | solution.py:266
  104.5 0.0 copy-start
  104.5 0.0 copy-start.1
  104.5 0.0 copy-start.2
  104.5 0.9 shard_map.86.a_ref
  105.4 0.0 copy-start.3
  105.4 0.0 copy-start.4
  105.5 0.0 copy-start.5
  105.5 2.1 %collective-permute-start.3 = (f32[320,768]{1,0:T(8,128)S(1)}, f32[320,768]{1,0:T(8,128)S(1)}, u32[]{:S(2)}, u32[]{:S(2)}) collective-permute-start(f32[320,768]{1,0:T(8,128)S(1)} %shard_map.86.a_ref), channel_id=1, source_target_pairs={{0,1},{1,0},{2,3},{3,2},{4,5},{5,4},{6,7},{7,6},{8,9},{9,8},{10,11... | collective-permute-start | bytes 2949128 | tf_op jit(solution)/shard_map/ppermute | solution.py:272
  107.5 0.0 copy-done
  107.5 0.0 copy-done.1
  107.5 0.0 copy-done.2
  107.6 0.9 shard_map.85.a_ref
  108.5 2.4 %collective-permute-start.4 = (f32[320,768]{1,0:T(8,128)S(1)}, f32[320,768]{1,0:T(8,128)S(1)}, u32[]{:S(2)}, u32[]{:S(2)}) collective-permute-start(f32[320,768]{1,0:T(8,128)S(1)} %shard_map.85.a_ref), channel_id=1, source_target_pairs={{0,1},{1,0},{2,3},{3,2},{4,5},{5,4},{6,7},{7,6},{8,9},{9,8},{10,11... | collective-permute-start | bytes 2949128 | tf_op jit(solution)/shard_map/ppermute | solution.py:272
  110.9 0.0 copy-done.3
  110.9 0.0 copy-done.4
  110.9 0.0 copy-done.5
  110.9 0.2 shard_map.89.combine_ref
  111.1 0.0 collective-permute-done.3.b_ref
  111.1 0.2 shard_map.87.d_ref
  111.3 0.7 shard_map.88.sum_ref
  112.0 1.1 collective-permute-done.4.b_ref
  113.1 0.2 shard_map.90.d_ref
  113.3 0.8 shard_map.91
  114.1 13.4 %all_to_all.21.in_ref = bf16[4,320,384]{2,1,0:T(8,128)(2,1)S(1)} all-to-all(bf16[4,320,384]{2,1,0:T(8,128)(2,1)S(1)} %shard_map.91), channel_id=1, replica_groups={{0,2,8,10},{4,6,12,14},{16,18,24,26},{20,22,28,30},{32,34,40,42},{36,38..., dimensions={0} | all-to-all | bytes 1966080 | tf_op jit(solution)/shard_map/all_to_all | solution.py:266
  127.5 0.2 shard_map.92
  127.7 24.9 %all_to_all.22 = bf16[64,16,128]{2,1,0:T(8,128)(2,1)S(1)} all-to-all(bf16[64,16,128]{2,1,0:T(8,128)(2,1)S(1)} %bitcast.29), channel_id=1, replica_groups={{0,4,64,68,128,132,192,196,256,260,320,324,384,388,448,452,16,20,80,84,..., dimensions={0} | all-to-all | bytes 524288 | tf_op jit(solution)/shard_map/all_to_all | solution.py:266
  152.7 1.0 shard_map.93
Async XLA Ops:
  2.1 79.9 %all-to-all-start = ((bf16[64,32,128]{2,1,0:T(8,128)(2,1)}), bf16[64,32,128]{2,1,0:T(8,128)(2,1)S(1)}, u32[]{:S(2)}, u32[]{:S(2)}) async-start(bf16[64,32,128]{2,1,0:T(8,128)(2,1)} %bitcast.3), calls=%async_computation | async-start | bytes 1048576 | tf_op jit(solution)/shard_map/all_to_all | solution.py:266
  72.9 7.2 %collective-permute-start = (bf16[1536,256]{1,0:T(8,128)(2,1)S(1)}, bf16[1536,256]{1,0:T(8,128)(2,1)S(1)}, u32[]{:S(2)}, u32[]{:S(2)}) collective-permute-start(bf16[1536,256]{1,0:T(8,128)(2,1)S(1)} %bitcast.37), channel_id=1, source_target_pairs={{0,1},{1,0},{2,3},{3,2},{4,5},{5,4},{6,7},{7,6},{8,9},{9,8},{10,11... | collective-permute-start | bytes 2359304 | tf_op jit(solution)/shard_map/ppermute | solution.py:272
  75.8 4.4 %collective-permute-start.1 = (bf16[1536,256]{1,0:T(8,128)(2,1)S(1)}, bf16[1536,256]{1,0:T(8,128)(2,1)S(1)}, u32[]{:S(2)}, u32[]{:S(2)}) collective-permute-start(bf16[1536,256]{1,0:T(8,128)(2,1)S(1)} %bitcast.36), channel_id=1, source_target_pairs={{0,1},{1,0},{2,3},{3,2},{4,5},{5,4},{6,7},{7,6},{8,9},{9,8},{10,11... | collective-permute-start | bytes 2359304 | tf_op jit(solution)/shard_map/ppermute | solution.py:272
  77.7 4.3 %collective-permute-start.2 = (bf16[1536,256]{1,0:T(8,128)(2,1)S(1)}, bf16[1536,256]{1,0:T(8,128)(2,1)S(1)}, u32[]{:S(2)}, u32[]{:S(2)}) collective-permute-start(bf16[1536,256]{1,0:T(8,128)(2,1)S(1)} %bitcast.35), channel_id=1, source_target_pairs={{0,1},{1,0},{2,3},{3,2},{4,5},{5,4},{6,7},{7,6},{8,9},{9,8},{10,11... | collective-permute-start | bytes 2359304 | tf_op jit(solution)/shard_map/ppermute | solution.py:272
  104.5 3.0 %copy-start = (bf16[4,3,4,2,16,256]{5,4,3,2,1,0:T(8,128)(2,1)S(1)}, bf16[4,3,4,2,16,256]{5,4,3,2,1,0:T(8,128)(2,1)}, u32[]{:S(2)}) copy-start(bf16[4,3,4,2,16,256]{5,4,3,2,1,0:T(8,128)(2,1)} %get-tuple-element.20) | copy-start | bytes 2359300
  104.5 3.0 %copy-start.1 = (bf16[4,3,4,2,16,256]{5,4,3,2,1,0:T(8,128)(2,1)S(1)}, bf16[4,3,4,2,16,256]{5,4,3,2,1,0:T(8,128)(2,1)}, u32[]{:S(2)}) copy-start(bf16[4,3,4,2,16,256]{5,4,3,2,1,0:T(8,128)(2,1)} %get-tuple-element.21) | copy-start | bytes 2359300
  104.5 3.0 %copy-start.2 = (bf16[4,3,4,2,16,256]{5,4,3,2,1,0:T(8,128)(2,1)S(1)}, bf16[4,3,4,2,16,256]{5,4,3,2,1,0:T(8,128)(2,1)}, u32[]{:S(2)}) copy-start(bf16[4,3,4,2,16,256]{5,4,3,2,1,0:T(8,128)(2,1)} %get-tuple-element.22) | copy-start | bytes 2359300
  105.4 5.5 %copy-start.3 = (s32[128,2]{0,1:T(2,128)S(1)}, s32[128,2]{0,1:T(2,128)}, u32[]{:S(2)}) copy-start(s32[128,2]{0,1:T(2,128)} %param.12) | copy-start | bytes 3076
  105.4 5.5 %copy-start.4 = (f32[128,2]{0,1:T(2,128)S(1)}, f32[128,2]{0,1:T(2,128)}, u32[]{:S(2)}) copy-start(f32[128,2]{0,1:T(2,128)} %param.11) | copy-start | bytes 3076
  105.5 5.5 %copy-start.5 = (f32[128]{0:T(128)S(1)}, f32[128]{0:T(128)}, u32[]{:S(2)}) copy-start(f32[128]{0:T(128)} %param.10) | copy-start | bytes 1540
  105.5 5.6 %collective-permute-start.3 = (f32[320,768]{1,0:T(8,128)S(1)}, f32[320,768]{1,0:T(8,128)S(1)}, u32[]{:S(2)}, u32[]{:S(2)}) collective-permute-start(f32[320,768]{1,0:T(8,128)S(1)} %shard_map.86.a_ref), channel_id=1, source_target_pairs={{0,1},{1,0},{2,3},{3,2},{4,5},{5,4},{6,7},{7,6},{8,9},{9,8},{10,11... | collective-permute-start | bytes 2949128 | tf_op jit(solution)/shard_map/ppermute | solution.py:272
  108.5 4.6 %collective-permute-start.4 = (f32[320,768]{1,0:T(8,128)S(1)}, f32[320,768]{1,0:T(8,128)S(1)}, u32[]{:S(2)}, u32[]{:S(2)}) collective-permute-start(f32[320,768]{1,0:T(8,128)S(1)} %shard_map.85.a_ref), channel_id=1, source_target_pairs={{0,1},{1,0},{2,3},{3,2},{4,5},{5,4},{6,7},{7,6},{8,9},{9,8},{10,11... | collective-permute-start | bytes 2949128 | tf_op jit(solution)/shard_map/ppermute | solution.py:272

commit v8 on v7

--- a/solution.py
+++ b/solution.py
@@ -123,25 +123,42 @@
             out_ref[:, z] = turned.reshape(out_ref.shape[0], out_ref.shape[2], FINE, LANES)
 
 
-def order_kernel(*refs):
-    core = lax.axis_index("c")
-    srcs, own, sent, sems = refs[:3], refs[3:6], refs[6:9], refs[9]
+def gather(src, half, dst, sems, first):
     copies = []
-    for outs, c in ((own, core), (sent, 1 - core)):
-        for src, out_ref in zip(srcs, outs):
-            for yb in range(2):
-                for xb in range(2):
-                    for p in range(src.shape[5]):
-                        copies.append(
-                            pltpu.make_async_copy(
-                                src.at[:, yb, :, xb, c, p],
-                                out_ref.at[2 * yb + xb, p],
-                                sems.at[len(copies)],
-                            )
-                        )
+    for member in range(4):
+        for p in range(src.shape[5]):
+            copies.append(
+                pltpu.make_async_copy(
+                    src.at[:, member // 2, :, member % 2, half, p],
+                    dst.at[member, p],
+                    sems.at[first + len(copies)],
+                )
+            )
     for copy in copies:
         copy.start()
-    for copy in copies:
+    return copies
+
+
+def order_kernel(kept, *refs):
+    core = lax.axis_index("c")
+    sent, out_refs = len(kept[0]), len(kept[0]) + len(kept[1])
+    sources = refs[: kept[2]]
+    outs = refs[kept[2] : kept[2] + out_refs]
+    sems = refs[kept[2] + out_refs]
+    held = refs[kept[2] + out_refs + 1 :]
+    waits, each = [], 4 * sources[0].shape[5]
+    for i, k in enumerate(kept[0]):
+        waits += gather(sources[k], 1 - core, outs[i], sems, i * each)
+    own = [
+        gather(sources[k], core, held[i], sems, (sent + i) * each) for i, k in enumerate(kept[1])
+    ]
+    for i, copies in enumerate(own):
+        for copy in copies:
+            copy.wait()
+        copy = pltpu.make_async_copy(held[i], outs[sent + i], sems.at[out_refs * each + i])
+        copy.start()
+        waits.append(copy)
+    for copy in waits:
         copy.wait()
 
 
@@ -299,21 +316,31 @@
 
     views = (ny // 2, 2, nx // 2, 2, nc, parts, FINE, hidden)
     ordered = (members, parts, ny // 2, nx // 2, FINE, hidden)
-    weights = pl.pallas_call(
-        order_kernel,
-        out_shape=[pltpu.HBM(ordered, BF16)] * 3 + [jax.ShapeDtypeStruct(ordered, BF16)] * 3,
-        in_specs=[pl.BlockSpec(memory_space=pl.ANY)] * 3,
-        out_specs=[pl.BlockSpec(memory_space=m) for m in [pltpu.HBM] * 3 + [pltpu.VMEM] * 3],
-        scratch_shapes=[pltpu.SemaphoreType.DMA((2 * 3 * members * parts,))],
-        compiler_params=pltpu.CompilerParams(vmem_limit_bytes=VMEM_LIMIT),
-        cost_estimate=pl.CostEstimate(flops=0, bytes_accessed=12 * 1024 * 1024, transcendentals=0),
-    )(
-        pltpu.with_memory_space_constraint(w_gate.reshape(views), pltpu.HBM),
-        pltpu.with_memory_space_constraint(w_up.reshape(views), pltpu.HBM),
-        w_down[0].T.reshape(views),
-    )
-    weights = [w.reshape(members * wide, hidden) for w in weights]
-    own, other = weights[:3], [other_core(w) for w in weights[3:]]
+    gate, up = (
+        pltpu.with_memory_space_constraint(w.reshape(views), pltpu.HBM) for w in (w_gate, w_up)
+    )
+    down = w_down[0].T.reshape(views)
+
+    def order(sent, kept, *sources):
+        spaces = [pltpu.VMEM] * len(sent) + [pltpu.HBM] * len(kept)
+        count = len(spaces) * members * parts + len(kept)
+        ordered_weights = pl.pallas_call(
+            functools.partial(order_kernel, (sent, kept, len(sources))),
+            out_shape=[space(ordered, BF16) for space in spaces],
+            in_specs=[pl.BlockSpec(memory_space=pl.ANY)] * len(sources),
+            out_specs=[pl.BlockSpec(memory_space=space) for space in spaces],
+            scratch_shapes=[pltpu.SemaphoreType.DMA((count,))]
+            + [pltpu.VMEM(ordered, BF16)] * len(kept),
+            compiler_params=pltpu.CompilerParams(vmem_limit_bytes=VMEM_LIMIT),
+            cost_estimate=pl.CostEstimate(
+                flops=0, bytes_accessed=6 * 1024 * 1024, transcendentals=0
+            ),
+        )(*sources)
+        return [w.reshape(members * wide, hidden) for w in ordered_weights]
+
+    *sent, own_down = order((0, 1, 2), (2,), gate, up, down)
+    own = [*order((), (0, 1), gate, up), own_down]
+    other = [other_core(w) for w in sent]
     got, own, other = lax.optimization_barrier((got, own, other))
 
     copies = call(

time: 154 us -> 109 us (0.71)
  Pallas kernels: 57 us -> 12.3 us
  blocking collectives: 60.5 us -> 54.8 us
  waiting for transfers between devices: 2.94 us -> 7.88 us
    pallas_call x1 -> x2, Pallas kernels: 49.5 us -> 4.76 us  [order(): pl.pallas_call(functools.partial(order_kernel, (sent, kept, len(sources))...]
    all_to_all x1, waiting for transfers between devices: 0.01 us -> 6.46 us  [swap(): lax.all_to_all(blocks, AXES, split_axis=0, concat_axis=0, axis_index_grou...]
    all_to_all x3, blocking collectives: 60.5 us -> 54.8 us  [swap(): lax.all_to_all(blocks, AXES, split_axis=0, concat_axis=0, axis_index_grou...]
  transfers between devices with their start and end apart: 6 -> 6, of which waited for: 2 -> 2; matrix products, arithmetic and copies ran while one was open for 1% -> 2% of each run, Pallas kernels for 33% -> 6%
where the time goes in v8:
time: 109 us; the launch traced here: 108 us
  blocking collectives  54.8 us (50%)
  starting transfers between devices  31.4 us (29%)
  Pallas kernels  12.3 us (11%)
  waiting for transfers between devices  7.88 us (7%)
  local copies, waits for them, and re-layouts  1.74 us (2%)
    all_to_all x3, blocking collectives, swap(): lax.all_to_all(blocks, AXES, split_axis=0, concat_axis=0, axis_index_grou...  54.8 us
    all_to_all x1, starting transfers between devices, swap(): lax.all_to_all(blocks, AXES, split_axis=0, concat_axis=0, axis_index_grou...  19.6 us
    ppermute x5, starting transfers between devices, other_core(): return lax.ppermute(values, 'c', [(0, 1), (1, 0)])  11.8 us
    all_to_all x1, waiting for transfers between devices, swap(): lax.all_to_all(blocks, AXES, split_axis=0, concat_axis=0, axis_index_grou...  6.46 us
    pallas_call x10, Pallas kernels, call(): pl.pallas_call(kernel, out_shape=jax.ShapeDtypeStruct(shape, dtype), in_s...  5.45 us
    pallas_call x2, Pallas kernels, order(): pl.pallas_call(functools.partial(order_kernel, (sent, kept, len(sources))...  4.76 us
  transfers between devices with their start and end apart: 6, of which 2 were waited for; matrix products, arithmetic and copies ran while one was open for 2% of the time, Pallas kernels for 6%

profile of v8, /device:TPU:1, one launch (start us, length us, event | category | flops | bytes accessed | tf_op | source)
XLA Modules:
  0.0 108.3 jit_solution(6490679040775870429)
XLA Ops:
  0.0 2.1 %shard_map.82 = bf16[4,8,2,32,128]{4,3,2,1,0:T(8,128)(2,1)} custom-call(s32[2,128]{1,0:T(2,128)} %bitcast.31, bf16[48,128]{1,0:T(8,128)(2,1)} %bitcast.43, bf16[48,128]{1,0:T(8,128)(2,1)} %bitcast.44), custom_call_target="tpu_custom_call" | custom-call | tf_op jit(solution)/shard_map/pallas_call | solution.py:306
  2.1 19.6 %all-to-all-start = ((bf16[64,32,128]{2,1,0:T(8,128)(2,1)}), bf16[64,32,128]{2,1,0:T(8,128)(2,1)S(1)}, u32[]{:S(2)}, u32[]{:S(2)}) async-start(bf16[64,32,128]{2,1,0:T(8,128)(2,1)} %bitcast.3), calls=%async_computation | async-start | bytes 1048576 | tf_op jit(solution)/shard_map/all_to_all | solution.py:283
  21.7 1.7 %copy.9 = bf16[3072,256]{1,0:T(8,128)(2,1)S(1)} copy(bf16[3072,256]{0,1:T(8,128)(2,1)} %bitcast.42) | data formatting | bytes 3145728 | tf_op jit(solution)/shard_map/transpose | solution.py:322
  23.4 2.2 %shard_map.84 = (bf16[4,3,4,2,16,256]{5,4,3,2,1,0:T(8,128)(2,1)S(1)}, bf16[4,3,4,2,16,256]{5,4,3,2,1,0:T(8,128)(2,1)S(1)}, bf16[4,3,4,2,16,256]{5,4,3,2,1,0:T(8,128)(2,1)S(1)}, bf16[4,3,4,2,16,256]{5,4,3,2,1,0:T(8,128)(2,1)}) custom-call(bf16[4,2,2,2,2,3,16,256]{7,6,5,4,3,2,1,0:T(8,128)(2,1)} %bitcast.38, bf16[4,2,2,2,2,3,16,256]{7,6,5,4,3,2,1,0:T(8,128)(2,1)} %bitcast.40, ...), custom_call_target="tpu_custom_call" | custom-call | bytes 6291456 | tf_op jit(solution)/shard_map/pallas_call | solution.py:327
  25.6 2.9 %collective-permute-start = (bf16[1536,256]{1,0:T(8,128)(2,1)S(1)}, bf16[1536,256]{1,0:T(8,128)(2,1)S(1)}, u32[]{:S(2)}, u32[]{:S(2)}) collective-permute-start(bf16[1536,256]{1,0:T(8,128)(2,1)S(1)} %bitcast.37), channel_id=1, source_target_pairs={{0,1},{1,0},{2,3},{3,2},{4,5},{5,4},{6,7},{7,6},{8,9},{9,8},{10,11... | collective-permute-start | bytes 2359304 | tf_op jit(solution)/shard_map/ppermute | solution.py:289
  28.5 1.9 %collective-permute-start.1 = (bf16[1536,256]{1,0:T(8,128)(2,1)S(1)}, bf16[1536,256]{1,0:T(8,128)(2,1)S(1)}, u32[]{:S(2)}, u32[]{:S(2)}) collective-permute-start(bf16[1536,256]{1,0:T(8,128)(2,1)S(1)} %bitcast.36), channel_id=1, source_target_pairs={{0,1},{1,0},{2,3},{3,2},{4,5},{5,4},{6,7},{7,6},{8,9},{9,8},{10,11... | collective-permute-start | bytes 2359304 | tf_op jit(solution)/shard_map/ppermute | solution.py:289
  30.4 2.4 %collective-permute-start.2 = (bf16[1536,256]{1,0:T(8,128)(2,1)S(1)}, bf16[1536,256]{1,0:T(8,128)(2,1)S(1)}, u32[]{:S(2)}, u32[]{:S(2)}) collective-permute-start(bf16[1536,256]{1,0:T(8,128)(2,1)S(1)} %bitcast.35), channel_id=1, source_target_pairs={{0,1},{1,0},{2,3},{3,2},{4,5},{5,4},{6,7},{7,6},{8,9},{9,8},{10,11... | collective-permute-start | bytes 2359304 | tf_op jit(solution)/shard_map/ppermute | solution.py:289
  32.8 2.6 %shard_map.83 = (bf16[4,3,4,2,16,256]{5,4,3,2,1,0:T(8,128)(2,1)}, bf16[4,3,4,2,16,256]{5,4,3,2,1,0:T(8,128)(2,1)}) custom-call(bf16[4,2,2,2,2,3,16,256]{7,6,5,4,3,2,1,0:T(8,128)(2,1)} %bitcast.39, bf16[4,2,2,2,2,3,16,256]{7,6,5,4,3,2,1,0:T(8,128)(2,1)} %bitcast.41), custom_call_target="tpu_custom_call" | custom-call | bytes 6291456 | tf_op jit(solution)/shard_map/pallas_call | solution.py:327
  35.4 0.0 collective-permute-done.gate_ref
  35.4 0.0 collective-permute-done.1.up_ref
  35.4 0.0 collective-permute-done.2.down_ref
  35.4 6.5 %all-to-all-done = bf16[64,32,128]{2,1,0:T(8,128)(2,1)S(1)} async-done(((bf16[64,32,128]{2,1,0:T(8,128)(2,1)}), bf16[64,32,128]{2,1,0:T(8,128)(2,1)S(1)}, u32[]{:S(2)}, u32[]{:S(2)}) %all-to-all-start) | async-done | bytes 524320 | tf_op jit(solution)/shard_map/all_to_all | solution.py:283
  41.9 0.3 shard_map.85
  42.2 18.6 %all_to_all.20.in_ref = bf16[4,640,384]{2,1,0:T(8,128)(2,1)S(1)} all-to-all(bf16[4,640,384]{2,1,0:T(8,128)(2,1)S(1)} %shard_map.85), channel_id=1, replica_groups={{0,2,8,10},{4,6,12,14},{16,18,24,26},{20,22,28,30},{32,34,40,42},{36,38..., dimensions={0} | all-to-all | bytes 3932160 | tf_op jit(solution)/shard_map/all_to_all | solution.py:283
  60.8 0.0 copy-start
  60.8 0.0 copy-start.1
  60.8 0.0 copy-start.2
  60.8 0.9 shard_map.87.a_ref
  61.7 0.0 copy-start.3
  61.8 0.0 copy-start.4
  61.8 0.0 copy-start.5
  61.8 2.7 %collective-permute-start.3 = (f32[320,768]{1,0:T(8,128)S(1)}, f32[320,768]{1,0:T(8,128)S(1)}, u32[]{:S(2)}, u32[]{:S(2)}) collective-permute-start(f32[320,768]{1,0:T(8,128)S(1)} %shard_map.87.a_ref), channel_id=1, source_target_pairs={{0,1},{1,0},{2,3},{3,2},{4,5},{5,4},{6,7},{7,6},{8,9},{9,8},{10,11... | collective-permute-start | bytes 2949128 | tf_op jit(solution)/shard_map/ppermute | solution.py:289
  64.5 0.0 copy-done
  64.5 0.0 copy-done.1
  64.5 0.0 copy-done.2
  64.5 0.9 shard_map.86.a_ref
  65.4 1.9 %collective-permute-start.4 = (f32[320,768]{1,0:T(8,128)S(1)}, f32[320,768]{1,0:T(8,128)S(1)}, u32[]{:S(2)}, u32[]{:S(2)}) collective-permute-start(f32[320,768]{1,0:T(8,128)S(1)} %shard_map.86.a_ref), channel_id=1, source_target_pairs={{0,1},{1,0},{2,3},{3,2},{4,5},{5,4},{6,7},{7,6},{8,9},{9,8},{10,11... | collective-permute-start | bytes 2949128 | tf_op jit(solution)/shard_map/ppermute | solution.py:289
  67.4 0.0 copy-done.3
  67.4 0.0 copy-done.4
  67.4 0.0 copy-done.5
  67.4 0.2 shard_map.90.combine_ref
  67.6 0.0 collective-permute-done.3.b_ref
  67.6 0.2 shard_map.88.d_ref
  67.8 0.7 shard_map.89.sum_ref
  68.5 1.4 %collective-permute-done.4.b_ref = f32[320,768]{1,0:T(8,128)S(1)} collective-permute-done((f32[320,768]{1,0:T(8,128)S(1)}, f32[320,768]{1,0:T(8,128)S(1)}, u32[]{:S(2)}, u32[]{:S(2)}) %collective-permute-start.4) | collective-permute-done | bytes 983072 | tf_op jit(solution)/shard_map/ppermute | solution.py:289
  69.9 0.2 shard_map.91.d_ref
  70.1 0.9 shard_map.92
  70.9 13.4 %all_to_all.21.in_ref = bf16[4,320,384]{2,1,0:T(8,128)(2,1)S(1)} all-to-all(bf16[4,320,384]{2,1,0:T(8,128)(2,1)S(1)} %shard_map.92), channel_id=1, replica_groups={{0,2,8,10},{4,6,12,14},{16,18,24,26},{20,22,28,30},{32,34,40,42},{36,38..., dimensions={0} | all-to-all | bytes 1966080 | tf_op jit(solution)/shard_map/all_to_all | solution.py:283
  84.4 0.2 shard_map.93
  84.6 22.8 %all_to_all.22 = bf16[64,16,128]{2,1,0:T(8,128)(2,1)S(1)} all-to-all(bf16[64,16,128]{2,1,0:T(8,128)(2,1)S(1)} %bitcast.29), channel_id=1, replica_groups={{0,4,64,68,128,132,192,196,256,260,320,324,384,388,448,452,16,20,80,84,..., dimensions={0} | all-to-all | bytes 524288 | tf_op jit(solution)/shard_map/all_to_all | solution.py:283
  107.3 1.0 shard_map.94
Async XLA Ops:
  2.1 39.8 %all-to-all-start = ((bf16[64,32,128]{2,1,0:T(8,128)(2,1)}), bf16[64,32,128]{2,1,0:T(8,128)(2,1)S(1)}, u32[]{:S(2)}, u32[]{:S(2)}) async-start(bf16[64,32,128]{2,1,0:T(8,128)(2,1)} %bitcast.3), calls=%async_computation | async-start | bytes 1048576 | tf_op jit(solution)/shard_map/all_to_all | solution.py:283
  25.6 9.8 %collective-permute-start = (bf16[1536,256]{1,0:T(8,128)(2,1)S(1)}, bf16[1536,256]{1,0:T(8,128)(2,1)S(1)}, u32[]{:S(2)}, u32[]{:S(2)}) collective-permute-start(bf16[1536,256]{1,0:T(8,128)(2,1)S(1)} %bitcast.37), channel_id=1, source_target_pairs={{0,1},{1,0},{2,3},{3,2},{4,5},{5,4},{6,7},{7,6},{8,9},{9,8},{10,11... | collective-permute-start | bytes 2359304 | tf_op jit(solution)/shard_map/ppermute | solution.py:289
  28.5 7.0 %collective-permute-start.1 = (bf16[1536,256]{1,0:T(8,128)(2,1)S(1)}, bf16[1536,256]{1,0:T(8,128)(2,1)S(1)}, u32[]{:S(2)}, u32[]{:S(2)}) collective-permute-start(bf16[1536,256]{1,0:T(8,128)(2,1)S(1)} %bitcast.36), channel_id=1, source_target_pairs={{0,1},{1,0},{2,3},{3,2},{4,5},{5,4},{6,7},{7,6},{8,9},{9,8},{10,11... | collective-permute-start | bytes 2359304 | tf_op jit(solution)/shard_map/ppermute | solution.py:289
  30.4 5.0 %collective-permute-start.2 = (bf16[1536,256]{1,0:T(8,128)(2,1)S(1)}, bf16[1536,256]{1,0:T(8,128)(2,1)S(1)}, u32[]{:S(2)}, u32[]{:S(2)}) collective-permute-start(bf16[1536,256]{1,0:T(8,128)(2,1)S(1)} %bitcast.35), channel_id=1, source_target_pairs={{0,1},{1,0},{2,3},{3,2},{4,5},{5,4},{6,7},{7,6},{8,9},{9,8},{10,11... | collective-permute-start | bytes 2359304 | tf_op jit(solution)/shard_map/ppermute | solution.py:289
  60.8 3.7 %copy-start = (bf16[4,3,4,2,16,256]{5,4,3,2,1,0:T(8,128)(2,1)S(1)}, bf16[4,3,4,2,16,256]{5,4,3,2,1,0:T(8,128)(2,1)}, u32[]{:S(2)}) copy-start(bf16[4,3,4,2,16,256]{5,4,3,2,1,0:T(8,128)(2,1)} %get-tuple-element.20) | copy-start | bytes 2359300
  60.8 3.7 %copy-start.1 = (bf16[4,3,4,2,16,256]{5,4,3,2,1,0:T(8,128)(2,1)S(1)}, bf16[4,3,4,2,16,256]{5,4,3,2,1,0:T(8,128)(2,1)}, u32[]{:S(2)}) copy-start(bf16[4,3,4,2,16,256]{5,4,3,2,1,0:T(8,128)(2,1)} %get-tuple-element.21) | copy-start | bytes 2359300
  60.8 3.7 %copy-start.2 = (bf16[4,3,4,2,16,256]{5,4,3,2,1,0:T(8,128)(2,1)S(1)}, bf16[4,3,4,2,16,256]{5,4,3,2,1,0:T(8,128)(2,1)}, u32[]{:S(2)}) copy-start(bf16[4,3,4,2,16,256]{5,4,3,2,1,0:T(8,128)(2,1)} %get-tuple-element.22) | copy-start | bytes 2359300
  61.7 5.6 %copy-start.3 = (s32[128,2]{0,1:T(2,128)S(1)}, s32[128,2]{0,1:T(2,128)}, u32[]{:S(2)}) copy-start(s32[128,2]{0,1:T(2,128)} %param.12) | copy-start | bytes 3076
  61.8 5.6 %copy-start.4 = (f32[128,2]{0,1:T(2,128)S(1)}, f32[128,2]{0,1:T(2,128)}, u32[]{:S(2)}) copy-start(f32[128,2]{0,1:T(2,128)} %param.11) | copy-start | bytes 3076
  61.8 5.6 %copy-start.5 = (f32[128]{0:T(128)S(1)}, f32[128]{0:T(128)}, u32[]{:S(2)}) copy-start(f32[128]{0:T(128)} %param.10) | copy-start | bytes 1540
  61.8 5.8 %collective-permute-start.3 = (f32[320,768]{1,0:T(8,128)S(1)}, f32[320,768]{1,0:T(8,128)S(1)}, u32[]{:S(2)}, u32[]{:S(2)}) collective-permute-start(f32[320,768]{1,0:T(8,128)S(1)} %shard_map.87.a_ref), channel_id=1, source_target_pairs={{0,1},{1,0},{2,3},{3,2},{4,5},{5,4},{6,7},{7,6},{8,9},{9,8},{10,11... | collective-permute-start | bytes 2949128 | tf_op jit(solution)/shard_map/ppermute | solution.py:289
  65.4 4.5 %collective-permute-start.4 = (f32[320,768]{1,0:T(8,128)S(1)}, f32[320,768]{1,0:T(8,128)S(1)}, u32[]{:S(2)}, u32[]{:S(2)}) collective-permute-start(f32[320,768]{1,0:T(8,128)S(1)} %shard_map.86.a_ref), channel_id=1, source_target_pairs={{0,1},{1,0},{2,3},{3,2},{4,5},{5,4},{6,7},{7,6},{8,9},{9,8},{10,11... | collective-permute-start | bytes 2949128 | tf_op jit(solution)/shard_map/ppermute | solution.py:289

commit v9 on v8

--- a/solution.py
+++ b/solution.py
@@ -48,14 +48,14 @@
     return jnp.where(hit, before, -2.0), first
 
 
-def pack_kernel(capacity, ids_hbm, x_hbm, g_hbm, out_ref, ids_ref, x_ref, g_ref, sems):
+def pack_kernel(capacity, ids_hbm, x_hbm, g_hbm, out_hbm, ids_ref, x_ref, g_ref, held, sems):
     copies = [
         pltpu.make_async_copy(src, dst, sems.at[i])
         for i, (src, dst) in enumerate(((ids_hbm, ids_ref), (x_hbm, x_ref), (g_hbm, g_ref)))
     ]
     for copy in copies:
         copy.start()
-    nya, nz, nxa = out_ref.shape[:3]
+    nya, nz, nxa = out_hbm.shape[:3]
     feats, tokens = x_ref.shape
     parts = feats // FINE
     lanes = nz * LANES
@@ -79,11 +79,19 @@
         for p in range(parts):
             block = jnp.where(part == p, spread[p * FINE : (p + 1) * FINE], block)
         block = block.astype(BF16)
+        here = pl.ds(kind * FINE, FINE)
         for z in range(nz):
-            piece = block[:, z * LANES : (z + 1) * LANES]
-            for ya in range(nya):
-                for xa in range(nxa):
-                    out_ref[ya, z, xa, kind * FINE : (kind + 1) * FINE, :] = piece
+            held[z, kind * FINE : (kind + 1) * FINE, :] = block[:, z * LANES : (z + 1) * LANES]
+        for ya in range(nya):
+            for xa in range(nxa):
+                copies.append(
+                    pltpu.make_async_copy(
+                        held.at[:, here], out_hbm.at[ya, :, xa, here], sems.at[len(copies)]
+                    )
+                )
+                copies[-1].start()
+    for copy in copies[3:]:
+        copy.wait()
 
 
 def unpack_kernel(capacity, parts, in_ref, out_ref):
@@ -173,55 +181,49 @@
     out_ref[:, 2 * hidden :] = jnp.dot(g, down_ref[...], preferred_element_type=F32)
 
 
-def tail_kernel(a_ref, b_ref, out_ref):
-    hidden = a_ref.shape[1] // 3
+def return_part(a_ref, b_ref, gate_ref, up_ref):
+    hidden = gate_ref.shape[1]
     gate, upper, back = (
         a_ref[:, k * hidden : (k + 1) * hidden] + b_ref[:, k * hidden : (k + 1) * hidden]
         for k in range(3)
     )
     d_gate, d_upper = backward_tail(gate, upper, back)
-    out_ref[:, :hidden] = d_gate
-    out_ref[:, hidden:] = d_upper
-
-
-def return_part(d_ref, gate_ref, up_ref, here):
-    hidden = gate_ref.shape[1]
     across = (((1,), (1,)), ((), ()))
-    part = lax.dot_general(
-        d_ref[:, :hidden], gate_ref[here, :], across, preferred_element_type=F32
-    )
-    return part + lax.dot_general(
-        d_ref[:, hidden:], up_ref[here, :], across, preferred_element_type=F32
-    )
-
-
-def return_kernel(d_ref, gate_ref, up_ref, out_ref):
-    out_ref[...] = return_part(d_ref, gate_ref, up_ref, slice(None))
-
-
-def return_add_kernel(d_ref, gate_ref, up_ref, sum_ref, out_ref):
+    part = lax.dot_general(d_gate, gate_ref[...], across, preferred_element_type=F32)
+    return part + lax.dot_general(d_upper, up_ref[...], across, preferred_element_type=F32)
+
+
+def return_kernel(a_ref, b_ref, gate_ref, up_ref, out_ref):
+    out_ref[...] = return_part(a_ref, b_ref, gate_ref, up_ref)
+
+
+def return_add_kernel(a_ref, b_ref, gate_ref, up_ref, sum_ref, out_ref):
     members, _, wide = out_ref.shape
+    part = (return_part(a_ref, b_ref, gate_ref, up_ref) + sum_ref[...]).astype(out_ref.dtype)
     for i in range(members):
-        here = slice(i * wide, (i + 1) * wide)
-        part = return_part(d_ref, gate_ref, up_ref, here)
-        out_ref[i] = (part + sum_ref[:, here]).astype(out_ref.dtype)
+        out_ref[i] = part[:, i * wide : (i + 1) * wide]
+
+
+def two_parts(values):
+    high = values.astype(BF16)
+    return high, (values - high.astype(F32)).astype(BF16)
 
 
 def combine_kernel(capacity, parts, ids_ref, prob_ref, scale_ref, out_ref):
-    lanes, tokens = out_ref.shape
+    _, lanes, tokens = out_ref.shape
     experts = lanes // LANES
     slots, first = token_slots(ids_ref[...].astype(F32), experts)
     weights = jnp.where(first, prob_ref[0:1, :], prob_ref[1:2, :]) * scale_ref[...]
     slot_of_lane = lane_slots(tokens, capacity, parts)
     for z in range(experts):
-        out_ref[z * LANES : (z + 1) * LANES, :] = jnp.where(
-            slots[z : z + 1] == slot_of_lane, weights[z : z + 1], 0.0
-        )
+        here = slice(z * LANES, (z + 1) * LANES)
+        weight = jnp.where(slots[z : z + 1] == slot_of_lane, weights[z : z + 1], 0.0)
+        out_ref[0, here, :], out_ref[1, here, :] = two_parts(weight)
 
 
 def final_kernel(capacity, parts, combine_ref, in_ref, out_ref):
-    lanes = combine_ref.shape[0]
-    nz = lanes // LANES
+    nz = combine_ref.shape[1] // LANES
+    feats = out_ref.shape[0]
     sums = []
     for z in range(nz):
         total = jnp.zeros((FINE, LANES), F32)
@@ -232,13 +234,12 @@
     sums = jnp.concatenate(sums, axis=1)
     part = lane_parts(sums.shape, 1, capacity)
     spread = jnp.concatenate([jnp.where(part == p, sums, 0.0) for p in range(parts)], axis=0)
-    out_ref[...] = lax.dot_general(
-        spread,
-        combine_ref[...],
-        (((1,), (0,)), ((), ())),
-        precision=lax.Precision.HIGHEST,
-        preferred_element_type=F32,
-    ).astype(out_ref.dtype)
+    high, low = two_parts(spread)
+    first = jnp.dot(
+        jnp.concatenate([high, low], axis=0), combine_ref[0], preferred_element_type=F32
+    )
+    second = jnp.dot(high, combine_ref[1], preferred_element_type=F32)
+    out_ref[...] = (first[:feats] + first[feats:] + second).astype(out_ref.dtype)
 
 
 def call(kernel, shape, dtype, *operands, flops=0):
@@ -305,11 +306,11 @@
     heads = [route_ids.T, activations.T, out_grad.T]
     send = pl.pallas_call(
         functools.partial(pack_kernel, capacity),
-        out_shape=jax.ShapeDtypeStruct((ny // 2, nz, nx // 2, 2 * FINE, LANES), BF16),
+        out_shape=pltpu.HBM((ny // 2, nz, nx // 2, 2 * FINE, LANES), BF16),
         in_specs=[pl.BlockSpec(memory_space=pl.ANY)] * 3,
-        out_specs=pl.BlockSpec(memory_space=pltpu.VMEM),
+        out_specs=pl.BlockSpec(memory_space=pltpu.HBM),
         scratch_shapes=[pltpu.VMEM(h.shape, h.dtype) for h in heads]
-        + [pltpu.SemaphoreType.DMA((3,))],
+        + [pltpu.VMEM((nz, 2 * FINE, LANES), BF16), pltpu.SemaphoreType.DMA((3 + 2 * spread,))],
         compiler_params=pltpu.CompilerParams(vmem_limit_bytes=VMEM_LIMIT),
     )(*(pltpu.with_memory_space_constraint(h, pltpu.HBM) for h in heads))
     got = swap(send.reshape(nz * spread, 2 * FINE, LANES), far)
@@ -356,28 +357,32 @@
     def project(w):
         return call(project_kernel, (rows, 3 * hidden), F32, block, *w, flops=flops)
 
-    def tail(a, b):
-        return call(tail_kernel, (rows, 2 * hidden), BF16, a, b)
-
     part_other = project(other)
     rest_own = other_core(part_other)
     part_own = project(own)
     rest_other = other_core(part_own)
-    d_own = tail(part_own, rest_own)
     flops = flops // 3 * 2
-    part = call(return_kernel, (rows, members * wide), F32, d_own, *own[:2], flops=flops)
+    part = call(
+        return_kernel, (rows, members * wide), F32, part_own, rest_own, *own[:2], flops=flops
+    )
     combine = call(
         functools.partial(combine_kernel, capacity, parts),
-        (nz * LANES, tokens),
-        F32,
+        (2, nz * LANES, tokens),
+        BF16,
         route_ids.T,
         route_prob.T,
         token_scale.reshape(1, tokens),
     )
     part, combine = lax.optimization_barrier((part, combine))
-    d_other = tail(part_other, rest_other)
     part = call(
-        return_add_kernel, (members, rows, wide), BF16, d_other, *other[:2], part, flops=flops
+        return_add_kernel,
+        (members, rows, wide),
+        BF16,
+        part_other,
+        rest_other,
+        *other[:2],
+        part,
+        flops=flops,
     )
     part = swap(part, near)
     part = call(

time: 109 us -> 109 us (level)
    pallas_call x10 -> x8, Pallas kernels: 5.45 us -> 4.92 us  [call(): pl.pallas_call(kernel, out_shape=jax.ShapeDtypeStruct(shape, dtype), in_s...]
where the time goes in v9:
time: 109 us; the launch traced here: 108 us
  blocking collectives  54.8 us (50%)
  starting transfers between devices  31.4 us (29%)
  Pallas kernels  11.8 us (11%)
  waiting for transfers between devices  8.02 us (7%)
  local copies, waits for them, and re-layouts  1.74 us (2%)
    all_to_all x3, blocking collectives, swap(): lax.all_to_all(blocks, AXES, split_axis=0, concat_axis=0, axis_index_grou...  54.8 us
    all_to_all x1, starting transfers between devices, swap(): lax.all_to_all(blocks, AXES, split_axis=0, concat_axis=0, axis_index_grou...  19.6 us
    ppermute x5, starting transfers between devices, other_core(): return lax.ppermute(values, 'c', [(0, 1), (1, 0)])  11.8 us
    all_to_all x1, waiting for transfers between devices, swap(): lax.all_to_all(blocks, AXES, split_axis=0, concat_axis=0, axis_index_grou...  6.47 us
    pallas_call x8, Pallas kernels, call(): pl.pallas_call(kernel, out_shape=jax.ShapeDtypeStruct(shape, dtype), in_s...  4.92 us
    pallas_call x2, Pallas kernels, order(): pl.pallas_call(functools.partial(order_kernel, (sent, kept, len(sources))...  4.76 us
  transfers between devices with their start and end apart: 6, of which 2 were waited for; matrix products, arithmetic and copies ran while one was open for 2% of the time, Pallas kernels for 6%

profile of v9, /device:TPU:1, one launch (start us, length us, event | category | flops | bytes accessed | tf_op | source)
XLA Modules:
  0.0 108.0 jit_solution(11071768577402345634)
XLA Ops:
  0.0 2.1 %shard_map.82 = bf16[4,8,2,32,128]{4,3,2,1,0:T(8,128)(2,1)} custom-call(s32[2,128]{1,0:T(2,128)} %bitcast.31, bf16[48,128]{1,0:T(8,128)(2,1)} %bitcast.44, bf16[48,128]{1,0:T(8,128)(2,1)} %bitcast.45), custom_call_target="tpu_custom_call" | custom-call | tf_op jit(solution)/shard_map/pallas_call | solution.py:307
  2.1 19.6 %all-to-all-start = ((bf16[64,32,128]{2,1,0:T(8,128)(2,1)}), bf16[64,32,128]{2,1,0:T(8,128)(2,1)S(1)}, u32[]{:S(2)}, u32[]{:S(2)}) async-start(bf16[64,32,128]{2,1,0:T(8,128)(2,1)} %bitcast.42), calls=%async_computation | async-start | bytes 1048576 | tf_op jit(solution)/shard_map/all_to_all | solution.py:284
  21.7 1.7 %copy.9 = bf16[3072,256]{1,0:T(8,128)(2,1)S(1)} copy(bf16[3072,256]{0,1:T(8,128)(2,1)} %bitcast.43) | data formatting | bytes 3145728 | tf_op jit(solution)/shard_map/transpose | solution.py:323
  23.5 2.2 %shard_map.84 = (bf16[4,3,4,2,16,256]{5,4,3,2,1,0:T(8,128)(2,1)S(1)}, bf16[4,3,4,2,16,256]{5,4,3,2,1,0:T(8,128)(2,1)S(1)}, bf16[4,3,4,2,16,256]{5,4,3,2,1,0:T(8,128)(2,1)S(1)}, bf16[4,3,4,2,16,256]{5,4,3,2,1,0:T(8,128)(2,1)}) custom-call(bf16[4,2,2,2,2,3,16,256]{7,6,5,4,3,2,1,0:T(8,128)(2,1)} %bitcast.38, bf16[4,2,2,2,2,3,16,256]{7,6,5,4,3,2,1,0:T(8,128)(2,1)} %bitcast.40, ...), custom_call_target="tpu_custom_call" | custom-call | bytes 6291456 | tf_op jit(solution)/shard_map/pallas_call | solution.py:328
  25.6 2.9 %collective-permute-start = (bf16[1536,256]{1,0:T(8,128)(2,1)S(1)}, bf16[1536,256]{1,0:T(8,128)(2,1)S(1)}, u32[]{:S(2)}, u32[]{:S(2)}) collective-permute-start(bf16[1536,256]{1,0:T(8,128)(2,1)S(1)} %bitcast.37), channel_id=1, source_target_pairs={{0,1},{1,0},{2,3},{3,2},{4,5},{5,4},{6,7},{7,6},{8,9},{9,8},{10,11... | collective-permute-start | bytes 2359304 | tf_op jit(solution)/shard_map/ppermute | solution.py:290
  28.5 1.9 %collective-permute-start.1 = (bf16[1536,256]{1,0:T(8,128)(2,1)S(1)}, bf16[1536,256]{1,0:T(8,128)(2,1)S(1)}, u32[]{:S(2)}, u32[]{:S(2)}) collective-permute-start(bf16[1536,256]{1,0:T(8,128)(2,1)S(1)} %bitcast.36), channel_id=1, source_target_pairs={{0,1},{1,0},{2,3},{3,2},{4,5},{5,4},{6,7},{7,6},{8,9},{9,8},{10,11... | collective-permute-start | bytes 2359304 | tf_op jit(solution)/shard_map/ppermute | solution.py:290
  30.4 2.4 %collective-permute-start.2 = (bf16[1536,256]{1,0:T(8,128)(2,1)S(1)}, bf16[1536,256]{1,0:T(8,128)(2,1)S(1)}, u32[]{:S(2)}, u32[]{:S(2)}) collective-permute-start(bf16[1536,256]{1,0:T(8,128)(2,1)S(1)} %bitcast.35), channel_id=1, source_target_pairs={{0,1},{1,0},{2,3},{3,2},{4,5},{5,4},{6,7},{7,6},{8,9},{9,8},{10,11... | collective-permute-start | bytes 2359304 | tf_op jit(solution)/shard_map/ppermute | solution.py:290
  32.9 2.6 %shard_map.83 = (bf16[4,3,4,2,16,256]{5,4,3,2,1,0:T(8,128)(2,1)}, bf16[4,3,4,2,16,256]{5,4,3,2,1,0:T(8,128)(2,1)}) custom-call(bf16[4,2,2,2,2,3,16,256]{7,6,5,4,3,2,1,0:T(8,128)(2,1)} %bitcast.39, bf16[4,2,2,2,2,3,16,256]{7,6,5,4,3,2,1,0:T(8,128)(2,1)} %bitcast.41), custom_call_target="tpu_custom_call" | custom-call | bytes 6291456 | tf_op jit(solution)/shard_map/pallas_call | solution.py:328
  35.5 0.0 collective-permute-done.gate_ref
  35.5 0.0 collective-permute-done.1.up_ref
  35.5 0.0 collective-permute-done.2.down_ref
  35.5 6.5 %all-to-all-done = bf16[64,32,128]{2,1,0:T(8,128)(2,1)S(1)} async-done(((bf16[64,32,128]{2,1,0:T(8,128)(2,1)}), bf16[64,32,128]{2,1,0:T(8,128)(2,1)S(1)}, u32[]{:S(2)}, u32[]{:S(2)}) %all-to-all-start) | async-done | bytes 524320 | tf_op jit(solution)/shard_map/all_to_all | solution.py:284
  42.0 0.3 shard_map.85
  42.3 18.6 %all_to_all.20.in_ref = bf16[4,640,384]{2,1,0:T(8,128)(2,1)S(1)} all-to-all(bf16[4,640,384]{2,1,0:T(8,128)(2,1)S(1)} %shard_map.85), channel_id=1, replica_groups={{0,2,8,10},{4,6,12,14},{16,18,24,26},{20,22,28,30},{32,34,40,42},{36,38..., dimensions={0} | all-to-all | bytes 3932160 | tf_op jit(solution)/shard_map/all_to_all | solution.py:284
  60.9 0.0 copy-start
  60.9 0.0 copy-start.1
  60.9 0.0 copy-start.2
  60.9 0.9 shard_map.87.a_ref
  61.8 0.0 copy-start.3
  61.8 0.0 copy-start.4
  61.8 0.0 copy-start.5
  61.8 2.7 %collective-permute-start.3 = (f32[320,768]{1,0:T(8,128)S(1)}, f32[320,768]{1,0:T(8,128)S(1)}, u32[]{:S(2)}, u32[]{:S(2)}) collective-permute-start(f32[320,768]{1,0:T(8,128)S(1)} %shard_map.87.a_ref), channel_id=1, source_target_pairs={{0,1},{1,0},{2,3},{3,2},{4,5},{5,4},{6,7},{7,6},{8,9},{9,8},{10,11... | collective-permute-start | bytes 2949128 | tf_op jit(solution)/shard_map/ppermute | solution.py:290
  64.5 0.0 copy-done
  64.5 0.0 copy-done.1
  64.5 0.0 copy-done.2
  64.5 0.9 shard_map.86.a_ref
  65.5 1.9 %collective-permute-start.4 = (f32[320,768]{1,0:T(8,128)S(1)}, f32[320,768]{1,0:T(8,128)S(1)}, u32[]{:S(2)}, u32[]{:S(2)}) collective-permute-start(f32[320,768]{1,0:T(8,128)S(1)} %shard_map.86.a_ref), channel_id=1, source_target_pairs={{0,1},{1,0},{2,3},{3,2},{4,5},{5,4},{6,7},{7,6},{8,9},{9,8},{10,11... | collective-permute-start | bytes 2949128 | tf_op jit(solution)/shard_map/ppermute | solution.py:290
  67.4 0.0 copy-done.3
  67.4 0.0 copy-done.4
  67.4 0.0 copy-done.5
  67.4 0.2 shard_map.89.combine_ref
  67.7 0.0 collective-permute-done.3.b_ref
  67.7 0.7 shard_map.88.sum_ref
  68.4 1.5 %collective-permute-done.4.b_ref = f32[320,768]{1,0:T(8,128)S(1)} collective-permute-done((f32[320,768]{1,0:T(8,128)S(1)}, f32[320,768]{1,0:T(8,128)S(1)}, u32[]{:S(2)}, u32[]{:S(2)}) %collective-permute-start.4) | collective-permute-done | bytes 983072 | tf_op jit(solution)/shard_map/ppermute | solution.py:290
  69.9 0.8 shard_map.90
  70.7 13.4 %all_to_all.21.in_ref = bf16[4,320,384]{2,1,0:T(8,128)(2,1)S(1)} all-to-all(bf16[4,320,384]{2,1,0:T(8,128)(2,1)S(1)} %shard_map.90), channel_id=1, replica_groups={{0,2,8,10},{4,6,12,14},{16,18,24,26},{20,22,28,30},{32,34,40,42},{36,38..., dimensions={0} | all-to-all | bytes 1966080 | tf_op jit(solution)/shard_map/all_to_all | solution.py:284
  84.1 0.2 shard_map.91
  84.3 22.8 %all_to_all.22 = bf16[64,16,128]{2,1,0:T(8,128)(2,1)S(1)} all-to-all(bf16[64,16,128]{2,1,0:T(8,128)(2,1)S(1)} %bitcast.29), channel_id=1, replica_groups={{0,4,64,68,128,132,192,196,256,260,320,324,384,388,448,452,16,20,80,84,..., dimensions={0} | all-to-all | bytes 524288 | tf_op jit(solution)/shard_map/all_to_all | solution.py:284
  107.1 0.9 shard_map.92
Async XLA Ops:
  2.1 39.8 %all-to-all-start = ((bf16[64,32,128]{2,1,0:T(8,128)(2,1)}), bf16[64,32,128]{2,1,0:T(8,128)(2,1)S(1)}, u32[]{:S(2)}, u32[]{:S(2)}) async-start(bf16[64,32,128]{2,1,0:T(8,128)(2,1)} %bitcast.42), calls=%async_computation | async-start | bytes 1048576 | tf_op jit(solution)/shard_map/all_to_all | solution.py:284
  25.6 9.8 %collective-permute-start = (bf16[1536,256]{1,0:T(8,128)(2,1)S(1)}, bf16[1536,256]{1,0:T(8,128)(2,1)S(1)}, u32[]{:S(2)}, u32[]{:S(2)}) collective-permute-start(bf16[1536,256]{1,0:T(8,128)(2,1)S(1)} %bitcast.37), channel_id=1, source_target_pairs={{0,1},{1,0},{2,3},{3,2},{4,5},{5,4},{6,7},{7,6},{8,9},{9,8},{10,11... | collective-permute-start | bytes 2359304 | tf_op jit(solution)/shard_map/ppermute | solution.py:290
  28.5 7.0 %collective-permute-start.1 = (bf16[1536,256]{1,0:T(8,128)(2,1)S(1)}, bf16[1536,256]{1,0:T(8,128)(2,1)S(1)}, u32[]{:S(2)}, u32[]{:S(2)}) collective-permute-start(bf16[1536,256]{1,0:T(8,128)(2,1)S(1)} %bitcast.36), channel_id=1, source_target_pairs={{0,1},{1,0},{2,3},{3,2},{4,5},{5,4},{6,7},{7,6},{8,9},{9,8},{10,11... | collective-permute-start | bytes 2359304 | tf_op jit(solution)/shard_map/ppermute | solution.py:290
  30.4 5.0 %collective-permute-start.2 = (bf16[1536,256]{1,0:T(8,128)(2,1)S(1)}, bf16[1536,256]{1,0:T(8,128)(2,1)S(1)}, u32[]{:S(2)}, u32[]{:S(2)}) collective-permute-start(bf16[1536,256]{1,0:T(8,128)(2,1)S(1)} %bitcast.35), channel_id=1, source_target_pairs={{0,1},{1,0},{2,3},{3,2},{4,5},{5,4},{6,7},{7,6},{8,9},{9,8},{10,11... | collective-permute-start | bytes 2359304 | tf_op jit(solution)/shard_map/ppermute | solution.py:290
  60.9 3.6 %copy-start = (bf16[4,3,4,2,16,256]{5,4,3,2,1,0:T(8,128)(2,1)S(1)}, bf16[4,3,4,2,16,256]{5,4,3,2,1,0:T(8,128)(2,1)}, u32[]{:S(2)}) copy-start(bf16[4,3,4,2,16,256]{5,4,3,2,1,0:T(8,128)(2,1)} %get-tuple-element.20) | copy-start | bytes 2359300
  60.9 3.7 %copy-start.1 = (bf16[4,3,4,2,16,256]{5,4,3,2,1,0:T(8,128)(2,1)S(1)}, bf16[4,3,4,2,16,256]{5,4,3,2,1,0:T(8,128)(2,1)}, u32[]{:S(2)}) copy-start(bf16[4,3,4,2,16,256]{5,4,3,2,1,0:T(8,128)(2,1)} %get-tuple-element.21) | copy-start | bytes 2359300
  60.9 3.7 %copy-start.2 = (bf16[4,3,4,2,16,256]{5,4,3,2,1,0:T(8,128)(2,1)S(1)}, bf16[4,3,4,2,16,256]{5,4,3,2,1,0:T(8,128)(2,1)}, u32[]{:S(2)}) copy-start(bf16[4,3,4,2,16,256]{5,4,3,2,1,0:T(8,128)(2,1)} %get-tuple-element.22) | copy-start | bytes 2359300
  61.8 5.6 %copy-start.3 = (s32[128,2]{0,1:T(2,128)S(1)}, s32[128,2]{0,1:T(2,128)}, u32[]{:S(2)}) copy-start(s32[128,2]{0,1:T(2,128)} %param.12) | copy-start | bytes 3076
  61.8 5.6 %copy-start.4 = (f32[128,2]{0,1:T(2,128)S(1)}, f32[128,2]{0,1:T(2,128)}, u32[]{:S(2)}) copy-start(f32[128,2]{0,1:T(2,128)} %param.11) | copy-start | bytes 3076
  61.8 5.6 %copy-start.5 = (f32[128]{0:T(128)S(1)}, f32[128]{0:T(128)}, u32[]{:S(2)}) copy-start(f32[128]{0:T(128)} %param.10) | copy-start | bytes 1540
  61.8 5.8 %collective-permute-start.3 = (f32[320,768]{1,0:T(8,128)S(1)}, f32[320,768]{1,0:T(8,128)S(1)}, u32[]{:S(2)}, u32[]{:S(2)}) collective-permute-start(f32[320,768]{1,0:T(8,128)S(1)} %shard_map.87.a_ref), channel_id=1, source_target_pairs={{0,1},{1,0},{2,3},{3,2},{4,5},{5,4},{6,7},{7,6},{8,9},{9,8},{10,11... | collective-permute-start | bytes 2949128 | tf_op jit(solution)/shard_map/ppermute | solution.py:290
  65.5 4.5 %collective-permute-start.4 = (f32[320,768]{1,0:T(8,128)S(1)}, f32[320,768]{1,0:T(8,128)S(1)}, u32[]{:S(2)}, u32[]{:S(2)}) collective-permute-start(f32[320,768]{1,0:T(8,128)S(1)} %shard_map.86.a_ref), channel_id=1, source_target_pairs={{0,1},{1,0},{2,3},{3,2},{4,5},{5,4},{6,7},{7,6},{8,9},{9,8},{10,11... | collective-permute-start | bytes 2949128 | tf_op jit(solution)/shard_map/ppermute | solution.py:290

commit v10 on v9

--- a/solution.py
+++ b/solution.py
@@ -132,16 +132,22 @@
 
 
 def gather(src, half, dst, sems, first):
+    pieces = (
+        (0, pl.ds(0, 1), pl.ds(0, 1)),
+        (0, pl.ds(1, 1), pl.ds(3 - 2 * half, 1)),
+        (1, pl.ds(0, 2), pl.ds(1 + half, 2)),
+    )
     copies = []
-    for member in range(4):
-        for p in range(src.shape[5]):
-            copies.append(
-                pltpu.make_async_copy(
-                    src.at[:, member // 2, :, member % 2, half, p],
-                    dst.at[member, p],
-                    sems.at[first + len(copies)],
+    for yb in range(2):
+        for column, there, here in pieces:
+            for p in range(src.shape[4]):
+                copies.append(
+                    pltpu.make_async_copy(
+                        src.at[:, yb, here, half, p],
+                        dst.at[2 * yb + column, p, :, there],
+                        sems.at[first + len(copies)],
+                    )
                 )
-            )
     for copy in copies:
         copy.start()
     return copies
@@ -154,7 +160,7 @@
     outs = refs[kept[2] : kept[2] + out_refs]
     sems = refs[kept[2] + out_refs]
     held = refs[kept[2] + out_refs + 1 :]
-    waits, each = [], 4 * sources[0].shape[5]
+    waits, each = [], 6 * sources[0].shape[4]
     for i, k in enumerate(kept[0]):
         waits += gather(sources[k], 1 - core, outs[i], sems, i * each)
     own = [
@@ -255,27 +261,33 @@
     )(*operands)
 
 
+def columns(half, nx):
+    return (
+        [x for a in range(0, nx, 4) for x in (a, a + 3 - 2 * half)],
+        [x for a in range(0, nx, 4) for x in (a + 1 + half, a + 2 + half)],
+    )
+
+
 def exchange_groups(nz, ny, nx, nc):
     def index(z, y, x, c):
         return ((z * ny + y % ny) * nx + x % nx) * nc + c
 
-    halves = [(yb, xb) for yb in range(2) for xb in range(2)]
-    places = [(2 * ya, 2 * xa) for ya in range(ny // 2) for xa in range(nx // 2)]
     far = [
-        [
-            index(z, 2 * ya + yb, 2 * xa + xb, c)
-            for ya in range(ny // 2)
-            for z in range(nz)
-            for xa in range(nx // 2)
-        ]
+        [index(z, y, x, c) for y in range(yb, ny, 2) for z in range(nz) for x in xs]
         for c in range(nc)
-        for yb, xb in halves
+        for yb in range(2)
+        for xs in columns(c, nx)
     ]
     near = [
-        [index(z, y + c + (yb + c) % 2, x + c + (xb + c) % 2, c) for yb, xb in halves]
+        [
+            index(z, y + c + (yb + c) % 2, next(v for v in (x + c, x + c + 1) if v % nx in xs), c)
+            for yb in range(2)
+            for xs in columns(c, nx)
+        ]
         for z in range(nz)
         for c in range(nc)
-        for y, x in places
+        for y in range(0, ny, 2)
+        for x in range(0, nx, 2)
     ]
     return far, near
 
@@ -315,7 +327,7 @@
     )(*(pltpu.with_memory_space_constraint(h, pltpu.HBM) for h in heads))
     got = swap(send.reshape(nz * spread, 2 * FINE, LANES), far)
 
-    views = (ny // 2, 2, nx // 2, 2, nc, parts, FINE, hidden)
+    views = (ny // 2, 2, nx, nc, parts, FINE, hidden)
     ordered = (members, parts, ny // 2, nx // 2, FINE, hidden)
     gate, up = (
         pltpu.with_memory_space_constraint(w.reshape(views), pltpu.HBM) for w in (w_gate, w_up)
@@ -324,7 +336,7 @@
 
     def order(sent, kept, *sources):
         spaces = [pltpu.VMEM] * len(sent) + [pltpu.HBM] * len(kept)
-        count = len(spaces) * members * parts + len(kept)
+        count = len(spaces) * 6 * parts + len(kept)
         ordered_weights = pl.pallas_call(
             functools.partial(order_kernel, (sent, kept, len(sources))),
             out_shape=[space(ordered, BF16) for space in spaces],

time: 109 us -> 106 us (0.972)
  waiting for transfers between devices: 8.02 us -> 5.15 us
    all_to_all x1, waiting for transfers between devices: 6.47 us -> 3.6 us  [swap(): lax.all_to_all(blocks, AXES, split_axis=0, concat_axis=0, axis_index_grou...]
    ppermute x5, starting transfers between devices: 11.8 us -> 13.8 us  [other_core(): return lax.ppermute(values, 'c', [(0, 1), (1, 0)])]
    all_to_all x1, starting transfers between devices: 19.6 us -> 18.1 us  [swap(): lax.all_to_all(blocks, AXES, split_axis=0, concat_axis=0, axis_index_grou...]
where the time goes in v10:
time: 106 us; the launch traced here: 105 us
  blocking collectives  53.9 us (51%)
  starting transfers between devices  31.9 us (30%)
  Pallas kernels  12 us (11%)
  waiting for transfers between devices  5.15 us (5%)
  local copies, waits for them, and re-layouts  1.74 us (2%)
    all_to_all x3, blocking collectives, swap(): lax.all_to_all(blocks, AXES, split_axis=0, concat_axis=0, axis_index_grou...  53.9 us
    all_to_all x1, starting transfers between devices, swap(): lax.all_to_all(blocks, AXES, split_axis=0, concat_axis=0, axis_index_grou...  18.1 us
    ppermute x5, starting transfers between devices, other_core(): return lax.ppermute(values, 'c', [(0, 1), (1, 0)])  13.8 us
    pallas_call x8, Pallas kernels, call(): pl.pallas_call(kernel, out_shape=jax.ShapeDtypeStruct(shape, dtype), in_s...  4.92 us
    pallas_call x2, Pallas kernels, order(): pl.pallas_call(functools.partial(order_kernel, (sent, kept, len(sources))...  4.91 us
    all_to_all x1, waiting for transfers between devices, swap(): lax.all_to_all(blocks, AXES, split_axis=0, concat_axis=0, axis_index_grou...  3.6 us
  transfers between devices with their start and end apart: 6, of which 2 were waited for; matrix products, arithmetic and copies ran while one was open for 2% of the time, Pallas kernels for 6%

profile of v10, /device:TPU:1, one launch (start us, length us, event | category | flops | bytes accessed | tf_op | source)
XLA Modules:
  0.0 104.9 jit_solution(17494238497391020329)
XLA Ops:
  0.0 2.1 %shard_map.82 = bf16[4,8,2,32,128]{4,3,2,1,0:T(8,128)(2,1)} custom-call(s32[2,128]{1,0:T(2,128)} %bitcast.31, bf16[48,128]{1,0:T(8,128)(2,1)} %bitcast.44, bf16[48,128]{1,0:T(8,128)(2,1)} %bitcast.45), custom_call_target="tpu_custom_call" | custom-call | tf_op jit(solution)/shard_map/pallas_call | solution.py:319
  2.1 18.1 %all-to-all-start = ((bf16[64,32,128]{2,1,0:T(8,128)(2,1)}), bf16[64,32,128]{2,1,0:T(8,128)(2,1)S(1)}, u32[]{:S(2)}, u32[]{:S(2)}) async-start(bf16[64,32,128]{2,1,0:T(8,128)(2,1)} %bitcast.42), calls=%async_computation | async-start | bytes 1048576 | tf_op jit(solution)/shard_map/all_to_all | solution.py:296
  20.2 1.7 %copy.9 = bf16[3072,256]{1,0:T(8,128)(2,1)S(1)} copy(bf16[3072,256]{0,1:T(8,128)(2,1)} %bitcast.43) | data formatting | bytes 3145728 | tf_op jit(solution)/shard_map/transpose | solution.py:335
  21.9 2.2 %shard_map.84 = (bf16[4,3,4,2,16,256]{5,4,3,2,1,0:T(8,128)(2,1)S(1)}, bf16[4,3,4,2,16,256]{5,4,3,2,1,0:T(8,128)(2,1)S(1)}, bf16[4,3,4,2,16,256]{5,4,3,2,1,0:T(8,128)(2,1)S(1)}, bf16[4,3,4,2,16,256]{5,4,3,2,1,0:T(8,128)(2,1)}) custom-call(bf16[4,2,4,2,3,16,256]{6,5,4,3,2,1,0:T(8,128)(2,1)} %bitcast.38, bf16[4,2,4,2,3,16,256]{6,5,4,3,2,1,0:T(8,128)(2,1)} %bitcast.40, ...), custom_call_target="tpu_custom_call" | custom-call | bytes 6291456 | tf_op jit(solution)/shard_map/pallas_call | solution.py:340
  24.1 4.1 %collective-permute-start = (bf16[1536,256]{1,0:T(8,128)(2,1)S(1)}, bf16[1536,256]{1,0:T(8,128)(2,1)S(1)}, u32[]{:S(2)}, u32[]{:S(2)}) collective-permute-start(bf16[1536,256]{1,0:T(8,128)(2,1)S(1)} %bitcast.37), channel_id=1, source_target_pairs={{0,1},{1,0},{2,3},{3,2},{4,5},{5,4},{6,7},{7,6},{8,9},{9,8},{10,11... | collective-permute-start | bytes 2359304 | tf_op jit(solution)/shard_map/ppermute | solution.py:302
  28.3 1.9 %collective-permute-start.1 = (bf16[1536,256]{1,0:T(8,128)(2,1)S(1)}, bf16[1536,256]{1,0:T(8,128)(2,1)S(1)}, u32[]{:S(2)}, u32[]{:S(2)}) collective-permute-start(bf16[1536,256]{1,0:T(8,128)(2,1)S(1)} %bitcast.36), channel_id=1, source_target_pairs={{0,1},{1,0},{2,3},{3,2},{4,5},{5,4},{6,7},{7,6},{8,9},{9,8},{10,11... | collective-permute-start | bytes 2359304 | tf_op jit(solution)/shard_map/ppermute | solution.py:302
  30.2 2.4 %collective-permute-start.2 = (bf16[1536,256]{1,0:T(8,128)(2,1)S(1)}, bf16[1536,256]{1,0:T(8,128)(2,1)S(1)}, u32[]{:S(2)}, u32[]{:S(2)}) collective-permute-start(bf16[1536,256]{1,0:T(8,128)(2,1)S(1)} %bitcast.35), channel_id=1, source_target_pairs={{0,1},{1,0},{2,3},{3,2},{4,5},{5,4},{6,7},{7,6},{8,9},{9,8},{10,11... | collective-permute-start | bytes 2359304 | tf_op jit(solution)/shard_map/ppermute | solution.py:302
  32.6 2.7 %shard_map.83 = (bf16[4,3,4,2,16,256]{5,4,3,2,1,0:T(8,128)(2,1)}, bf16[4,3,4,2,16,256]{5,4,3,2,1,0:T(8,128)(2,1)}) custom-call(bf16[4,2,4,2,3,16,256]{6,5,4,3,2,1,0:T(8,128)(2,1)} %bitcast.39, bf16[4,2,4,2,3,16,256]{6,5,4,3,2,1,0:T(8,128)(2,1)} %bitcast.41), custom_call_target="tpu_custom_call" | custom-call | bytes 6291456 | tf_op jit(solution)/shard_map/pallas_call | solution.py:340
  35.3 0.0 collective-permute-done.gate_ref
  35.4 0.0 collective-permute-done.1.up_ref
  35.4 0.0 collective-permute-done.2.down_ref
  35.4 3.6 %all-to-all-done = bf16[64,32,128]{2,1,0:T(8,128)(2,1)S(1)} async-done(((bf16[64,32,128]{2,1,0:T(8,128)(2,1)}), bf16[64,32,128]{2,1,0:T(8,128)(2,1)S(1)}, u32[]{:S(2)}, u32[]{:S(2)}) %all-to-all-start) | async-done | bytes 524320 | tf_op jit(solution)/shard_map/all_to_all | solution.py:296
  39.0 0.3 shard_map.85
  39.3 19.1 %all_to_all.20.in_ref = bf16[4,640,384]{2,1,0:T(8,128)(2,1)S(1)} all-to-all(bf16[4,640,384]{2,1,0:T(8,128)(2,1)S(1)} %shard_map.85), channel_id=1, replica_groups={{0,2,8,10},{6,4,14,12},{16,18,24,26},{22,20,30,28},{32,34,40,42},{38,36..., dimensions={0} | all-to-all | bytes 3932160 | tf_op jit(solution)/shard_map/all_to_all | solution.py:296
  58.4 0.0 copy-start
  58.4 0.0 copy-start.1
  58.4 0.0 copy-start.2
  58.4 0.9 shard_map.87.a_ref
  59.3 0.0 copy-start.3
  59.3 0.0 copy-start.4
  59.3 0.0 copy-start.5
  59.3 3.5 %collective-permute-start.3 = (f32[320,768]{1,0:T(8,128)S(1)}, f32[320,768]{1,0:T(8,128)S(1)}, u32[]{:S(2)}, u32[]{:S(2)}) collective-permute-start(f32[320,768]{1,0:T(8,128)S(1)} %shard_map.87.a_ref), channel_id=1, source_target_pairs={{0,1},{1,0},{2,3},{3,2},{4,5},{5,4},{6,7},{7,6},{8,9},{9,8},{10,11... | collective-permute-start | bytes 2949128 | tf_op jit(solution)/shard_map/ppermute | solution.py:302
  62.8 0.0 copy-done
  62.8 0.0 copy-done.1
  62.8 0.0 copy-done.2
  62.8 0.9 shard_map.86.a_ref
  63.8 1.9 %collective-permute-start.4 = (f32[320,768]{1,0:T(8,128)S(1)}, f32[320,768]{1,0:T(8,128)S(1)}, u32[]{:S(2)}, u32[]{:S(2)}) collective-permute-start(f32[320,768]{1,0:T(8,128)S(1)} %shard_map.86.a_ref), channel_id=1, source_target_pairs={{0,1},{1,0},{2,3},{3,2},{4,5},{5,4},{6,7},{7,6},{8,9},{9,8},{10,11... | collective-permute-start | bytes 2949128 | tf_op jit(solution)/shard_map/ppermute | solution.py:302
  65.7 0.0 copy-done.3
  65.7 0.0 copy-done.4
  65.7 0.0 copy-done.5
  65.7 0.2 shard_map.89.combine_ref
  66.0 0.0 collective-permute-done.3.b_ref
  66.0 0.7 shard_map.88.sum_ref
  66.7 1.5 %collective-permute-done.4.b_ref = f32[320,768]{1,0:T(8,128)S(1)} collective-permute-done((f32[320,768]{1,0:T(8,128)S(1)}, f32[320,768]{1,0:T(8,128)S(1)}, u32[]{:S(2)}, u32[]{:S(2)}) %collective-permute-start.4) | collective-permute-done | bytes 983072 | tf_op jit(solution)/shard_map/ppermute | solution.py:302
  68.2 0.8 shard_map.90
  69.0 13.4 %all_to_all.21.in_ref = bf16[4,320,384]{2,1,0:T(8,128)(2,1)S(1)} all-to-all(bf16[4,320,384]{2,1,0:T(8,128)(2,1)S(1)} %shard_map.90), channel_id=1, replica_groups={{0,2,8,10},{6,4,14,12},{16,18,24,26},{22,20,30,28},{32,34,40,42},{38,36..., dimensions={0} | all-to-all | bytes 1966080 | tf_op jit(solution)/shard_map/all_to_all | solution.py:296
  82.4 0.2 shard_map.91
  82.6 21.4 %all_to_all.22 = bf16[64,16,128]{2,1,0:T(8,128)(2,1)S(1)} all-to-all(bf16[64,16,128]{2,1,0:T(8,128)(2,1)S(1)} %bitcast.29), channel_id=1, replica_groups={{0,6,64,70,128,134,192,198,256,262,320,326,384,390,448,454,16,22,80,86,..., dimensions={0} | all-to-all | bytes 524288 | tf_op jit(solution)/shard_map/all_to_all | solution.py:296
  104.0 0.9 shard_map.92
Async XLA Ops:
  2.1 36.8 %all-to-all-start = ((bf16[64,32,128]{2,1,0:T(8,128)(2,1)}), bf16[64,32,128]{2,1,0:T(8,128)(2,1)S(1)}, u32[]{:S(2)}, u32[]{:S(2)}) async-start(bf16[64,32,128]{2,1,0:T(8,128)(2,1)} %bitcast.42), calls=%async_computation | async-start | bytes 1048576 | tf_op jit(solution)/shard_map/all_to_all | solution.py:296
  24.1 11.2 %collective-permute-start = (bf16[1536,256]{1,0:T(8,128)(2,1)S(1)}, bf16[1536,256]{1,0:T(8,128)(2,1)S(1)}, u32[]{:S(2)}, u32[]{:S(2)}) collective-permute-start(bf16[1536,256]{1,0:T(8,128)(2,1)S(1)} %bitcast.37), channel_id=1, source_target_pairs={{0,1},{1,0},{2,3},{3,2},{4,5},{5,4},{6,7},{7,6},{8,9},{9,8},{10,11... | collective-permute-start | bytes 2359304 | tf_op jit(solution)/shard_map/ppermute | solution.py:302
  28.3 7.1 %collective-permute-start.1 = (bf16[1536,256]{1,0:T(8,128)(2,1)S(1)}, bf16[1536,256]{1,0:T(8,128)(2,1)S(1)}, u32[]{:S(2)}, u32[]{:S(2)}) collective-permute-start(bf16[1536,256]{1,0:T(8,128)(2,1)S(1)} %bitcast.36), channel_id=1, source_target_pairs={{0,1},{1,0},{2,3},{3,2},{4,5},{5,4},{6,7},{7,6},{8,9},{9,8},{10,11... | collective-permute-start | bytes 2359304 | tf_op jit(solution)/shard_map/ppermute | solution.py:302
  30.2 5.2 %collective-permute-start.2 = (bf16[1536,256]{1,0:T(8,128)(2,1)S(1)}, bf16[1536,256]{1,0:T(8,128)(2,1)S(1)}, u32[]{:S(2)}, u32[]{:S(2)}) collective-permute-start(bf16[1536,256]{1,0:T(8,128)(2,1)S(1)} %bitcast.35), channel_id=1, source_target_pairs={{0,1},{1,0},{2,3},{3,2},{4,5},{5,4},{6,7},{7,6},{8,9},{9,8},{10,11... | collective-permute-start | bytes 2359304 | tf_op jit(solution)/shard_map/ppermute | solution.py:302
  58.4 4.4 %copy-start = (bf16[4,3,4,2,16,256]{5,4,3,2,1,0:T(8,128)(2,1)S(1)}, bf16[4,3,4,2,16,256]{5,4,3,2,1,0:T(8,128)(2,1)}, u32[]{:S(2)}) copy-start(bf16[4,3,4,2,16,256]{5,4,3,2,1,0:T(8,128)(2,1)} %get-tuple-element.20) | copy-start | bytes 2359300
  58.4 4.5 %copy-start.1 = (bf16[4,3,4,2,16,256]{5,4,3,2,1,0:T(8,128)(2,1)S(1)}, bf16[4,3,4,2,16,256]{5,4,3,2,1,0:T(8,128)(2,1)}, u32[]{:S(2)}) copy-start(bf16[4,3,4,2,16,256]{5,4,3,2,1,0:T(8,128)(2,1)} %get-tuple-element.21) | copy-start | bytes 2359300
  58.4 4.5 %copy-start.2 = (bf16[4,3,4,2,16,256]{5,4,3,2,1,0:T(8,128)(2,1)S(1)}, bf16[4,3,4,2,16,256]{5,4,3,2,1,0:T(8,128)(2,1)}, u32[]{:S(2)}) copy-start(bf16[4,3,4,2,16,256]{5,4,3,2,1,0:T(8,128)(2,1)} %get-tuple-element.22) | copy-start | bytes 2359300
  59.3 6.4 %copy-start.3 = (s32[128,2]{0,1:T(2,128)S(1)}, s32[128,2]{0,1:T(2,128)}, u32[]{:S(2)}) copy-start(s32[128,2]{0,1:T(2,128)} %param.12) | copy-start | bytes 3076
  59.3 6.4 %copy-start.4 = (f32[128,2]{0,1:T(2,128)S(1)}, f32[128,2]{0,1:T(2,128)}, u32[]{:S(2)}) copy-start(f32[128,2]{0,1:T(2,128)} %param.11) | copy-start | bytes 3076
  59.3 6.4 %copy-start.5 = (f32[128]{0:T(128)S(1)}, f32[128]{0:T(128)}, u32[]{:S(2)}) copy-start(f32[128]{0:T(128)} %param.10) | copy-start | bytes 1540
  59.3 6.6 %collective-permute-start.3 = (f32[320,768]{1,0:T(8,128)S(1)}, f32[320,768]{1,0:T(8,128)S(1)}, u32[]{:S(2)}, u32[]{:S(2)}) collective-permute-start(f32[320,768]{1,0:T(8,128)S(1)} %shard_map.87.a_ref), channel_id=1, source_target_pairs={{0,1},{1,0},{2,3},{3,2},{4,5},{5,4},{6,7},{7,6},{8,9},{9,8},{10,11... | collective-permute-start | bytes 2949128 | tf_op jit(solution)/shard_map/ppermute | solution.py:302
  63.8 4.5 %collective-permute-start.4 = (f32[320,768]{1,0:T(8,128)S(1)}, f32[320,768]{1,0:T(8,128)S(1)}, u32[]{:S(2)}, u32[]{:S(2)}) collective-permute-start(f32[320,768]{1,0:T(8,128)S(1)} %shard_map.86.a_ref), channel_id=1, source_target_pairs={{0,1},{1,0},{2,3},{3,2},{4,5},{5,4},{6,7},{7,6},{8,9},{9,8},{10,11... | collective-permute-start | bytes 2949128 | tf_op jit(solution)/shard_map/ppermute | solution.py:302

commit v11 on v10

--- a/solution.py
+++ b/solution.py
@@ -153,25 +153,39 @@
     return copies
 
 
-def order_kernel(kept, *refs):
+def sent_kernel(gate_hbm, up_hbm, down_hbm, gate_ref, up_ref, down_ref, own_hbm, raw, turned, sems):
     core = lax.axis_index("c")
-    sent, out_refs = len(kept[0]), len(kept[0]) + len(kept[1])
-    sources = refs[: kept[2]]
-    outs = refs[kept[2] : kept[2] + out_refs]
-    sems = refs[kept[2] + out_refs]
-    held = refs[kept[2] + out_refs + 1 :]
-    waits, each = [], 6 * sources[0].shape[4]
-    for i, k in enumerate(kept[0]):
-        waits += gather(sources[k], 1 - core, outs[i], sems, i * each)
-    own = [
-        gather(sources[k], core, held[i], sems, (sent + i) * each) for i, k in enumerate(kept[1])
+    chunks, _, width = raw.shape
+    loads = [
+        pltpu.make_async_copy(down_hbm.at[:, pl.ds(k * width, width)], raw.at[k], sems.at[k])
+        for k in range(chunks)
     ]
-    for i, copies in enumerate(own):
-        for copy in copies:
+    for copy in loads:
+        copy.start()
+    each = 6 * gate_hbm.shape[4]
+    waits = gather(gate_hbm, 1 - core, gate_ref, sems, chunks)
+    waits += gather(up_hbm, 1 - core, up_ref, sems, chunks + each)
+    for k, copy in enumerate(loads):
+        copy.wait()
+        turned[k] = raw[k].T.reshape(turned.shape[1:])
+    waits += gather(turned, 1 - core, down_ref, sems, chunks + 2 * each)
+    waits += gather(turned, core, own_hbm, sems, chunks + 3 * each)
+    for copy in waits:
+        copy.wait()
+
+
+def own_kernel(gate_hbm, up_hbm, own_gate, own_up, held, sems):
+    core = lax.axis_index("c")
+    each = 6 * gate_hbm.shape[4]
+    parts = [
+        gather(src, core, held.at[k], sems, k * each) for k, src in enumerate((gate_hbm, up_hbm))
+    ]
+    waits = []
+    for k, out in enumerate((own_gate, own_up)):
+        for copy in parts[k]:
             copy.wait()
-        copy = pltpu.make_async_copy(held[i], outs[sent + i], sems.at[out_refs * each + i])
-        copy.start()
-        waits.append(copy)
+        waits.append(pltpu.make_async_copy(held.at[k], out, sems.at[2 * each + k]))
+        waits[-1].start()
     for copy in waits:
         copy.wait()
 
@@ -332,18 +346,16 @@
     gate, up = (
         pltpu.with_memory_space_constraint(w.reshape(views), pltpu.HBM) for w in (w_gate, w_up)
     )
-    down = w_down[0].T.reshape(views)
-
-    def order(sent, kept, *sources):
-        spaces = [pltpu.VMEM] * len(sent) + [pltpu.HBM] * len(kept)
-        count = len(spaces) * 6 * parts + len(kept)
+    down = pltpu.with_memory_space_constraint(w_down[0], pltpu.HBM)
+    chunks, each = ny // 2, 6 * parts
+
+    def order(kernel, spaces, scratch, *sources):
         ordered_weights = pl.pallas_call(
-            functools.partial(order_kernel, (sent, kept, len(sources))),
+            kernel,
             out_shape=[space(ordered, BF16) for space in spaces],
             in_specs=[pl.BlockSpec(memory_space=pl.ANY)] * len(sources),
             out_specs=[pl.BlockSpec(memory_space=space) for space in spaces],
-            scratch_shapes=[pltpu.SemaphoreType.DMA((count,))]
-            + [pltpu.VMEM(ordered, BF16)] * len(kept),
+            scratch_shapes=scratch,
             compiler_params=pltpu.CompilerParams(vmem_limit_bytes=VMEM_LIMIT),
             cost_estimate=pl.CostEstimate(
                 flops=0, bytes_accessed=6 * 1024 * 1024, transcendentals=0
@@ -351,8 +363,26 @@
         )(*sources)
         return [w.reshape(members * wide, hidden) for w in ordered_weights]
 
-    *sent, own_down = order((0, 1, 2), (2,), gate, up, down)
-    own = [*order((), (0, 1), gate, up), own_down]
+    *sent, own_down = order(
+        sent_kernel,
+        [pltpu.VMEM] * 3 + [pltpu.HBM],
+        [
+            pltpu.VMEM((chunks, hidden, down.shape[1] // chunks), BF16),
+            pltpu.VMEM(views, BF16),
+            pltpu.SemaphoreType.DMA((chunks + 4 * each,)),
+        ],
+        gate,
+        up,
+        down,
+    )
+    own = order(
+        own_kernel,
+        [pltpu.HBM] * 2,
+        [pltpu.VMEM((2,) + ordered, BF16), pltpu.SemaphoreType.DMA((2 * each + 2,))],
+        gate,
+        up,
+    )
+    own = [*own, own_down]
     other = [other_core(w) for w in sent]
     got, own, other = lax.optimization_barrier((got, own, other))
 

time: 106 us -> 105 us (level)
  local copies, waits for them, and re-layouts: 1.74 us -> 0.03 us
  Pallas kernels: 12 us -> 13.1 us
    transpose x1 -> x0, local copies, waits for them, and re-layouts: 1.71 us -> none  [shards(): down = w_down[0].T.reshape(views)]
    pallas_call x2, Pallas kernels: 4.91 us -> 6.12 us  [order(): pl.pallas_call(kernel, out_shape=[space(ordered, BF16) for space in space...]
  transfers between devices with their start and end apart: 6 -> 6, of which waited for: 2 -> 2; matrix products, arithmetic and copies ran while one was open for 2% -> 0% of each run, Pallas kernels for 6% -> 8%
where the time goes in v11:
time: 105 us; the launch traced here: 104 us
  blocking collectives  53.5 us (51%)
  starting transfers between devices  31.9 us (30%)
  Pallas kernels  13.1 us (12%)
  waiting for transfers between devices  5.66 us (5%)
    all_to_all x3, blocking collectives, swap(): lax.all_to_all(blocks, AXES, split_axis=0, concat_axis=0, axis_index_grou...  53.5 us
    all_to_all x1, starting transfers between devices, swap(): lax.all_to_all(blocks, AXES, split_axis=0, concat_axis=0, axis_index_grou...  18.1 us
    ppermute x5, starting transfers between devices, other_core(): return lax.ppermute(values, 'c', [(0, 1), (1, 0)])  13.8 us
    pallas_call x2, Pallas kernels, order(): pl.pallas_call(kernel, out_shape=[space(ordered, BF16) for space in space...  6.12 us
    pallas_call x8, Pallas kernels, call(): pl.pallas_call(kernel, out_shape=jax.ShapeDtypeStruct(shape, dtype), in_s...  4.91 us
    all_to_all x1, waiting for transfers between devices, swap(): lax.all_to_all(blocks, AXES, split_axis=0, concat_axis=0, axis_index_grou...  4.11 us
    pallas_call x1, Pallas kernels, shards(): pl.pallas_call(functools.partial(pack_kernel, capacity), out_shape=pltpu....  2.12 us
  transfers between devices with their start and end apart: 6, of which 2 were waited for; matrix products, arithmetic and copies ran while one was open for 0% of the time, Pallas kernels for 8%

profile of v11, /device:TPU:1, one launch (start us, length us, event | category | flops | bytes accessed | tf_op | source)
XLA Modules:
  0.0 104.4 jit_solution(16214862314172176046)
XLA Ops:
  0.0 2.1 %shard_map.82 = bf16[4,8,2,32,128]{4,3,2,1,0:T(8,128)(2,1)} custom-call(s32[2,128]{1,0:T(2,128)} %bitcast.27, bf16[48,128]{1,0:T(8,128)(2,1)} %bitcast.40, bf16[48,128]{1,0:T(8,128)(2,1)} %bitcast.41), custom_call_target="tpu_custom_call" | custom-call | tf_op jit(solution)/shard_map/pallas_call | solution.py:333
  2.1 18.1 %all-to-all-start = ((bf16[64,32,128]{2,1,0:T(8,128)(2,1)}), bf16[64,32,128]{2,1,0:T(8,128)(2,1)S(1)}, u32[]{:S(2)}, u32[]{:S(2)}) async-start(bf16[64,32,128]{2,1,0:T(8,128)(2,1)} %bitcast.38), calls=%async_computation | async-start | bytes 1048576 | tf_op jit(solution)/shard_map/all_to_all | solution.py:310
  20.2 3.4 %shard_map.84 = (bf16[4,3,4,2,16,256]{5,4,3,2,1,0:T(8,128)(2,1)S(1)}, bf16[4,3,4,2,16,256]{5,4,3,2,1,0:T(8,128)(2,1)S(1)}, bf16[4,3,4,2,16,256]{5,4,3,2,1,0:T(8,128)(2,1)S(1)}, bf16[4,3,4,2,16,256]{5,4,3,2,1,0:T(8,128)(2,1)}) custom-call(bf16[4,2,4,2,3,16,256]{6,5,4,3,2,1,0:T(8,128)(2,1)} %bitcast.34, bf16[4,2,4,2,3,16,256]{6,5,4,3,2,1,0:T(8,128)(2,1)} %bitcast.36, ...), custom_call_target="tpu_custom_call" | custom-call | bytes 6291456 | tf_op jit(solution)/shard_map/pallas_call | solution.py:353
  23.6 4.1 %collective-permute-start = (bf16[1536,256]{1,0:T(8,128)(2,1)S(1)}, bf16[1536,256]{1,0:T(8,128)(2,1)S(1)}, u32[]{:S(2)}, u32[]{:S(2)}) collective-permute-start(bf16[1536,256]{1,0:T(8,128)(2,1)S(1)} %bitcast.33), channel_id=1, source_target_pairs={{0,1},{1,0},{2,3},{3,2},{4,5},{5,4},{6,7},{7,6},{8,9},{9,8},{10,11... | collective-permute-start | bytes 2359304 | tf_op jit(solution)/shard_map/ppermute | solution.py:316
  27.8 1.9 %collective-permute-start.1 = (bf16[1536,256]{1,0:T(8,128)(2,1)S(1)}, bf16[1536,256]{1,0:T(8,128)(2,1)S(1)}, u32[]{:S(2)}, u32[]{:S(2)}) collective-permute-start(bf16[1536,256]{1,0:T(8,128)(2,1)S(1)} %bitcast.32), channel_id=1, source_target_pairs={{0,1},{1,0},{2,3},{3,2},{4,5},{5,4},{6,7},{7,6},{8,9},{9,8},{10,11... | collective-permute-start | bytes 2359304 | tf_op jit(solution)/shard_map/ppermute | solution.py:316
  29.7 2.4 %collective-permute-start.2 = (bf16[1536,256]{1,0:T(8,128)(2,1)S(1)}, bf16[1536,256]{1,0:T(8,128)(2,1)S(1)}, u32[]{:S(2)}, u32[]{:S(2)}) collective-permute-start(bf16[1536,256]{1,0:T(8,128)(2,1)S(1)} %bitcast.31), channel_id=1, source_target_pairs={{0,1},{1,0},{2,3},{3,2},{4,5},{5,4},{6,7},{7,6},{8,9},{9,8},{10,11... | collective-permute-start | bytes 2359304 | tf_op jit(solution)/shard_map/ppermute | solution.py:316
  32.1 2.7 %shard_map.83 = (bf16[4,3,4,2,16,256]{5,4,3,2,1,0:T(8,128)(2,1)}, bf16[4,3,4,2,16,256]{5,4,3,2,1,0:T(8,128)(2,1)}) custom-call(bf16[4,2,4,2,3,16,256]{6,5,4,3,2,1,0:T(8,128)(2,1)} %bitcast.35, bf16[4,2,4,2,3,16,256]{6,5,4,3,2,1,0:T(8,128)(2,1)} %bitcast.37), custom_call_target="tpu_custom_call" | custom-call | bytes 6291456 | tf_op jit(solution)/shard_map/pallas_call | solution.py:353
  34.8 0.0 collective-permute-done.gate_ref
  34.8 0.0 collective-permute-done.1.up_ref
  34.8 0.0 collective-permute-done.2.down_ref
  34.9 4.1 %all-to-all-done = bf16[64,32,128]{2,1,0:T(8,128)(2,1)S(1)} async-done(((bf16[64,32,128]{2,1,0:T(8,128)(2,1)}), bf16[64,32,128]{2,1,0:T(8,128)(2,1)S(1)}, u32[]{:S(2)}, u32[]{:S(2)}) %all-to-all-start) | async-done | bytes 524320 | tf_op jit(solution)/shard_map/all_to_all | solution.py:310
  39.0 0.3 shard_map.85
  39.3 19.1 %all_to_all.20.in_ref = bf16[4,640,384]{2,1,0:T(8,128)(2,1)S(1)} all-to-all(bf16[4,640,384]{2,1,0:T(8,128)(2,1)S(1)} %shard_map.85), channel_id=1, replica_groups={{0,2,8,10},{6,4,14,12},{16,18,24,26},{22,20,30,28},{32,34,40,42},{38,36..., dimensions={0} | all-to-all | bytes 3932160 | tf_op jit(solution)/shard_map/all_to_all | solution.py:310
  58.4 0.0 copy-start
  58.4 0.0 copy-start.1
  58.4 0.0 copy-start.2
  58.4 0.9 shard_map.87.a_ref
  59.3 0.0 copy-start.3
  59.3 0.0 copy-start.4
  59.3 0.0 copy-start.5
  59.4 3.5 %collective-permute-start.3 = (f32[320,768]{1,0:T(8,128)S(1)}, f32[320,768]{1,0:T(8,128)S(1)}, u32[]{:S(2)}, u32[]{:S(2)}) collective-permute-start(f32[320,768]{1,0:T(8,128)S(1)} %shard_map.87.a_ref), channel_id=1, source_target_pairs={{0,1},{1,0},{2,3},{3,2},{4,5},{5,4},{6,7},{7,6},{8,9},{9,8},{10,11... | collective-permute-start | bytes 2949128 | tf_op jit(solution)/shard_map/ppermute | solution.py:316
  62.8 0.0 copy-done
  62.8 0.0 copy-done.1
  62.8 0.0 copy-done.2
  62.9 0.9 shard_map.86.a_ref
  63.8 1.9 %collective-permute-start.4 = (f32[320,768]{1,0:T(8,128)S(1)}, f32[320,768]{1,0:T(8,128)S(1)}, u32[]{:S(2)}, u32[]{:S(2)}) collective-permute-start(f32[320,768]{1,0:T(8,128)S(1)} %shard_map.86.a_ref), channel_id=1, source_target_pairs={{0,1},{1,0},{2,3},{3,2},{4,5},{5,4},{6,7},{7,6},{8,9},{9,8},{10,11... | collective-permute-start | bytes 2949128 | tf_op jit(solution)/shard_map/ppermute | solution.py:316
  65.7 0.0 copy-done.3
  65.7 0.0 copy-done.4
  65.8 0.0 copy-done.5
  65.8 0.2 shard_map.89.combine_ref
  66.0 0.0 collective-permute-done.3.b_ref
  66.0 0.7 shard_map.88.sum_ref
  66.7 1.5 %collective-permute-done.4.b_ref = f32[320,768]{1,0:T(8,128)S(1)} collective-permute-done((f32[320,768]{1,0:T(8,128)S(1)}, f32[320,768]{1,0:T(8,128)S(1)}, u32[]{:S(2)}, u32[]{:S(2)}) %collective-permute-start.4) | collective-permute-done | bytes 983072 | tf_op jit(solution)/shard_map/ppermute | solution.py:316
  68.3 0.7 shard_map.90
  69.0 13.4 %all_to_all.21.in_ref = bf16[4,320,384]{2,1,0:T(8,128)(2,1)S(1)} all-to-all(bf16[4,320,384]{2,1,0:T(8,128)(2,1)S(1)} %shard_map.90), channel_id=1, replica_groups={{0,2,8,10},{6,4,14,12},{16,18,24,26},{22,20,30,28},{32,34,40,42},{38,36..., dimensions={0} | all-to-all | bytes 1966080 | tf_op jit(solution)/shard_map/all_to_all | solution.py:310
  82.4 0.2 shard_map.91
  82.6 21.0 %all_to_all.22 = bf16[64,16,128]{2,1,0:T(8,128)(2,1)S(1)} all-to-all(bf16[64,16,128]{2,1,0:T(8,128)(2,1)S(1)} %bitcast.25), channel_id=1, replica_groups={{0,6,64,70,128,134,192,198,256,262,320,326,384,390,448,454,16,22,80,86,..., dimensions={0} | all-to-all | bytes 524288 | tf_op jit(solution)/shard_map/all_to_all | solution.py:310
  103.6 0.9 shard_map.92
Async XLA Ops:
  2.1 36.8 %all-to-all-start = ((bf16[64,32,128]{2,1,0:T(8,128)(2,1)}), bf16[64,32,128]{2,1,0:T(8,128)(2,1)S(1)}, u32[]{:S(2)}, u32[]{:S(2)}) async-start(bf16[64,32,128]{2,1,0:T(8,128)(2,1)} %bitcast.38), calls=%async_computation | async-start | bytes 1048576 | tf_op jit(solution)/shard_map/all_to_all | solution.py:310
  23.6 11.2 %collective-permute-start = (bf16[1536,256]{1,0:T(8,128)(2,1)S(1)}, bf16[1536,256]{1,0:T(8,128)(2,1)S(1)}, u32[]{:S(2)}, u32[]{:S(2)}) collective-permute-start(bf16[1536,256]{1,0:T(8,128)(2,1)S(1)} %bitcast.33), channel_id=1, source_target_pairs={{0,1},{1,0},{2,3},{3,2},{4,5},{5,4},{6,7},{7,6},{8,9},{9,8},{10,11... | collective-permute-start | bytes 2359304 | tf_op jit(solution)/shard_map/ppermute | solution.py:316
  27.8 7.1 %collective-permute-start.1 = (bf16[1536,256]{1,0:T(8,128)(2,1)S(1)}, bf16[1536,256]{1,0:T(8,128)(2,1)S(1)}, u32[]{:S(2)}, u32[]{:S(2)}) collective-permute-start(bf16[1536,256]{1,0:T(8,128)(2,1)S(1)} %bitcast.32), channel_id=1, source_target_pairs={{0,1},{1,0},{2,3},{3,2},{4,5},{5,4},{6,7},{7,6},{8,9},{9,8},{10,11... | collective-permute-start | bytes 2359304 | tf_op jit(solution)/shard_map/ppermute | solution.py:316
  29.7 5.2 %collective-permute-start.2 = (bf16[1536,256]{1,0:T(8,128)(2,1)S(1)}, bf16[1536,256]{1,0:T(8,128)(2,1)S(1)}, u32[]{:S(2)}, u32[]{:S(2)}) collective-permute-start(bf16[1536,256]{1,0:T(8,128)(2,1)S(1)} %bitcast.31), channel_id=1, source_target_pairs={{0,1},{1,0},{2,3},{3,2},{4,5},{5,4},{6,7},{7,6},{8,9},{9,8},{10,11... | collective-permute-start | bytes 2359304 | tf_op jit(solution)/shard_map/ppermute | solution.py:316
  58.4 4.5 %copy-start = (bf16[4,3,4,2,16,256]{5,4,3,2,1,0:T(8,128)(2,1)S(1)}, bf16[4,3,4,2,16,256]{5,4,3,2,1,0:T(8,128)(2,1)}, u32[]{:S(2)}) copy-start(bf16[4,3,4,2,16,256]{5,4,3,2,1,0:T(8,128)(2,1)} %get-tuple-element.20) | copy-start | bytes 2359300
  58.4 4.5 %copy-start.1 = (bf16[4,3,4,2,16,256]{5,4,3,2,1,0:T(8,128)(2,1)S(1)}, bf16[4,3,4,2,16,256]{5,4,3,2,1,0:T(8,128)(2,1)}, u32[]{:S(2)}) copy-start(bf16[4,3,4,2,16,256]{5,4,3,2,1,0:T(8,128)(2,1)} %get-tuple-element.21) | copy-start | bytes 2359300
  58.4 4.5 %copy-start.2 = (bf16[4,3,4,2,16,256]{5,4,3,2,1,0:T(8,128)(2,1)S(1)}, bf16[4,3,4,2,16,256]{5,4,3,2,1,0:T(8,128)(2,1)}, u32[]{:S(2)}) copy-start(bf16[4,3,4,2,16,256]{5,4,3,2,1,0:T(8,128)(2,1)} %get-tuple-element.22) | copy-start | bytes 2359300
  59.3 6.4 %copy-start.3 = (s32[128,2]{0,1:T(2,128)S(1)}, s32[128,2]{0,1:T(2,128)}, u32[]{:S(2)}) copy-start(s32[128,2]{0,1:T(2,128)} %param.12) | copy-start | bytes 3076
  59.3 6.4 %copy-start.4 = (f32[128,2]{0,1:T(2,128)S(1)}, f32[128,2]{0,1:T(2,128)}, u32[]{:S(2)}) copy-start(f32[128,2]{0,1:T(2,128)} %param.11) | copy-start | bytes 3076
  59.3 6.4 %copy-start.5 = (f32[128]{0:T(128)S(1)}, f32[128]{0:T(128)}, u32[]{:S(2)}) copy-start(f32[128]{0:T(128)} %param.10) | copy-start | bytes 1540
  59.4 6.6 %collective-permute-start.3 = (f32[320,768]{1,0:T(8,128)S(1)}, f32[320,768]{1,0:T(8,128)S(1)}, u32[]{:S(2)}, u32[]{:S(2)}) collective-permute-start(f32[320,768]{1,0:T(8,128)S(1)} %shard_map.87.a_ref), channel_id=1, source_target_pairs={{0,1},{1,0},{2,3},{3,2},{4,5},{5,4},{6,7},{7,6},{8,9},{9,8},{10,11... | collective-permute-start | bytes 2949128 | tf_op jit(solution)/shard_map/ppermute | solution.py:316
  63.8 4.5 %collective-permute-start.4 = (f32[320,768]{1,0:T(8,128)S(1)}, f32[320,768]{1,0:T(8,128)S(1)}, u32[]{:S(2)}, u32[]{:S(2)}) collective-permute-start(f32[320,768]{1,0:T(8,128)S(1)} %shard_map.86.a_ref), channel_id=1, source_target_pairs={{0,1},{1,0},{2,3},{3,2},{4,5},{5,4},{6,7},{7,6},{8,9},{9,8},{10,11... | collective-permute-start | bytes 2949128 | tf_op jit(solution)/shard_map/ppermute | solution.py:316

commit v12 on v11

--- a/solution.py
+++ b/solution.py
@@ -190,36 +190,63 @@
         copy.wait()
 
 
-def project_kernel(in_ref, gate_ref, up_ref, down_ref, out_ref):
-    members = in_ref.shape[0]
+def side_by_side(in_ref, rows):
+    return jnp.concatenate([in_ref[i, rows, :] for i in range(in_ref.shape[0])], axis=1)
+
+
+def first_kernel(in_ref, gate_ref, up_ref, down_ref, own_down_ref, out_ref):
     rows = out_ref.shape[0]
     hidden = gate_ref.shape[1]
-    x = jnp.concatenate([in_ref[i, :rows, :] for i in range(members)], axis=1)
-    out_ref[:, :hidden] = jnp.dot(x, gate_ref[...], preferred_element_type=F32)
-    out_ref[:, hidden : 2 * hidden] = jnp.dot(x, up_ref[...], preferred_element_type=F32)
-    g = jnp.concatenate([in_ref[i, rows:, :] for i in range(members)], axis=1)
-    out_ref[:, 2 * hidden :] = jnp.dot(g, down_ref[...], preferred_element_type=F32)
-
-
-def return_part(a_ref, b_ref, gate_ref, up_ref):
+    x, g = side_by_side(in_ref, slice(0, rows)), side_by_side(in_ref, slice(rows, 2 * rows))
+    pairs = ((x, gate_ref), (x, up_ref), (g, down_ref), (g, own_down_ref))
+    for k, (values, w_ref) in enumerate(pairs):
+        out_ref[:, k * hidden : (k + 1) * hidden] = jnp.dot(
+            values, w_ref[...], preferred_element_type=F32
+        )
+
+
+def second_kernel(in_ref, gate_ref, up_ref, out_ref):
     hidden = gate_ref.shape[1]
-    gate, upper, back = (
-        a_ref[:, k * hidden : (k + 1) * hidden] + b_ref[:, k * hidden : (k + 1) * hidden]
-        for k in range(3)
-    )
+    x = side_by_side(in_ref, slice(0, out_ref.shape[0]))
+    for k, w_ref in enumerate((gate_ref, up_ref)):
+        out_ref[:, k * hidden : (k + 1) * hidden] = jnp.dot(
+            x, w_ref[...], preferred_element_type=F32
+        )
+
+
+def return_part(gate, upper, back, gate_ref, up_ref):
     d_gate, d_upper = backward_tail(gate, upper, back)
     across = (((1,), (1,)), ((), ()))
     part = lax.dot_general(d_gate, gate_ref[...], across, preferred_element_type=F32)
     return part + lax.dot_general(d_upper, up_ref[...], across, preferred_element_type=F32)
 
 
-def return_kernel(a_ref, b_ref, gate_ref, up_ref, out_ref):
-    out_ref[...] = return_part(a_ref, b_ref, gate_ref, up_ref)
-
-
-def return_add_kernel(a_ref, b_ref, gate_ref, up_ref, sum_ref, out_ref):
+def return_kernel(first_ref, second_ref, got_first_ref, gate_ref, up_ref, out_ref):
+    hidden = gate_ref.shape[1]
+    a, b, c, d = (slice(k * hidden, (k + 1) * hidden) for k in range(4))
+    out_ref[...] = return_part(
+        second_ref[:, a] + got_first_ref[:, a],
+        second_ref[:, b] + got_first_ref[:, b],
+        first_ref[:, d] + got_first_ref[:, c],
+        gate_ref,
+        up_ref,
+    )
+
+
+def return_add_kernel(
+    first_ref, got_first_ref, got_second_ref, gate_ref, up_ref, sum_ref, out_ref
+):
     members, _, wide = out_ref.shape
-    part = (return_part(a_ref, b_ref, gate_ref, up_ref) + sum_ref[...]).astype(out_ref.dtype)
+    hidden = gate_ref.shape[1]
+    a, b, c, d = (slice(k * hidden, (k + 1) * hidden) for k in range(4))
+    part = return_part(
+        first_ref[:, a] + got_second_ref[:, a],
+        first_ref[:, b] + got_second_ref[:, b],
+        first_ref[:, c] + got_first_ref[:, d],
+        gate_ref,
+        up_ref,
+    )
+    part = (part + sum_ref[...]).astype(out_ref.dtype)
     for i in range(members):
         out_ref[i] = part[:, i * wide : (i + 1) * wide]
 
@@ -394,18 +421,23 @@
     )
     block = swap(copies, near)
 
-    flops = 2 * rows * members * wide * 3 * hidden
-
-    def project(w):
-        return call(project_kernel, (rows, 3 * hidden), F32, block, *w, flops=flops)
-
-    part_other = project(other)
-    rest_own = other_core(part_other)
-    part_own = project(own)
-    rest_other = other_core(part_own)
-    flops = flops // 3 * 2
+    flops = 2 * rows * members * wide * hidden
+
+    first = call(
+        first_kernel, (rows, 4 * hidden), F32, block, *other, own[2], flops=4 * flops
+    )
+    got_first = other_core(first)
+    second = call(second_kernel, (rows, 2 * hidden), F32, block, *own[:2], flops=2 * flops)
+    got_second = other_core(second)
     part = call(
-        return_kernel, (rows, members * wide), F32, part_own, rest_own, *own[:2], flops=flops
+        return_kernel,
+        (rows, members * wide),
+        F32,
+        first,
+        second,
+        got_first,
+        *own[:2],
+        flops=2 * flops,
     )
     combine = call(
         functools.partial(combine_kernel, capacity, parts),
@@ -420,11 +452,12 @@
         return_add_kernel,
         (members, rows, wide),
         BF16,
-        part_other,
-        rest_other,
+        first,
+        got_first,
+        got_second,
         *other[:2],
         part,
-        flops=flops,
+        flops=2 * flops,
     )
     part = swap(part, near)
     part = call(

time: 105 us -> 105 us (level)
  transfers between devices with their start and end apart: 6 -> 6, of which waited for: 2 -> 2; matrix products, arithmetic and copies ran while one was open for 0% -> 0% of each run, Pallas kernels for 8% -> 7%
where the time goes in v12:
time: 105 us; the launch traced here: 104 us
  blocking collectives  53.6 us (51%)
  starting transfers between devices  31.9 us (30%)
  Pallas kernels  13.1 us (12%)
  waiting for transfers between devices  5.19 us (5%)
    all_to_all x3, blocking collectives, swap(): lax.all_to_all(blocks, AXES, split_axis=0, concat_axis=0, axis_index_grou...  53.6 us
    all_to_all x1, starting transfers between devices, swap(): lax.all_to_all(blocks, AXES, split_axis=0, concat_axis=0, axis_index_grou...  18.1 us
    ppermute x5, starting transfers between devices, other_core(): return lax.ppermute(values, 'c', [(0, 1), (1, 0)])  13.8 us
    pallas_call x2, Pallas kernels, order(): pl.pallas_call(kernel, out_shape=[space(ordered, BF16) for space in space...  6.12 us
    pallas_call x8, Pallas kernels, call(): pl.pallas_call(kernel, out_shape=jax.ShapeDtypeStruct(shape, dtype), in_s...  4.9 us
    all_to_all x1, waiting for transfers between devices, swap(): lax.all_to_all(blocks, AXES, split_axis=0, concat_axis=0, axis_index_grou...  4.11 us
    pallas_call x1, Pallas kernels, shards(): pl.pallas_call(functools.partial(pack_kernel, capacity), out_shape=pltpu....  2.12 us
  transfers between devices with their start and end apart: 6, of which 2 were waited for; matrix products, arithmetic and copies ran while one was open for 0% of the time, Pallas kernels for 7%

profile of v12, /device:TPU:1, one launch (start us, length us, event | category | flops | bytes accessed | tf_op | source)
XLA Modules:
  0.0 104.1 jit_solution(11014848591478254916)
XLA Ops:
  0.0 2.1 %shard_map.82 = bf16[4,8,2,32,128]{4,3,2,1,0:T(8,128)(2,1)} custom-call(s32[2,128]{1,0:T(2,128)} %bitcast.27, bf16[48,128]{1,0:T(8,128)(2,1)} %bitcast.40, bf16[48,128]{1,0:T(8,128)(2,1)} %bitcast.41), custom_call_target="tpu_custom_call" | custom-call | tf_op jit(solution)/shard_map/pallas_call | solution.py:360
  2.1 18.1 %all-to-all-start = ((bf16[64,32,128]{2,1,0:T(8,128)(2,1)}), bf16[64,32,128]{2,1,0:T(8,128)(2,1)S(1)}, u32[]{:S(2)}, u32[]{:S(2)}) async-start(bf16[64,32,128]{2,1,0:T(8,128)(2,1)} %bitcast.38), calls=%async_computation | async-start | bytes 1048576 | tf_op jit(solution)/shard_map/all_to_all | solution.py:337
  20.2 3.4 %shard_map.84 = (bf16[4,3,4,2,16,256]{5,4,3,2,1,0:T(8,128)(2,1)S(1)}, bf16[4,3,4,2,16,256]{5,4,3,2,1,0:T(8,128)(2,1)S(1)}, bf16[4,3,4,2,16,256]{5,4,3,2,1,0:T(8,128)(2,1)S(1)}, bf16[4,3,4,2,16,256]{5,4,3,2,1,0:T(8,128)(2,1)}) custom-call(bf16[4,2,4,2,3,16,256]{6,5,4,3,2,1,0:T(8,128)(2,1)} %bitcast.34, bf16[4,2,4,2,3,16,256]{6,5,4,3,2,1,0:T(8,128)(2,1)} %bitcast.36, ...), custom_call_target="tpu_custom_call" | custom-call | bytes 6291456 | tf_op jit(solution)/shard_map/pallas_call | solution.py:380
  23.6 4.1 %collective-permute-start = (bf16[1536,256]{1,0:T(8,128)(2,1)S(1)}, bf16[1536,256]{1,0:T(8,128)(2,1)S(1)}, u32[]{:S(2)}, u32[]{:S(2)}) collective-permute-start(bf16[1536,256]{1,0:T(8,128)(2,1)S(1)} %bitcast.33), channel_id=1, source_target_pairs={{0,1},{1,0},{2,3},{3,2},{4,5},{5,4},{6,7},{7,6},{8,9},{9,8},{10,11... | collective-permute-start | bytes 2359304 | tf_op jit(solution)/shard_map/ppermute | solution.py:343
  27.8 1.9 %collective-permute-start.1 = (bf16[1536,256]{1,0:T(8,128)(2,1)S(1)}, bf16[1536,256]{1,0:T(8,128)(2,1)S(1)}, u32[]{:S(2)}, u32[]{:S(2)}) collective-permute-start(bf16[1536,256]{1,0:T(8,128)(2,1)S(1)} %bitcast.32), channel_id=1, source_target_pairs={{0,1},{1,0},{2,3},{3,2},{4,5},{5,4},{6,7},{7,6},{8,9},{9,8},{10,11... | collective-permute-start | bytes 2359304 | tf_op jit(solution)/shard_map/ppermute | solution.py:343
  29.7 2.4 %collective-permute-start.2 = (bf16[1536,256]{1,0:T(8,128)(2,1)S(1)}, bf16[1536,256]{1,0:T(8,128)(2,1)S(1)}, u32[]{:S(2)}, u32[]{:S(2)}) collective-permute-start(bf16[1536,256]{1,0:T(8,128)(2,1)S(1)} %bitcast.31), channel_id=1, source_target_pairs={{0,1},{1,0},{2,3},{3,2},{4,5},{5,4},{6,7},{7,6},{8,9},{9,8},{10,11... | collective-permute-start | bytes 2359304 | tf_op jit(solution)/shard_map/ppermute | solution.py:343
  32.1 2.7 %shard_map.83 = (bf16[4,3,4,2,16,256]{5,4,3,2,1,0:T(8,128)(2,1)}, bf16[4,3,4,2,16,256]{5,4,3,2,1,0:T(8,128)(2,1)}) custom-call(bf16[4,2,4,2,3,16,256]{6,5,4,3,2,1,0:T(8,128)(2,1)} %bitcast.35, bf16[4,2,4,2,3,16,256]{6,5,4,3,2,1,0:T(8,128)(2,1)} %bitcast.37), custom_call_target="tpu_custom_call" | custom-call | bytes 6291456 | tf_op jit(solution)/shard_map/pallas_call | solution.py:380
  34.8 0.0 collective-permute-done.gate_ref
  34.8 0.0 collective-permute-done.1.up_ref
  34.8 0.0 collective-permute-done.2.down_ref
  34.9 4.1 %all-to-all-done = bf16[64,32,128]{2,1,0:T(8,128)(2,1)S(1)} async-done(((bf16[64,32,128]{2,1,0:T(8,128)(2,1)}), bf16[64,32,128]{2,1,0:T(8,128)(2,1)S(1)}, u32[]{:S(2)}, u32[]{:S(2)}) %all-to-all-start) | async-done | bytes 524320 | tf_op jit(solution)/shard_map/all_to_all | solution.py:337
  39.0 0.3 shard_map.85
  39.3 0.0 copy-start.2
  39.3 19.2 %all_to_all.20.in_ref = bf16[4,640,384]{2,1,0:T(8,128)(2,1)S(1)} all-to-all(bf16[4,640,384]{2,1,0:T(8,128)(2,1)S(1)} %shard_map.85), channel_id=1, replica_groups={{0,2,8,10},{6,4,14,12},{16,18,24,26},{22,20,30,28},{32,34,40,42},{38,36..., dimensions={0} | all-to-all | bytes 3932160 | tf_op jit(solution)/shard_map/all_to_all | solution.py:337
  58.5 0.0 copy-done.2
  58.5 0.0 copy-start
  58.5 0.0 copy-start.1
  58.5 1.2 %shard_map.86.first_ref = f32[320,1024]{1,0:T(8,128)S(1)} custom-call(bf16[4,640,384]{2,1,0:T(8,128)(2,1)S(1)} %all_to_all.20.in_ref, bf16[1536,256]{1,0:T(8,128)(2,1)S(1)} %collective-permute-done.gate_ref, bf16[1536,256]{1,0:T(8,128)(2,1)S(1)} %collective-permute-done.1.up_ref, bf16[1536,256]{1,0:T(8,128)(2,1)S(1)} %collective-permute-done.2.down_ref, ...), custom_call_target="tpu_custom_call" | custom-call | flops 1006632960 | bytes 6422528 | tf_op jit(solution)/shard_map/pallas_call | solution.py:295
  59.7 0.0 copy-start.3
  59.7 0.0 copy-start.4
  59.7 0.0 copy-start.5
  59.8 3.5 %collective-permute-start.3 = (f32[320,1024]{1,0:T(8,128)S(1)}, f32[320,1024]{1,0:T(8,128)S(1)}, u32[]{:S(2)}, u32[]{:S(2)}) collective-permute-start(f32[320,1024]{1,0:T(8,128)S(1)} %shard_map.86.first_ref), channel_id=1, source_target_pairs={{0,1},{1,0},{2,3},{3,2},{4,5},{5,4},{6,7},{7,6},{8,9},{9,8},{10,11... | collective-permute-start | bytes 3932168 | tf_op jit(solution)/shard_map/ppermute | solution.py:343
  63.2 0.0 copy-done
  63.2 0.0 copy-done.1
  63.2 0.7 shard_map.87.second_ref
  63.9 1.9 %collective-permute-start.4 = (f32[320,512]{1,0:T(8,128)S(1)}, f32[320,512]{1,0:T(8,128)S(1)}, u32[]{:S(2)}, u32[]{:S(2)}) collective-permute-start(f32[320,512]{1,0:T(8,128)S(1)} %shard_map.87.second_ref), channel_id=1, source_target_pairs={{0,1},{1,0},{2,3},{3,2},{4,5},{5,4},{6,7},{7,6},{8,9},{9,8},{10,11... | collective-permute-start | bytes 1966088 | tf_op jit(solution)/shard_map/ppermute | solution.py:343
  65.9 0.0 copy-done.3
  65.9 0.0 copy-done.4
  65.9 0.0 copy-done.5
  65.9 0.2 shard_map.89.combine_ref
  66.1 0.0 collective-permute-done.3.got_first_ref
  66.1 0.7 shard_map.88.sum_ref
  66.8 1.1 %collective-permute-done.4.got_second_ref = f32[320,512]{1,0:T(8,128)S(1)} collective-permute-done((f32[320,512]{1,0:T(8,128)S(1)}, f32[320,512]{1,0:T(8,128)S(1)}, u32[]{:S(2)}, u32[]{:S(2)}) %collective-permute-start.4) | collective-permute-done | bytes 655392 | tf_op jit(solution)/shard_map/ppermute | solution.py:343
  67.9 0.7 shard_map.90
  68.6 13.4 %all_to_all.21.in_ref = bf16[4,320,384]{2,1,0:T(8,128)(2,1)S(1)} all-to-all(bf16[4,320,384]{2,1,0:T(8,128)(2,1)S(1)} %shard_map.90), channel_id=1, replica_groups={{0,2,8,10},{6,4,14,12},{16,18,24,26},{22,20,30,28},{32,34,40,42},{38,36..., dimensions={0} | all-to-all | bytes 1966080 | tf_op jit(solution)/shard_map/all_to_all | solution.py:337
  82.1 0.2 shard_map.91
  82.3 21.0 %all_to_all.22 = bf16[64,16,128]{2,1,0:T(8,128)(2,1)S(1)} all-to-all(bf16[64,16,128]{2,1,0:T(8,128)(2,1)S(1)} %bitcast.25), channel_id=1, replica_groups={{0,6,64,70,128,134,192,198,256,262,320,326,384,390,448,454,16,22,80,86,..., dimensions={0} | all-to-all | bytes 524288 | tf_op jit(solution)/shard_map/all_to_all | solution.py:337
  103.2 0.9 shard_map.92
Async XLA Ops:
  2.1 36.8 %all-to-all-start = ((bf16[64,32,128]{2,1,0:T(8,128)(2,1)}), bf16[64,32,128]{2,1,0:T(8,128)(2,1)S(1)}, u32[]{:S(2)}, u32[]{:S(2)}) async-start(bf16[64,32,128]{2,1,0:T(8,128)(2,1)} %bitcast.38), calls=%async_computation | async-start | bytes 1048576 | tf_op jit(solution)/shard_map/all_to_all | solution.py:337
  23.6 11.2 %collective-permute-start = (bf16[1536,256]{1,0:T(8,128)(2,1)S(1)}, bf16[1536,256]{1,0:T(8,128)(2,1)S(1)}, u32[]{:S(2)}, u32[]{:S(2)}) collective-permute-start(bf16[1536,256]{1,0:T(8,128)(2,1)S(1)} %bitcast.33), channel_id=1, source_target_pairs={{0,1},{1,0},{2,3},{3,2},{4,5},{5,4},{6,7},{7,6},{8,9},{9,8},{10,11... | collective-permute-start | bytes 2359304 | tf_op jit(solution)/shard_map/ppermute | solution.py:343
  27.8 7.1 %collective-permute-start.1 = (bf16[1536,256]{1,0:T(8,128)(2,1)S(1)}, bf16[1536,256]{1,0:T(8,128)(2,1)S(1)}, u32[]{:S(2)}, u32[]{:S(2)}) collective-permute-start(bf16[1536,256]{1,0:T(8,128)(2,1)S(1)} %bitcast.32), channel_id=1, source_target_pairs={{0,1},{1,0},{2,3},{3,2},{4,5},{5,4},{6,7},{7,6},{8,9},{9,8},{10,11... | collective-permute-start | bytes 2359304 | tf_op jit(solution)/shard_map/ppermute | solution.py:343
  29.7 5.2 %collective-permute-start.2 = (bf16[1536,256]{1,0:T(8,128)(2,1)S(1)}, bf16[1536,256]{1,0:T(8,128)(2,1)S(1)}, u32[]{:S(2)}, u32[]{:S(2)}) collective-permute-start(bf16[1536,256]{1,0:T(8,128)(2,1)S(1)} %bitcast.31), channel_id=1, source_target_pairs={{0,1},{1,0},{2,3},{3,2},{4,5},{5,4},{6,7},{7,6},{8,9},{9,8},{10,11... | collective-permute-start | bytes 2359304 | tf_op jit(solution)/shard_map/ppermute | solution.py:343
  39.3 19.2 %copy-start.2 = (bf16[4,3,4,2,16,256]{5,4,3,2,1,0:T(8,128)(2,1)S(1)}, bf16[4,3,4,2,16,256]{5,4,3,2,1,0:T(8,128)(2,1)}, u32[]{:S(2)}) copy-start(bf16[4,3,4,2,16,256]{5,4,3,2,1,0:T(8,128)(2,1)} %get-tuple-element.22) | copy-start | bytes 2359300
  58.5 4.7 %copy-start = (bf16[4,3,4,2,16,256]{5,4,3,2,1,0:T(8,128)(2,1)S(1)}, bf16[4,3,4,2,16,256]{5,4,3,2,1,0:T(8,128)(2,1)}, u32[]{:S(2)}) copy-start(bf16[4,3,4,2,16,256]{5,4,3,2,1,0:T(8,128)(2,1)} %get-tuple-element.20) | copy-start | bytes 2359300
  58.5 4.7 %copy-start.1 = (bf16[4,3,4,2,16,256]{5,4,3,2,1,0:T(8,128)(2,1)S(1)}, bf16[4,3,4,2,16,256]{5,4,3,2,1,0:T(8,128)(2,1)}, u32[]{:S(2)}) copy-start(bf16[4,3,4,2,16,256]{5,4,3,2,1,0:T(8,128)(2,1)} %get-tuple-element.21) | copy-start | bytes 2359300
  59.7 6.1 %copy-start.3 = (s32[128,2]{0,1:T(2,128)S(1)}, s32[128,2]{0,1:T(2,128)}, u32[]{:S(2)}) copy-start(s32[128,2]{0,1:T(2,128)} %param.12) | copy-start | bytes 3076
  59.7 6.1 %copy-start.4 = (f32[128,2]{0,1:T(2,128)S(1)}, f32[128,2]{0,1:T(2,128)}, u32[]{:S(2)}) copy-start(f32[128,2]{0,1:T(2,128)} %param.11) | copy-start | bytes 3076
  59.7 6.1 %copy-start.5 = (f32[128]{0:T(128)S(1)}, f32[128]{0:T(128)}, u32[]{:S(2)}) copy-start(f32[128]{0:T(128)} %param.10) | copy-start | bytes 1540
  59.8 6.4 %collective-permute-start.3 = (f32[320,1024]{1,0:T(8,128)S(1)}, f32[320,1024]{1,0:T(8,128)S(1)}, u32[]{:S(2)}, u32[]{:S(2)}) collective-permute-start(f32[320,1024]{1,0:T(8,128)S(1)} %shard_map.86.first_ref), channel_id=1, source_target_pairs={{0,1},{1,0},{2,3},{3,2},{4,5},{5,4},{6,7},{7,6},{8,9},{9,8},{10,11... | collective-permute-start | bytes 3932168 | tf_op jit(solution)/shard_map/ppermute | solution.py:343
  63.9 4.0 %collective-permute-start.4 = (f32[320,512]{1,0:T(8,128)S(1)}, f32[320,512]{1,0:T(8,128)S(1)}, u32[]{:S(2)}, u32[]{:S(2)}) collective-permute-start(f32[320,512]{1,0:T(8,128)S(1)} %shard_map.87.second_ref), channel_id=1, source_target_pairs={{0,1},{1,0},{2,3},{3,2},{4,5},{5,4},{6,7},{7,6},{8,9},{9,8},{10,11... | collective-permute-start | bytes 1966088 | tf_op jit(solution)/shard_map/ppermute | solution.py:343

commit v13 on v12

--- a/solution.py
+++ b/solution.py
@@ -194,24 +194,20 @@
     return jnp.concatenate([in_ref[i, rows, :] for i in range(in_ref.shape[0])], axis=1)
 
 
-def first_kernel(in_ref, gate_ref, up_ref, down_ref, own_down_ref, out_ref):
+def first_kernel(in_ref, gate_ref, up_ref, down_ref, own_down_ref, own_gate_ref, out_ref):
     rows = out_ref.shape[0]
     hidden = gate_ref.shape[1]
     x, g = side_by_side(in_ref, slice(0, rows)), side_by_side(in_ref, slice(rows, 2 * rows))
-    pairs = ((x, gate_ref), (x, up_ref), (g, down_ref), (g, own_down_ref))
+    pairs = ((x, gate_ref), (x, up_ref), (g, down_ref), (g, own_down_ref), (x, own_gate_ref))
     for k, (values, w_ref) in enumerate(pairs):
         out_ref[:, k * hidden : (k + 1) * hidden] = jnp.dot(
             values, w_ref[...], preferred_element_type=F32
         )
 
 
-def second_kernel(in_ref, gate_ref, up_ref, out_ref):
-    hidden = gate_ref.shape[1]
+def second_kernel(in_ref, up_ref, out_ref):
     x = side_by_side(in_ref, slice(0, out_ref.shape[0]))
-    for k, w_ref in enumerate((gate_ref, up_ref)):
-        out_ref[:, k * hidden : (k + 1) * hidden] = jnp.dot(
-            x, w_ref[...], preferred_element_type=F32
-        )
+    out_ref[...] = jnp.dot(x, up_ref[...], preferred_element_type=F32)
 
 
 def return_part(gate, upper, back, gate_ref, up_ref):
@@ -223,10 +219,10 @@
 
 def return_kernel(first_ref, second_ref, got_first_ref, gate_ref, up_ref, out_ref):
     hidden = gate_ref.shape[1]
-    a, b, c, d = (slice(k * hidden, (k + 1) * hidden) for k in range(4))
+    a, b, c, d, e = (slice(k * hidden, (k + 1) * hidden) for k in range(5))
     out_ref[...] = return_part(
-        second_ref[:, a] + got_first_ref[:, a],
-        second_ref[:, b] + got_first_ref[:, b],
+        first_ref[:, e] + got_first_ref[:, a],
+        second_ref[...] + got_first_ref[:, b],
         first_ref[:, d] + got_first_ref[:, c],
         gate_ref,
         up_ref,
@@ -238,10 +234,10 @@
 ):
     members, _, wide = out_ref.shape
     hidden = gate_ref.shape[1]
-    a, b, c, d = (slice(k * hidden, (k + 1) * hidden) for k in range(4))
+    a, b, c, d, e = (slice(k * hidden, (k + 1) * hidden) for k in range(5))
     part = return_part(
-        first_ref[:, a] + got_second_ref[:, a],
-        first_ref[:, b] + got_second_ref[:, b],
+        first_ref[:, a] + got_first_ref[:, e],
+        first_ref[:, b] + got_second_ref[...],
         first_ref[:, c] + got_first_ref[:, d],
         gate_ref,
         up_ref,
@@ -424,10 +420,10 @@
     flops = 2 * rows * members * wide * hidden
 
     first = call(
-        first_kernel, (rows, 4 * hidden), F32, block, *other, own[2], flops=4 * flops
+        first_kernel, (rows, 5 * hidden), F32, block, *other, own[2], own[0], flops=5 * flops
     )
     got_first = other_core(first)
-    second = call(second_kernel, (rows, 2 * hidden), F32, block, *own[:2], flops=2 * flops)
+    second = call(second_kernel, (rows, hidden), F32, block, own[1], flops=flops)
     got_second = other_core(second)
     part = call(
         return_kernel,

time: 105 us -> 104 us (level)
  transfers between devices with their start and end apart: 6 -> 6, of which waited for: 2 -> 3; matrix products, arithmetic and copies ran while one was open for 0% -> 0% of each run, Pallas kernels for 7% -> 7%
where the time goes in v13:
time: 104 us
  blocking collectives  53.5 us (51%)
  starting transfers between devices  31.9 us (31%)
  Pallas kernels  13.2 us (13%)
  waiting for transfers between devices  4.73 us (5%)
    all_to_all x3, blocking collectives, swap(): lax.all_to_all(blocks, AXES, split_axis=0, concat_axis=0, axis_index_grou...  53.5 us
    all_to_all x1, starting transfers between devices, swap(): lax.all_to_all(blocks, AXES, split_axis=0, concat_axis=0, axis_index_grou...  18.1 us
    ppermute x5, starting transfers between devices, other_core(): return lax.ppermute(values, 'c', [(0, 1), (1, 0)])  13.8 us
    pallas_call x2, Pallas kernels, order(): pl.pallas_call(kernel, out_shape=[space(ordered, BF16) for space in space...  6.12 us
    pallas_call x8, Pallas kernels, call(): pl.pallas_call(kernel, out_shape=jax.ShapeDtypeStruct(shape, dtype), in_s...  4.92 us
    all_to_all x1, waiting for transfers between devices, swap(): lax.all_to_all(blocks, AXES, split_axis=0, concat_axis=0, axis_index_grou...  4.11 us
    pallas_call x1, Pallas kernels, shards(): pl.pallas_call(functools.partial(pack_kernel, capacity), out_shape=pltpu....  2.12 us
  transfers between devices with their start and end apart: 6, of which 3 were waited for; matrix products, arithmetic and copies ran while one was open for 0% of the time, Pallas kernels for 7%

profile of v13, /device:TPU:1, one launch (start us, length us, event | category | flops | bytes accessed | tf_op | source)
XLA Modules:
  0.0 103.6 jit_solution(13924703325992499350)
XLA Ops:
  0.0 2.1 %shard_map.82 = bf16[4,8,2,32,128]{4,3,2,1,0:T(8,128)(2,1)} custom-call(s32[2,128]{1,0:T(2,128)} %bitcast.27, bf16[48,128]{1,0:T(8,128)(2,1)} %bitcast.40, bf16[48,128]{1,0:T(8,128)(2,1)} %bitcast.41), custom_call_target="tpu_custom_call" | custom-call | tf_op jit(solution)/shard_map/pallas_call | solution.py:356
  2.1 18.1 %all-to-all-start = ((bf16[64,32,128]{2,1,0:T(8,128)(2,1)}), bf16[64,32,128]{2,1,0:T(8,128)(2,1)S(1)}, u32[]{:S(2)}, u32[]{:S(2)}) async-start(bf16[64,32,128]{2,1,0:T(8,128)(2,1)} %bitcast.38), calls=%async_computation | async-start | bytes 1048576 | tf_op jit(solution)/shard_map/all_to_all | solution.py:333
  20.2 3.4 %shard_map.84 = (bf16[4,3,4,2,16,256]{5,4,3,2,1,0:T(8,128)(2,1)S(1)}, bf16[4,3,4,2,16,256]{5,4,3,2,1,0:T(8,128)(2,1)S(1)}, bf16[4,3,4,2,16,256]{5,4,3,2,1,0:T(8,128)(2,1)S(1)}, bf16[4,3,4,2,16,256]{5,4,3,2,1,0:T(8,128)(2,1)}) custom-call(bf16[4,2,4,2,3,16,256]{6,5,4,3,2,1,0:T(8,128)(2,1)} %bitcast.34, bf16[4,2,4,2,3,16,256]{6,5,4,3,2,1,0:T(8,128)(2,1)} %bitcast.36, ...), custom_call_target="tpu_custom_call" | custom-call | bytes 6291456 | tf_op jit(solution)/shard_map/pallas_call | solution.py:376
  23.6 4.1 %collective-permute-start = (bf16[1536,256]{1,0:T(8,128)(2,1)S(1)}, bf16[1536,256]{1,0:T(8,128)(2,1)S(1)}, u32[]{:S(2)}, u32[]{:S(2)}) collective-permute-start(bf16[1536,256]{1,0:T(8,128)(2,1)S(1)} %bitcast.33), channel_id=1, source_target_pairs={{0,1},{1,0},{2,3},{3,2},{4,5},{5,4},{6,7},{7,6},{8,9},{9,8},{10,11... | collective-permute-start | bytes 2359304 | tf_op jit(solution)/shard_map/ppermute | solution.py:339
  27.8 1.9 %collective-permute-start.1 = (bf16[1536,256]{1,0:T(8,128)(2,1)S(1)}, bf16[1536,256]{1,0:T(8,128)(2,1)S(1)}, u32[]{:S(2)}, u32[]{:S(2)}) collective-permute-start(bf16[1536,256]{1,0:T(8,128)(2,1)S(1)} %bitcast.32), channel_id=1, source_target_pairs={{0,1},{1,0},{2,3},{3,2},{4,5},{5,4},{6,7},{7,6},{8,9},{9,8},{10,11... | collective-permute-start | bytes 2359304 | tf_op jit(solution)/shard_map/ppermute | solution.py:339
  29.7 2.4 %collective-permute-start.2 = (bf16[1536,256]{1,0:T(8,128)(2,1)S(1)}, bf16[1536,256]{1,0:T(8,128)(2,1)S(1)}, u32[]{:S(2)}, u32[]{:S(2)}) collective-permute-start(bf16[1536,256]{1,0:T(8,128)(2,1)S(1)} %bitcast.31), channel_id=1, source_target_pairs={{0,1},{1,0},{2,3},{3,2},{4,5},{5,4},{6,7},{7,6},{8,9},{9,8},{10,11... | collective-permute-start | bytes 2359304 | tf_op jit(solution)/shard_map/ppermute | solution.py:339
  32.1 2.7 %shard_map.83 = (bf16[4,3,4,2,16,256]{5,4,3,2,1,0:T(8,128)(2,1)}, bf16[4,3,4,2,16,256]{5,4,3,2,1,0:T(8,128)(2,1)}) custom-call(bf16[4,2,4,2,3,16,256]{6,5,4,3,2,1,0:T(8,128)(2,1)} %bitcast.35, bf16[4,2,4,2,3,16,256]{6,5,4,3,2,1,0:T(8,128)(2,1)} %bitcast.37), custom_call_target="tpu_custom_call" | custom-call | bytes 6291456 | tf_op jit(solution)/shard_map/pallas_call | solution.py:376
  34.8 0.0 collective-permute-done.gate_ref
  34.8 0.0 collective-permute-done.1.up_ref
  34.9 0.0 collective-permute-done.2.down_ref
  34.9 4.1 %all-to-all-done = bf16[64,32,128]{2,1,0:T(8,128)(2,1)S(1)} async-done(((bf16[64,32,128]{2,1,0:T(8,128)(2,1)}), bf16[64,32,128]{2,1,0:T(8,128)(2,1)S(1)}, u32[]{:S(2)}, u32[]{:S(2)}) %all-to-all-start) | async-done | bytes 524320 | tf_op jit(solution)/shard_map/all_to_all | solution.py:333
  39.0 0.3 shard_map.85
  39.3 0.0 copy-start
  39.3 0.0 copy-start.2
  39.3 19.2 %all_to_all.20.in_ref = bf16[4,640,384]{2,1,0:T(8,128)(2,1)S(1)} all-to-all(bf16[4,640,384]{2,1,0:T(8,128)(2,1)S(1)} %shard_map.85), channel_id=1, replica_groups={{0,2,8,10},{6,4,14,12},{16,18,24,26},{22,20,30,28},{32,34,40,42},{38,36..., dimensions={0} | all-to-all | bytes 3932160 | tf_op jit(solution)/shard_map/all_to_all | solution.py:333
  58.5 0.0 copy-done
  58.5 0.0 copy-done.2
  58.5 0.0 copy-start.1
  58.5 1.5 %shard_map.86.first_ref = f32[320,1280]{1,0:T(8,128)S(1)} custom-call(bf16[4,640,384]{2,1,0:T(8,128)(2,1)S(1)} %all_to_all.20.in_ref, bf16[1536,256]{1,0:T(8,128)(2,1)S(1)} %collective-permute-done.gate_ref, bf16[1536,256]{1,0:T(8,128)(2,1)S(1)} %collective-permute-done.1.up_ref, bf16[1536,256]{1,0:T(8,128)(2,1)S(1)} %collective-permute-done.2.down_ref, ...), custom_call_target="tpu_custom_call" | custom-call | flops 1258291200 | bytes 7536640 | tf_op jit(solution)/shard_map/pallas_call | solution.py:291
  60.0 0.0 copy-start.3
  60.0 0.0 copy-start.4
  60.0 0.0 copy-start.5
  60.0 3.5 %collective-permute-start.3 = (f32[320,1280]{1,0:T(8,128)S(1)}, f32[320,1280]{1,0:T(8,128)S(1)}, u32[]{:S(2)}, u32[]{:S(2)}) collective-permute-start(f32[320,1280]{1,0:T(8,128)S(1)} %shard_map.86.first_ref), channel_id=1, source_target_pairs={{0,1},{1,0},{2,3},{3,2},{4,5},{5,4},{6,7},{7,6},{8,9},{9,8},{10,11... | collective-permute-start | bytes 4915208 | tf_op jit(solution)/shard_map/ppermute | solution.py:339
  63.5 0.0 copy-done.1
  63.5 0.4 shard_map.87.second_ref
  63.9 1.9 %collective-permute-start.4 = (f32[320,256]{1,0:T(8,128)S(1)}, f32[320,256]{1,0:T(8,128)S(1)}, u32[]{:S(2)}, u32[]{:S(2)}) collective-permute-start(f32[320,256]{1,0:T(8,128)S(1)} %shard_map.87.second_ref), channel_id=1, source_target_pairs={{0,1},{1,0},{2,3},{3,2},{4,5},{5,4},{6,7},{7,6},{8,9},{9,8},{10,11... | collective-permute-start | bytes 983048 | tf_op jit(solution)/shard_map/ppermute | solution.py:339
  65.9 0.0 copy-done.3
  65.9 0.0 copy-done.4
  65.9 0.0 copy-done.5
  65.9 0.2 shard_map.89.combine_ref
  66.1 0.5 collective-permute-done.3.got_first_ref
  66.6 0.7 shard_map.88.sum_ref
  67.3 0.1 collective-permute-done.4.got_second_ref
  67.5 0.7 shard_map.90
  68.2 13.4 %all_to_all.21.in_ref = bf16[4,320,384]{2,1,0:T(8,128)(2,1)S(1)} all-to-all(bf16[4,320,384]{2,1,0:T(8,128)(2,1)S(1)} %shard_map.90), channel_id=1, replica_groups={{0,2,8,10},{6,4,14,12},{16,18,24,26},{22,20,30,28},{32,34,40,42},{38,36..., dimensions={0} | all-to-all | bytes 1966080 | tf_op jit(solution)/shard_map/all_to_all | solution.py:333
  81.6 0.2 shard_map.91
  81.8 20.9 %all_to_all.22 = bf16[64,16,128]{2,1,0:T(8,128)(2,1)S(1)} all-to-all(bf16[64,16,128]{2,1,0:T(8,128)(2,1)S(1)} %bitcast.25), channel_id=1, replica_groups={{0,6,64,70,128,134,192,198,256,262,320,326,384,390,448,454,16,22,80,86,..., dimensions={0} | all-to-all | bytes 524288 | tf_op jit(solution)/shard_map/all_to_all | solution.py:333
  102.7 0.9 shard_map.92
Async XLA Ops:
  2.1 36.8 %all-to-all-start = ((bf16[64,32,128]{2,1,0:T(8,128)(2,1)}), bf16[64,32,128]{2,1,0:T(8,128)(2,1)S(1)}, u32[]{:S(2)}, u32[]{:S(2)}) async-start(bf16[64,32,128]{2,1,0:T(8,128)(2,1)} %bitcast.38), calls=%async_computation | async-start | bytes 1048576 | tf_op jit(solution)/shard_map/all_to_all | solution.py:333
  23.6 11.2 %collective-permute-start = (bf16[1536,256]{1,0:T(8,128)(2,1)S(1)}, bf16[1536,256]{1,0:T(8,128)(2,1)S(1)}, u32[]{:S(2)}, u32[]{:S(2)}) collective-permute-start(bf16[1536,256]{1,0:T(8,128)(2,1)S(1)} %bitcast.33), channel_id=1, source_target_pairs={{0,1},{1,0},{2,3},{3,2},{4,5},{5,4},{6,7},{7,6},{8,9},{9,8},{10,11... | collective-permute-start | bytes 2359304 | tf_op jit(solution)/shard_map/ppermute | solution.py:339
  27.8 7.1 %collective-permute-start.1 = (bf16[1536,256]{1,0:T(8,128)(2,1)S(1)}, bf16[1536,256]{1,0:T(8,128)(2,1)S(1)}, u32[]{:S(2)}, u32[]{:S(2)}) collective-permute-start(bf16[1536,256]{1,0:T(8,128)(2,1)S(1)} %bitcast.32), channel_id=1, source_target_pairs={{0,1},{1,0},{2,3},{3,2},{4,5},{5,4},{6,7},{7,6},{8,9},{9,8},{10,11... | collective-permute-start | bytes 2359304 | tf_op jit(solution)/shard_map/ppermute | solution.py:339
  29.7 5.2 %collective-permute-start.2 = (bf16[1536,256]{1,0:T(8,128)(2,1)S(1)}, bf16[1536,256]{1,0:T(8,128)(2,1)S(1)}, u32[]{:S(2)}, u32[]{:S(2)}) collective-permute-start(bf16[1536,256]{1,0:T(8,128)(2,1)S(1)} %bitcast.31), channel_id=1, source_target_pairs={{0,1},{1,0},{2,3},{3,2},{4,5},{5,4},{6,7},{7,6},{8,9},{9,8},{10,11... | collective-permute-start | bytes 2359304 | tf_op jit(solution)/shard_map/ppermute | solution.py:339
  39.3 19.2 %copy-start = (bf16[4,3,4,2,16,256]{5,4,3,2,1,0:T(8,128)(2,1)S(1)}, bf16[4,3,4,2,16,256]{5,4,3,2,1,0:T(8,128)(2,1)}, u32[]{:S(2)}) copy-start(bf16[4,3,4,2,16,256]{5,4,3,2,1,0:T(8,128)(2,1)} %get-tuple-element.20) | copy-start | bytes 2359300
  39.3 19.2 %copy-start.2 = (bf16[4,3,4,2,16,256]{5,4,3,2,1,0:T(8,128)(2,1)S(1)}, bf16[4,3,4,2,16,256]{5,4,3,2,1,0:T(8,128)(2,1)}, u32[]{:S(2)}) copy-start(bf16[4,3,4,2,16,256]{5,4,3,2,1,0:T(8,128)(2,1)} %get-tuple-element.22) | copy-start | bytes 2359300
  58.5 5.0 %copy-start.1 = (bf16[4,3,4,2,16,256]{5,4,3,2,1,0:T(8,128)(2,1)S(1)}, bf16[4,3,4,2,16,256]{5,4,3,2,1,0:T(8,128)(2,1)}, u32[]{:S(2)}) copy-start(bf16[4,3,4,2,16,256]{5,4,3,2,1,0:T(8,128)(2,1)} %get-tuple-element.21) | copy-start | bytes 2359300
  60.0 5.9 %copy-start.3 = (s32[128,2]{0,1:T(2,128)S(1)}, s32[128,2]{0,1:T(2,128)}, u32[]{:S(2)}) copy-start(s32[128,2]{0,1:T(2,128)} %param.12) | copy-start | bytes 3076
  60.0 5.9 %copy-start.4 = (f32[128,2]{0,1:T(2,128)S(1)}, f32[128,2]{0,1:T(2,128)}, u32[]{:S(2)}) copy-start(f32[128,2]{0,1:T(2,128)} %param.11) | copy-start | bytes 3076
  60.0 5.9 %copy-start.5 = (f32[128]{0:T(128)S(1)}, f32[128]{0:T(128)}, u32[]{:S(2)}) copy-start(f32[128]{0:T(128)} %param.10) | copy-start | bytes 1540
  60.0 6.6 %collective-permute-start.3 = (f32[320,1280]{1,0:T(8,128)S(1)}, f32[320,1280]{1,0:T(8,128)S(1)}, u32[]{:S(2)}, u32[]{:S(2)}) collective-permute-start(f32[320,1280]{1,0:T(8,128)S(1)} %shard_map.86.first_ref), channel_id=1, source_target_pairs={{0,1},{1,0},{2,3},{3,2},{4,5},{5,4},{6,7},{7,6},{8,9},{9,8},{10,11... | collective-permute-start | bytes 4915208 | tf_op jit(solution)/shard_map/ppermute | solution.py:339
  63.9 3.5 %collective-permute-start.4 = (f32[320,256]{1,0:T(8,128)S(1)}, f32[320,256]{1,0:T(8,128)S(1)}, u32[]{:S(2)}, u32[]{:S(2)}) collective-permute-start(f32[320,256]{1,0:T(8,128)S(1)} %shard_map.87.second_ref), channel_id=1, source_target_pairs={{0,1},{1,0},{2,3},{3,2},{4,5},{5,4},{6,7},{7,6},{8,9},{9,8},{10,11... | collective-permute-start | bytes 983048 | tf_op jit(solution)/shard_map/ppermute | solution.py:339

commit v14 on v13

--- a/solution.py
+++ b/solution.py
@@ -153,7 +153,9 @@
     return copies
 
 
-def sent_kernel(gate_hbm, up_hbm, down_hbm, gate_ref, up_ref, down_ref, own_hbm, raw, turned, sems):
+def sent_kernel(
+    gate_hbm, up_hbm, down_hbm, gate_ref, up_ref, down_ref, own_down, own_gate, raw, turned, held, sems
+):
     core = lax.axis_index("c")
     chunks, _, width = raw.shape
     loads = [
@@ -165,29 +167,27 @@
     each = 6 * gate_hbm.shape[4]
     waits = gather(gate_hbm, 1 - core, gate_ref, sems, chunks)
     waits += gather(up_hbm, 1 - core, up_ref, sems, chunks + each)
+    own = gather(gate_hbm, core, held, sems, chunks + 4 * each)
     for k, copy in enumerate(loads):
         copy.wait()
         turned[k] = raw[k].T.reshape(turned.shape[1:])
     waits += gather(turned, 1 - core, down_ref, sems, chunks + 2 * each)
-    waits += gather(turned, core, own_hbm, sems, chunks + 3 * each)
+    waits += gather(turned, core, own_down, sems, chunks + 3 * each)
+    for copy in own:
+        copy.wait()
+    waits.append(pltpu.make_async_copy(held, own_gate, sems.at[chunks + 5 * each]))
+    waits[-1].start()
     for copy in waits:
         copy.wait()
 
 
-def own_kernel(gate_hbm, up_hbm, own_gate, own_up, held, sems):
-    core = lax.axis_index("c")
-    each = 6 * gate_hbm.shape[4]
-    parts = [
-        gather(src, core, held.at[k], sems, k * each) for k, src in enumerate((gate_hbm, up_hbm))
-    ]
-    waits = []
-    for k, out in enumerate((own_gate, own_up)):
-        for copy in parts[k]:
-            copy.wait()
-        waits.append(pltpu.make_async_copy(held.at[k], out, sems.at[2 * each + k]))
-        waits[-1].start()
-    for copy in waits:
+def own_kernel(up_hbm, own_up, held, sems):
+    copies = gather(up_hbm, lax.axis_index("c"), held, sems, 0)
+    for copy in copies:
         copy.wait()
+    whole = pltpu.make_async_copy(held, own_up, sems.at[len(copies)])
+    whole.start()
+    whole.wait()
 
 
 def side_by_side(in_ref, rows):
@@ -386,26 +386,26 @@
         )(*sources)
         return [w.reshape(members * wide, hidden) for w in ordered_weights]
 
-    *sent, own_down = order(
+    *sent, own_down, own_gate = order(
         sent_kernel,
-        [pltpu.VMEM] * 3 + [pltpu.HBM],
+        [pltpu.VMEM] * 3 + [pltpu.HBM] * 2,
         [
             pltpu.VMEM((chunks, hidden, down.shape[1] // chunks), BF16),
             pltpu.VMEM(views, BF16),
-            pltpu.SemaphoreType.DMA((chunks + 4 * each,)),
+            pltpu.VMEM(ordered, BF16),
+            pltpu.SemaphoreType.DMA((chunks + 5 * each + 1,)),
         ],
         gate,
         up,
         down,
     )
-    own = order(
+    (own_up,) = order(
         own_kernel,
-        [pltpu.HBM] * 2,
-        [pltpu.VMEM((2,) + ordered, BF16), pltpu.SemaphoreType.DMA((2 * each + 2,))],
-        gate,
+        [pltpu.HBM],
+        [pltpu.VMEM(ordered, BF16), pltpu.SemaphoreType.DMA((each + 1,))],
         up,
     )
-    own = [*own, own_down]
+    own = [own_gate, own_up, own_down]
     other = [other_core(w) for w in sent]
     got, own, other = lax.optimization_barrier((got, own, other))
 

time: 104 us -> 104 us (level)
  no operation moved by 1% of the time
where the time goes in v14:
time: 104 us
  blocking collectives  53.5 us (51%)
  starting transfers between devices  31.9 us (31%)
  Pallas kernels  13.1 us (13%)
  waiting for transfers between devices  4.77 us (5%)
    all_to_all x3, blocking collectives, swap(): lax.all_to_all(blocks, AXES, split_axis=0, concat_axis=0, axis_index_grou...  53.5 us
    all_to_all x1, starting transfers between devices, swap(): lax.all_to_all(blocks, AXES, split_axis=0, concat_axis=0, axis_index_grou...  18.1 us
    ppermute x5, starting transfers between devices, other_core(): return lax.ppermute(values, 'c', [(0, 1), (1, 0)])  13.8 us
    pallas_call x2, Pallas kernels, order(): pl.pallas_call(kernel, out_shape=[space(ordered, BF16) for space in space...  6.08 us
    pallas_call x8, Pallas kernels, call(): pl.pallas_call(kernel, out_shape=jax.ShapeDtypeStruct(shape, dtype), in_s...  4.91 us
    all_to_all x1, waiting for transfers between devices, swap(): lax.all_to_all(blocks, AXES, split_axis=0, concat_axis=0, axis_index_grou...  4.15 us
    pallas_call x1, Pallas kernels, shards(): pl.pallas_call(functools.partial(pack_kernel, capacity), out_shape=pltpu....  2.12 us
  transfers between devices with their start and end apart: 6, of which 3 were waited for; matrix products, arithmetic and copies ran while one was open for 0% of the time, Pallas kernels for 7%

profile of v14, /device:TPU:1, one launch (start us, length us, event | category | flops | bytes accessed | tf_op | source)
XLA Modules:
  0.0 103.6 jit_solution(1274451892803474538)
XLA Ops:
  0.0 2.1 %shard_map.82 = bf16[4,8,2,32,128]{4,3,2,1,0:T(8,128)(2,1)} custom-call(s32[2,128]{1,0:T(2,128)} %bitcast.27, bf16[48,128]{1,0:T(8,128)(2,1)} %bitcast.39, bf16[48,128]{1,0:T(8,128)(2,1)} %bitcast.40), custom_call_target="tpu_custom_call" | custom-call | tf_op jit(solution)/shard_map/pallas_call | solution.py:356
  2.1 18.1 %all-to-all-start = ((bf16[64,32,128]{2,1,0:T(8,128)(2,1)}), bf16[64,32,128]{2,1,0:T(8,128)(2,1)S(1)}, u32[]{:S(2)}, u32[]{:S(2)}) async-start(bf16[64,32,128]{2,1,0:T(8,128)(2,1)} %bitcast.36), calls=%async_computation | async-start | bytes 1048576 | tf_op jit(solution)/shard_map/all_to_all | solution.py:333
  20.2 3.9 %shard_map.83 = (bf16[4,3,4,2,16,256]{5,4,3,2,1,0:T(8,128)(2,1)S(1)}, bf16[4,3,4,2,16,256]{5,4,3,2,1,0:T(8,128)(2,1)S(1)}, bf16[4,3,4,2,16,256]{5,4,3,2,1,0:T(8,...) custom-call(bf16[4,2,4,2,3,16,256]{6,5,4,3,2,1,0:T(8,128)(2,1)} %bitcast.37, ...), custom_call_target="tpu_custom_call" | custom-call | bytes 6291456 | tf_op jit(solution)/shard_map/pallas_call | solution.py:376
  24.1 4.1 %collective-permute-start = (bf16[1536,256]{1,0:T(8,128)(2,1)S(1)}, bf16[1536,256]{1,0:T(8,128)(2,1)S(1)}, u32[]{:S(2)}, u32[]{:S(2)}) collective-permute-start(bf16[1536,256]{1,0:T(8,128)(2,1)S(1)} %bitcast.33), channel_id=1, source_target_pairs={{0,1},{1,0},{2,3},{3,2},{4,5},{5,4},{6,7},{7,6},{8,9},{9,8},{10,11... | collective-permute-start | bytes 2359304 | tf_op jit(solution)/shard_map/ppermute | solution.py:339
  28.2 1.9 %collective-permute-start.1 = (bf16[1536,256]{1,0:T(8,128)(2,1)S(1)}, bf16[1536,256]{1,0:T(8,128)(2,1)S(1)}, u32[]{:S(2)}, u32[]{:S(2)}) collective-permute-start(bf16[1536,256]{1,0:T(8,128)(2,1)S(1)} %bitcast.32), channel_id=1, source_target_pairs={{0,1},{1,0},{2,3},{3,2},{4,5},{5,4},{6,7},{7,6},{8,9},{9,8},{10,11... | collective-permute-start | bytes 2359304 | tf_op jit(solution)/shard_map/ppermute | solution.py:339
  30.1 2.4 %collective-permute-start.2 = (bf16[1536,256]{1,0:T(8,128)(2,1)S(1)}, bf16[1536,256]{1,0:T(8,128)(2,1)S(1)}, u32[]{:S(2)}, u32[]{:S(2)}) collective-permute-start(bf16[1536,256]{1,0:T(8,128)(2,1)S(1)} %bitcast.31), channel_id=1, source_target_pairs={{0,1},{1,0},{2,3},{3,2},{4,5},{5,4},{6,7},{7,6},{8,9},{9,8},{10,11... | collective-permute-start | bytes 2359304 | tf_op jit(solution)/shard_map/ppermute | solution.py:339
  32.6 2.2 %shard_map.84 = bf16[4,3,4,2,16,256]{5,4,3,2,1,0:T(8,128)(2,1)} custom-call(bf16[4,2,4,2,3,16,256]{6,5,4,3,2,1,0:T(8,128)(2,1)} %bitcast.35), custom_call_target="tpu_custom_call" | custom-call | bytes 6291456 | tf_op jit(solution)/shard_map/pallas_call | solution.py:376
  34.8 0.0 collective-permute-done.gate_ref
  34.8 0.0 collective-permute-done.1.up_ref
  34.8 0.0 collective-permute-done.2.down_ref
  34.8 4.1 %all-to-all-done = bf16[64,32,128]{2,1,0:T(8,128)(2,1)S(1)} async-done(((bf16[64,32,128]{2,1,0:T(8,128)(2,1)}), bf16[64,32,128]{2,1,0:T(8,128)(2,1)S(1)}, u32[]{:S(2)}, u32[]{:S(2)}) %all-to-all-start) | async-done | bytes 524320 | tf_op jit(solution)/shard_map/all_to_all | solution.py:333
  39.0 0.3 shard_map.85
  39.3 0.0 copy-start.1
  39.3 0.0 copy-start.2
  39.3 19.2 %all_to_all.20.in_ref = bf16[4,640,384]{2,1,0:T(8,128)(2,1)S(1)} all-to-all(bf16[4,640,384]{2,1,0:T(8,128)(2,1)S(1)} %shard_map.85), channel_id=1, replica_groups={{0,2,8,10},{6,4,14,12},{16,18,24,26},{22,20,30,28},{32,34,40,42},{38,36..., dimensions={0} | all-to-all | bytes 3932160 | tf_op jit(solution)/shard_map/all_to_all | solution.py:333
  58.5 0.0 copy-done.1
  58.5 0.0 copy-done.2
  58.5 0.0 copy-start
  58.5 1.5 %shard_map.86.first_ref = f32[320,1280]{1,0:T(8,128)S(1)} custom-call(bf16[4,640,384]{2,1,0:T(8,128)(2,1)S(1)} %all_to_all.20.in_ref, bf16[1536,256]{1,0:T(8,128)(2,1)S(1)} %collective-permute-done.gate_ref, bf16[1536,256]{1,0:T(8,128)(2,1)S(1)} %collective-permute-done.1.up_ref, bf16[1536,256]{1,0:T(8,128)(2,1)S(1)} %collective-permute-done.2.down_ref, ...), custom_call_target="tpu_custom_call" | custom-call | flops 1258291200 | bytes 7536640 | tf_op jit(solution)/shard_map/pallas_call | solution.py:291
  60.0 0.0 copy-start.3
  60.0 0.0 copy-start.4
  60.0 0.0 copy-start.5
  60.0 3.5 %collective-permute-start.3 = (f32[320,1280]{1,0:T(8,128)S(1)}, f32[320,1280]{1,0:T(8,128)S(1)}, u32[]{:S(2)}, u32[]{:S(2)}) collective-permute-start(f32[320,1280]{1,0:T(8,128)S(1)} %shard_map.86.first_ref), channel_id=1, source_target_pairs={{0,1},{1,0},{2,3},{3,2},{4,5},{5,4},{6,7},{7,6},{8,9},{9,8},{10,11... | collective-permute-start | bytes 4915208 | tf_op jit(solution)/shard_map/ppermute | solution.py:339
  63.5 0.0 copy-done
  63.5 0.4 shard_map.87.second_ref
  63.9 1.9 %collective-permute-start.4 = (f32[320,256]{1,0:T(8,128)S(1)}, f32[320,256]{1,0:T(8,128)S(1)}, u32[]{:S(2)}, u32[]{:S(2)}) collective-permute-start(f32[320,256]{1,0:T(8,128)S(1)} %shard_map.87.second_ref), channel_id=1, source_target_pairs={{0,1},{1,0},{2,3},{3,2},{4,5},{5,4},{6,7},{7,6},{8,9},{9,8},{10,11... | collective-permute-start | bytes 983048 | tf_op jit(solution)/shard_map/ppermute | solution.py:339
  65.9 0.0 copy-done.3
  65.9 0.0 copy-done.4
  65.9 0.0 copy-done.5
  65.9 0.2 shard_map.89.combine_ref
  66.1 0.5 collective-permute-done.3.got_first_ref
  66.6 0.7 shard_map.88.sum_ref
  67.3 0.1 collective-permute-done.4.got_second_ref
  67.5 0.7 shard_map.90
  68.2 13.4 %all_to_all.21.in_ref = bf16[4,320,384]{2,1,0:T(8,128)(2,1)S(1)} all-to-all(bf16[4,320,384]{2,1,0:T(8,128)(2,1)S(1)} %shard_map.90), channel_id=1, replica_groups={{0,2,8,10},{6,4,14,12},{16,18,24,26},{22,20,30,28},{32,34,40,42},{38,36..., dimensions={0} | all-to-all | bytes 1966080 | tf_op jit(solution)/shard_map/all_to_all | solution.py:333
  81.6 0.2 shard_map.91
  81.8 20.9 %all_to_all.22 = bf16[64,16,128]{2,1,0:T(8,128)(2,1)S(1)} all-to-all(bf16[64,16,128]{2,1,0:T(8,128)(2,1)S(1)} %bitcast.25), channel_id=1, replica_groups={{0,6,64,70,128,134,192,198,256,262,320,326,384,390,448,454,16,22,80,86,..., dimensions={0} | all-to-all | bytes 524288 | tf_op jit(solution)/shard_map/all_to_all | solution.py:333
  102.7 0.9 shard_map.92
Async XLA Ops:
  2.1 36.8 %all-to-all-start = ((bf16[64,32,128]{2,1,0:T(8,128)(2,1)}), bf16[64,32,128]{2,1,0:T(8,128)(2,1)S(1)}, u32[]{:S(2)}, u32[]{:S(2)}) async-start(bf16[64,32,128]{2,1,0:T(8,128)(2,1)} %bitcast.36), calls=%async_computation | async-start | bytes 1048576 | tf_op jit(solution)/shard_map/all_to_all | solution.py:333
  24.1 10.7 %collective-permute-start = (bf16[1536,256]{1,0:T(8,128)(2,1)S(1)}, bf16[1536,256]{1,0:T(8,128)(2,1)S(1)}, u32[]{:S(2)}, u32[]{:S(2)}) collective-permute-start(bf16[1536,256]{1,0:T(8,128)(2,1)S(1)} %bitcast.33), channel_id=1, source_target_pairs={{0,1},{1,0},{2,3},{3,2},{4,5},{5,4},{6,7},{7,6},{8,9},{9,8},{10,11... | collective-permute-start | bytes 2359304 | tf_op jit(solution)/shard_map/ppermute | solution.py:339
  28.2 6.6 %collective-permute-start.1 = (bf16[1536,256]{1,0:T(8,128)(2,1)S(1)}, bf16[1536,256]{1,0:T(8,128)(2,1)S(1)}, u32[]{:S(2)}, u32[]{:S(2)}) collective-permute-start(bf16[1536,256]{1,0:T(8,128)(2,1)S(1)} %bitcast.32), channel_id=1, source_target_pairs={{0,1},{1,0},{2,3},{3,2},{4,5},{5,4},{6,7},{7,6},{8,9},{9,8},{10,11... | collective-permute-start | bytes 2359304 | tf_op jit(solution)/shard_map/ppermute | solution.py:339
  30.1 4.7 %collective-permute-start.2 = (bf16[1536,256]{1,0:T(8,128)(2,1)S(1)}, bf16[1536,256]{1,0:T(8,128)(2,1)S(1)}, u32[]{:S(2)}, u32[]{:S(2)}) collective-permute-start(bf16[1536,256]{1,0:T(8,128)(2,1)S(1)} %bitcast.31), channel_id=1, source_target_pairs={{0,1},{1,0},{2,3},{3,2},{4,5},{5,4},{6,7},{7,6},{8,9},{9,8},{10,11... | collective-permute-start | bytes 2359304 | tf_op jit(solution)/shard_map/ppermute | solution.py:339
  39.3 19.2 %copy-start.1 = (bf16[4,3,4,2,16,256]{5,4,3,2,1,0:T(8,128)(2,1)S(1)}, bf16[4,3,4,2,16,256]{5,4,3,2,1,0:T(8,128)(2,1)}, u32[]{:S(2)}) copy-start(bf16[4,3,4,2,16,256]{5,4,3,2,1,0:T(8,128)(2,1)} %get-tuple-element.19) | copy-start | bytes 2359300
  39.3 19.2 %copy-start.2 = (bf16[4,3,4,2,16,256]{5,4,3,2,1,0:T(8,128)(2,1)S(1)}, bf16[4,3,4,2,16,256]{5,4,3,2,1,0:T(8,128)(2,1)}, u32[]{:S(2)}) copy-start(bf16[4,3,4,2,16,256]{5,4,3,2,1,0:T(8,128)(2,1)} %get-tuple-element.20) | copy-start | bytes 2359300
  58.5 5.0 %copy-start = (bf16[4,3,4,2,16,256]{5,4,3,2,1,0:T(8,128)(2,1)S(1)}, bf16[4,3,4,2,16,256]{5,4,3,2,1,0:T(8,128)(2,1)}, u32[]{:S(2)}) copy-start(bf16[4,3,4,2,16,256]{5,4,3,2,1,0:T(8,128)(2,1)} %shard_map.84) | copy-start | bytes 2359300
  60.0 5.9 %copy-start.3 = (s32[128,2]{0,1:T(2,128)S(1)}, s32[128,2]{0,1:T(2,128)}, u32[]{:S(2)}) copy-start(s32[128,2]{0,1:T(2,128)} %param.12) | copy-start | bytes 3076
  60.0 5.9 %copy-start.4 = (f32[128,2]{0,1:T(2,128)S(1)}, f32[128,2]{0,1:T(2,128)}, u32[]{:S(2)}) copy-start(f32[128,2]{0,1:T(2,128)} %param.11) | copy-start | bytes 3076
  60.0 5.9 %copy-start.5 = (f32[128]{0:T(128)S(1)}, f32[128]{0:T(128)}, u32[]{:S(2)}) copy-start(f32[128]{0:T(128)} %param.10) | copy-start | bytes 1540
  60.0 6.6 %collective-permute-start.3 = (f32[320,1280]{1,0:T(8,128)S(1)}, f32[320,1280]{1,0:T(8,128)S(1)}, u32[]{:S(2)}, u32[]{:S(2)}) collective-permute-start(f32[320,1280]{1,0:T(8,128)S(1)} %shard_map.86.first_ref), channel_id=1, source_target_pairs={{0,1},{1,0},{2,3},{3,2},{4,5},{5,4},{6,7},{7,6},{8,9},{9,8},{10,11... | collective-permute-start | bytes 4915208 | tf_op jit(solution)/shard_map/ppermute | solution.py:339
  63.9 3.5 %collective-permute-start.4 = (f32[320,256]{1,0:T(8,128)S(1)}, f32[320,256]{1,0:T(8,128)S(1)}, u32[]{:S(2)}, u32[]{:S(2)}) collective-permute-start(f32[320,256]{1,0:T(8,128)S(1)} %shard_map.87.second_ref), channel_id=1, source_target_pairs={{0,1},{1,0},{2,3},{3,2},{4,5},{5,4},{6,7},{7,6},{8,9},{9,8},{10,11... | collective-permute-start | bytes 983048 | tf_op jit(solution)/shard_map/ppermute | solution.py:339
